TPU v7x, 32 devices: a whole 2x2x4 slice. The times are simulated.
32 devices in a mesh: section: 4 (over y, x), frame: 4 (over z), chan: 2 (over core).
Axes of the slice: x: 2, y: 2, z: 4, core: 2. Of those that a mesh axis runs over, the one named last changes fastest.
Arguments:
- upstream: bfloat16 [512, 8, 4, 128], P('chan', None, 'frame'), may hold values from -6 to 6
- acts: bfloat16 [4, 512, 8, 4, 128], P('section', None, None, 'frame'), may hold values from -6 to 6
- weights: bfloat16 [4, 27, 512, 512], P('section', None, 'chan'), may hold values from -0.0625 to 0.0625
Outputs:
- grads: bfloat16 [4, 512, 8, 4, 128], P('section', 'chan', None, 'frame')
- weight_grads: bfloat16 [4, 27, 512, 512], P('section', None, 'chan')
All inputs are finite; a program needn't handle non-finite values.
Results may differ from a plain program's by a relative error of at most 0.03.
Values may be sent and summed in bfloat16 or wider, within the bound.
No kernel may reach another device: no remote copies, remote signals or barrier semaphores. Data moves between devices by JAX's collectives and lax.ppermute only.
A program may use at most 128 MiB of HBM per device.

v0:
```python
import functools

import jax
import jax.numpy as jnp
from jax import lax
from jax.experimental import pallas as pl
from jax.experimental.pallas import tpu as pltpu
from jax.sharding import PartitionSpec as P

BLOCK_FRAMES = 2
F32 = jnp.float32
BF16 = jnp.bfloat16


def back_kernel(cur_ref, later_ref, w_ref, out_ref, spread, acc):
    frames_n, rows_n, width_n, group = cur_ref.shape
    empty = jnp.zeros((width_n, 3 * group), F32)
    for frame in range(2 * frames_n):
        spread[frame, 0] = empty
        spread[frame, rows_n + 1] = empty
        for row in range(rows_n):
            source = cur_ref[frame, row] if frame < frames_n else later_ref[frame - frames_n, row]
            cells = source.astype(F32)
            spread[frame, row + 1, :, 0:group] = pltpu.roll(cells, width_n - 1, 0)
            spread[frame, row + 1, :, group : 2 * group] = cells
            spread[frame, row + 1, :, 2 * group : 3 * group] = pltpu.roll(cells, 1, 0)
    for step in range(9):
        lag, offset = step // 3, 2 - step % 3
        taken = spread[lag : lag + frames_n, offset : offset + rows_n]
        taken = taken.reshape(frames_n * rows_n * width_n, 3 * group).astype(BF16)
        part = jnp.dot(
            taken, w_ref[3 * step : 3 * step + 3].reshape(3 * group, -1), preferred_element_type=F32
        )
        if step == 0:
            acc[...] = part
        elif step < 8:
            acc[...] += part
        else:
            out_ref[...] = (acc[...] + part).astype(BF16)


def back_block(current, later, kernels):
    frames_n, rows_n, width_n, group = current.shape
    channels = kernels.shape[2]
    cells = frames_n * rows_n * width_n
    held = pl.BlockSpec(memory_space=pltpu.VMEM)
    return pl.pallas_call(
        back_kernel,
        in_specs=[held, held, held],
        out_specs=held,
        out_shape=jax.ShapeDtypeStruct((cells, channels), BF16),
        scratch_shapes=[
            pltpu.VMEM((2 * frames_n, rows_n + 2, width_n, 3 * group), F32),
            pltpu.VMEM((cells, channels), F32),
        ],
        compiler_params=pltpu.CompilerParams(vmem_limit_bytes=24 * 2**20),
        cost_estimate=pl.CostEstimate(
            flops=54 * group * channels * cells, bytes_accessed=54 * group * channels, transcendentals=0
        ),
    )(current, later, kernels)


def tap_kernel(first, f_first, has_sum, *refs):
    grad_ref, parts_ref, *refs = refs
    sum_ref = refs.pop(0) if has_sum else None
    out_ref, cells_ref, sides, feature_ref, total, g_here, f_here = refs
    step = pl.program_id(0)
    pieces_n, frames_n, rows_n, own, group = grad_ref.shape
    rings, chans, rows_l, _, width_c = parts_ref.shape
    width_n = pieces_n * own
    held_n = feature_ref.shape[1] // width_n

    @pl.when(step == 0)
    def _():
        g_copies, f_copies = [], []
        for piece in range(pieces_n):
            columns = pl.ds(piece * own, own)
            g_copies.append(pltpu.make_async_copy(grad_ref.at[piece], cells_ref.at[:, :, columns], g_here.at[piece]))
        for ring in range(rings):
            for chan in range(chans):
                f_copies.append(
                    pltpu.make_async_copy(
                        parts_ref.at[ring, chan, :, pl.ds(f_first * width_n, held_n * width_n)],
                        feature_ref.at[pl.ds(ring * rows_l, rows_l), :, pl.ds(chan * width_c, width_c)],
                        f_here.at[ring * chans + chan],
                    )
                )
        for copy in g_copies + f_copies:
            copy.start()
        same = lax.broadcasted_iota(jnp.int32, (group, group), 0) == lax.broadcasted_iota(jnp.int32, (group, group), 1)
        identity = jnp.where(same, 1.0, 0.0).astype(BF16)
        source = lax.broadcasted_iota(jnp.int32, (width_n, 2 * width_n), 0)
        target = lax.broadcasted_iota(jnp.int32, (width_n, 2 * width_n), 1)
        moved = (source == target + 1) & (target < width_n) | (source == target - width_n - 1)
        shifts = jnp.where(moved, 1.0, 0.0).astype(BF16)
        edge = jnp.zeros((3 * group, frames_n * width_n), BF16)
        sides[:, 0 : frames_n * width_n] = edge
        sides[:, (rows_n + 1) * frames_n * width_n :] = edge
        for copy in g_copies:
            copy.wait()
        for frame in range(frames_n):
            turned = lax.dot_general(
                identity,
                cells_ref[frame].reshape(rows_n * width_n, group),
                (((1,), (1,)), ((), ())),
                preferred_element_type=F32,
            ).astype(BF16)
            for row in range(rows_n):
                start = ((row + 1) * frames_n + frame) * width_n
                cells = turned[:, row * width_n : (row + 1) * width_n]
                both = jnp.dot(cells, shifts, preferred_element_type=F32).astype(BF16)
                sides[0:group, start : start + width_n] = both[:, :width_n]
                sides[group : 2 * group, start : start + width_n] = cells
                sides[2 * group : 3 * group, start : start + width_n] = both[:, width_n:]
        for copy in f_copies:
            copy.wait()

    offset = 2 - step % 3
    for lag in range(3):

        @pl.when(step // 3 == lag)
        def _():
            skipped = max(0, lag - first)
            span = (frames_n - skipped) * width_n
            low = (first + skipped - lag - f_first) * width_n
            for row in range(rows_n):
                start = ((row + offset) * frames_n + skipped) * width_n
                part = jnp.dot(
                    sides[:, pl.ds(pl.multiple_of(start, 128), span)],
                    feature_ref[row, low : low + span],
                    preferred_element_type=F32,
                )
                if row == 0:
                    total[...] = part
                elif row < rows_n - 1:
                    total[...] += part
                else:
                    whole = (total[...] + part).reshape(out_ref.shape)
                    if has_sum:
                        whole = whole + sum_ref[...].astype(F32)
                    out_ref[...] = whole.astype(out_ref.dtype)


def kernel_gradient(first, grads, parts, known):
    pieces_n, frames_n, rows_n, own, group = grads.shape
    rings, chans, rows_l, _, width_c = parts.shape
    channels = chans * width_c
    width_n = pieces_n * own
    f_first = max(0, first - 2)
    held_n = first + frames_n - f_first
    far = pl.BlockSpec(memory_space=pltpu.HBM)
    out_spec = pl.BlockSpec((3, group, channels), lambda step: (step, 0, 0))
    has_sum = known is not None
    return pl.pallas_call(
        functools.partial(tap_kernel, first, f_first, has_sum),
        grid=(9,),
        in_specs=[far, far] + [out_spec] * has_sum,
        out_specs=out_spec,
        out_shape=jax.ShapeDtypeStruct((27, group, channels), BF16),
        scratch_shapes=[
            pltpu.VMEM((frames_n, rows_n, width_n, group), BF16),
            pltpu.VMEM((3 * group, (rows_n + 2) * frames_n * width_n), BF16),
            pltpu.VMEM((rows_n, held_n * width_n, channels), BF16),
            pltpu.VMEM((3 * group, channels), F32),
            pltpu.SemaphoreType.DMA((pieces_n,)),
            pltpu.SemaphoreType.DMA((rings * chans,)),
        ],
        compiler_params=pltpu.CompilerParams(vmem_limit_bytes=58 * 2**20),
        cost_estimate=pl.CostEstimate(
            flops=54 * group * channels * rows_n * frames_n * width_n,
            bytes_accessed=6 * 27 * group * channels,
            transcendentals=0,
        ),
    )(*([grads, parts] + [known] * has_sum))


def body(upstream, acts, weights):
    group, frames_all, rows_l, width_n = upstream.shape
    sections, rings, chans = lax.axis_size("section"), lax.axis_size("frame"), lax.axis_size("chan")
    section_pos, ring_pos, chan_pos = lax.axis_index("section"), lax.axis_index("frame"), lax.axis_index("chan")
    rows_n = rows_l * rings
    own = width_n // rings
    halo = sections
    window = own + 2 * halo
    blocks_n = frames_all // BLOCK_FRAMES
    assert blocks_n == sections
    half = frames_all // 2
    ticks = blocks_n + sections - 1
    kernels = weights[0]

    def to_columns(cells):
        wide = jnp.pad(cells, [(0, 0)] * (cells.ndim - 2) + [(halo, halo), (0, 0)])
        pieces = jnp.stack([wide[..., own * i : own * i + window, :] for i in range(rings)])
        pieces = lax.all_to_all(pieces, "frame", 0, 0)
        pieces = jnp.moveaxis(pieces, 0, -4)
        return pieces.reshape(cells.shape[:-3] + (rows_n, window, group))

    mine = lax.dynamic_slice_in_dim(acts[0], chan_pos * group, group, 0)
    top = frames_all - BLOCK_FRAMES
    relayed = lax.dynamic_slice_in_dim(upstream, (blocks_n - 1 - section_pos) * BLOCK_FRAMES, BLOCK_FRAMES, 1)
    pair = to_columns(jnp.stack([relayed, mine[:, top:]]).transpose(0, 2, 3, 4, 1))
    relayed = pair[0]
    rest = to_columns(mine[:, :top].transpose(1, 2, 3, 0))
    stored = [pair[1]]
    for order in range(1, blocks_n):
        first = top - order * BLOCK_FRAMES
        stored.append(rest[first : first + BLOCK_FRAMES])

    shared = group % 128 == 0
    values = (mine if shared else acts[0]).astype(F32)
    feature_part = (values * jax.nn.sigmoid(values)).astype(BF16).transpose(2, 1, 3, 0)
    feature_part = feature_part.reshape(rows_l, frames_all * width_n, -1)

    column = ring_pos * own - halo + jnp.arange(window)
    inside = jnp.logical_and(column >= 0, column < width_n)[None, None, :, None]
    later = jnp.zeros((BLOCK_FRAMES, rows_n, window, group), BF16)
    current = jnp.where(section_pos == 0, relayed, later)
    held, gathered, results = [], [], []
    for tick in range(ticks):
        if tick == 1:
            feature_part, current, stored[-1] = lax.optimization_barrier((feature_part, current, stored[-1]))
            feature_all = lax.all_gather(feature_part, ("frame", "chan") if shared else "frame")
            feature_all = feature_all.reshape(rings, chans if shared else 1, *feature_part.shape)
        if tick == ticks - 2:
            current, feature_all = lax.optimization_barrier((current, feature_all))
        held.append(current[:, :, halo : halo + own])
        if tick in (ticks - 1 - blocks_n // 2, ticks - 1):
            begin = len(gathered) * (blocks_n // 2)
            taken = jnp.stack(held[begin:])
            taken = lax.dynamic_slice_in_dim(taken, section_pos, blocks_n // 2, 0)[::-1]
            taken, current = lax.optimization_barrier((taken, current))
            gathered.append(lax.all_gather(taken.reshape(half, rows_n, own, group), "frame"))
        partial = back_block(current, later, kernels)
        if tick == ticks - 1:
            partial, gathered[0] = lax.optimization_barrier((partial, gathered[0]))
        summed = lax.dynamic_slice_in_dim(partial, chan_pos * group, group, 1).astype(F32)
        for step in range(1, chans):
            there = lax.rem(chan_pos + step, chans)
            piece = lax.dynamic_slice_in_dim(partial, there * group, group, 1)
            arrived = lax.ppermute(piece, "chan", [(i, (i + step) % chans) for i in range(chans)])
            summed = summed + arrived.astype(F32)
        known = jnp.stack(stored[: tick + 1])
        place = jnp.clip(tick - section_pos, 0, known.shape[0] - 1)
        slot = lax.dynamic_index_in_dim(known, place, 0, keepdims=False).astype(F32)
        logistic = jax.nn.sigmoid(slot)
        slope = logistic * (1.0 + slot * (1.0 - logistic))
        updated = current.astype(F32) + slope * summed.reshape(current.shape)
        updated = jnp.where(inside, updated, 0.0).astype(BF16)
        results.append(updated[:, :, halo : halo + own])
        later = current
        if tick + 1 < ticks:
            pairs = [(i, i + 1) for i in range(sections - 1) if i <= tick < i + blocks_n]
            if tick + 1 < sections:
                updated = jnp.where(section_pos == tick + 1, relayed, updated)
                pairs.append((tick + 1, 0))
            current = lax.ppermute(updated, "section", pairs)

    if own % 16:
        gathered = [
            block.transpose(1, 2, 0, 3, 4).reshape(1, half, rows_n, width_n, group) for block in gathered
        ]
    kernel_sum = kernel_gradient(half, gathered[0], feature_all, None)

    outs = lax.dynamic_slice_in_dim(jnp.stack(results), section_pos, blocks_n, 0)[::-1]
    outs = outs.reshape(frames_all, rings, rows_l, own, group).transpose(1, 0, 2, 3, 4)
    outs, gathered[1], kernel_sum = lax.optimization_barrier((outs, gathered[1], kernel_sum))
    outs = lax.all_to_all(outs, "frame", 0, 0)
    kernel_total = kernel_gradient(0, gathered[1], feature_all, kernel_sum)
    outs, kernel_total = lax.optimization_barrier((outs, kernel_total))
    outs = outs.transpose(4, 1, 2, 0, 3).reshape(group, frames_all, rows_l, width_n)
    return (outs[None], kernel_total[None])


def solution(mesh):
    placed = (
        P("chan", None, "frame", None),
        P("section", None, None, "frame", None),
        P("section", None, "chan", None),
    )
    return jax.shard_map(
        body,
        mesh=mesh,
        in_specs=placed,
        out_specs=(P("section", "chan", None, "frame", None), P("section", None, "chan", None)),
        check_vma=False,
    )
```

profile of v0, /device:TPU:0, one launch (start us, length us, event | category | flops | bytes accessed | tf_op | source)
XLA Modules:
  0.0 185.1 jit_solution(10891583677835922771)
XLA Ops:
  9.9 6.3 %all-to-all-start = ((bf16[4,2,2,1,40,256]{5,4,2,3,1,0:T(8,128)(2,1)}), bf16[4,2,2,1,40,256]{5,4,2,3,1,0:T(8,128)(2,1)S(1)}, u32[]{:S(2)}, u32[]{:S(2)}) async-start(bf16[4,2,2,1,40,256]{5,4,2,3,1,0:T(8,128)(2,1)} %pad_maximum_fusion.2), calls=%async_computation | async-start | bytes 655360 | tf_op jit(solution)/shard_map/all_to_all | solution.py:194
  17.3 9.2 %all-to-all-done = bf16[4,2,2,1,40,256]{5,4,2,3,1,0:T(8,128)(2,1)S(1)} async-done(((bf16[4,2,2,1,40,256]{5,4,2,3,1,0:T(8,128)(2,1)}), bf16[4,2,2,1,40,256]{5,4,2,3,1,0:T(8,128)(2,1)S(1)}, u32[]{:S(2)}, u32[]{:S(2)}) %all-to-all-start) | async-done | bytes 327712 | tf_op jit(solution)/shard_map/all_to_all | solution.py:194
  26.5 3.5 %all-to-all-start.1 = ((bf16[4,6,1,40,256]{4,3,1,2,0:T(8,128)(2,1)}), bf16[4,6,1,40,256]{4,3,1,2,0:T(8,128)(2,1)S(1)}, u32[]{:S(2)}, u32[]{:S(2)}) async-start(bf16[4,6,1,40,256]{4,3,1,2,0:T(8,128)(2,1)} %pad_maximum_fusion.1), calls=%async_computation.1 | async-start | bytes 983040 | tf_op jit(solution)/shard_map/all_to_all | solution.py:194
  30.1 3.0 %copy-done.1 = bf16[1,27,256,512]{3,2,1,0:T(8,128)(2,1)S(1)} copy-done((bf16[1,27,256,512]{3,2,1,0:T(8,128)(2,1)S(1)}, bf16[1,27,256,512]{3,2,1,0:T(8,128)(2,1)}, u32[]{:S(2)}) %copy-start.1) | copy-done | bytes 7077912
  33.1 2.4 %shard_map.50 = bf16[320,512]{1,0:T(8,128)(2,1)S(1)} custom-call(bf16[2,4,40,256]{3,2,1,0:T(8,128)(2,1)S(1)} %broadcast_select_fusion.3.cur_ref.later_ref, bf16[2,4,40,256]{3,2,1,0:T(8,128)(2,1)S(1)} %broadcast_in_dim.44.later_ref, bf16[27,256,512]{2,1,0:T(8,128)(2,1)S(1)} %bitcast.170), custom_call_target="tpu_custom_call" | custom-call | flops 2264924160 | bytes 7077888 | tf_op jit(solution)/shard_map/pallas_call | solution.py:47
  37.4 3.4 %collective-permute-start.1 = (bf16[2,4,40,256]{3,2,1,0:T(8,128)(2,1)S(1)}, bf16[2,4,40,256]{3,2,1,0:T(8,128)(2,1)S(1)}, u32[]{:S(2)}, u32[]{:S(2)}) collective-permute-start(bf16[2,4,40,256]{3,2,1,0:T(8,128)(2,1)S(1)} %get-tuple-element.44), channel_id=1, source_target_pairs={{0,8},{8,0},{1,9},{9,1},{2,10},{10,2},{3,11},{11,3},{4,12},{12,4},... | collective-permute-start | bytes 491528 | tf_op jit(solution)/shard_map/ppermute | solution.py:256
  40.8 1.3 all-to-all-done.1
  42.2 3.4 %collective-permute-done.1.cur_ref.later_ref = bf16[2,4,40,256]{3,2,1,0:T(8,128)(2,1)S(1)} collective-permute-done((bf16[2,4,40,256]{3,2,1,0:T(8,128)(2,1)S(1)}, bf16[2,4,40,256]{3,2,1,0:T(8,128)(2,1)S(1)}, u32[]{:S(2)}, u32[]{:S(2)}) %collective-permute-start.1) | collective-permute-done | bytes 163872 | tf_op jit(solution)/shard_map/ppermute | solution.py:256
  45.8 3.0 %copy-done.2 = bf16[1,27,256,512]{3,2,1,0:T(8,128)(2,1)S(1)} copy-done((bf16[1,27,256,512]{3,2,1,0:T(8,128)(2,1)S(1)}, bf16[1,27,256,512]{3,2,1,0:T(8,128)(2,1)}, u32[]{:S(2)}) %copy-start.2) | copy-done | bytes 7077912
  48.8 2.4 %shard_map.51 = bf16[320,512]{1,0:T(8,128)(2,1)S(1)} custom-call(bf16[2,4,40,256]{3,2,1,0:T(8,128)(2,1)S(1)} %collective-permute-done.1.cur_ref.later_ref, bf16[2,4,40,256]{3,2,1,0:T(8,128)(2,1)S(1)} %broadcast_select_fusion.3.cur_ref.later_ref, bf16[27,256,512]{2,1,0:T(8,128)(2,1)S(1)} %bitcast.171), custom_call_target="tpu_custom_call" | custom-call | flops 2264924160 | bytes 7077888 | tf_op jit(solution)/shard_map/pallas_call | solution.py:47
  51.4 1.3 collective-permute-done.2
  53.1 3.4 %collective-permute-start.3 = (bf16[2,4,40,256]{3,2,1,0:T(8,128)(2,1)S(1)}, bf16[2,4,40,256]{3,2,1,0:T(8,128)(2,1)S(1)}, u32[]{:S(2)}, u32[]{:S(2)}) collective-permute-start(bf16[2,4,40,256]{3,2,1,0:T(8,128)(2,1)S(1)} %get-tuple-element.42), channel_id=1, source_target_pairs={{0,8},{8,16},{16,0},{1,9},{9,17},{17,1},{2,10},{10,18},{18,2},{3,1... | collective-permute-start | bytes 491528 | tf_op jit(solution)/shard_map/ppermute | solution.py:256
  56.6 4.6 %collective-permute-done.3.cur_ref.later_ref = bf16[2,4,40,256]{3,2,1,0:T(8,128)(2,1)S(1)} collective-permute-done((bf16[2,4,40,256]{3,2,1,0:T(8,128)(2,1)S(1)}, bf16[2,4,40,256]{3,2,1,0:T(8,128)(2,1)S(1)}, u32[]{:S(2)}, u32[]{:S(2)}) %collective-permute-start.3) | collective-permute-done | bytes 163872 | tf_op jit(solution)/shard_map/ppermute | solution.py:256
  61.2 2.4 %shard_map.52 = bf16[320,512]{1,0:T(8,128)(2,1)S(1)} custom-call(bf16[2,4,40,256]{3,2,1,0:T(8,128)(2,1)S(1)} %collective-permute-done.3.cur_ref.later_ref, bf16[2,4,40,256]{3,2,1,0:T(8,128)(2,1)S(1)} %collective-permute-done.1.cur_ref.later_ref, bf16[27,256,512]{2,1,0:T(8,128)(2,1)S(1)} %bitcast.172), custom_call_target="tpu_custom_call" | custom-call | flops 2264924160 | bytes 7077888 | tf_op jit(solution)/shard_map/pallas_call | solution.py:47
  63.8 1.3 collective-permute-done.4
  65.5 1.5 collective-permute-start.5
  67.1 5.6 %collective-permute-done.5.cur_ref.later_ref = bf16[2,4,40,256]{3,2,1,0:T(8,128)(2,1)S(1)} collective-permute-done((bf16[2,4,40,256]{3,2,1,0:T(8,128)(2,1)S(1)}, bf16[2,4,40,256]{3,2,1,0:T(8,128)(2,1)S(1)}, u32[]{:S(2)}, u32[]{:S(2)}) %collective-permute-start.5) | collective-permute-done | bytes 163872 | tf_op jit(solution)/shard_map/ppermute | solution.py:256
  72.7 2.4 %shard_map.53 = bf16[320,512]{1,0:T(8,128)(2,1)S(1)} custom-call(bf16[2,4,40,256]{3,2,1,0:T(8,128)(2,1)S(1)} %collective-permute-done.5.cur_ref.later_ref, bf16[2,4,40,256]{3,2,1,0:T(8,128)(2,1)S(1)} %collective-permute-done.3.cur_ref.later_ref, bf16[27,256,512]{2,1,0:T(8,128)(2,1)S(1)} %bitcast.173), custom_call_target="tpu_custom_call" | custom-call | flops 2264924160 | bytes 7077888 | tf_op jit(solution)/shard_map/pallas_call | solution.py:47
  76.8 2.7 %collective-permute-start.7 = (bf16[2,4,40,256]{3,2,1,0:T(8,128)(2,1)S(1)}, bf16[2,4,40,256]{3,2,1,0:T(8,128)(2,1)S(1)}, u32[]{:S(2)}, u32[]{:S(2)}) collective-permute-start(bf16[2,4,40,256]{3,2,1,0:T(8,128)(2,1)S(1)} %fusion.39), channel_id=1, source_target_pairs={{0,8},{8,16},{16,24},{1,9},{9,17},{17,25},{2,10},{10,18},{18,26},{... | collective-permute-start | bytes 491528 | tf_op jit(solution)/shard_map/ppermute | solution.py:256
  79.6 3.5 %collective-permute-done.7.cur_ref.later_ref = bf16[2,4,40,256]{3,2,1,0:T(8,128)(2,1)S(1)} collective-permute-done((bf16[2,4,40,256]{3,2,1,0:T(8,128)(2,1)S(1)}, bf16[2,4,40,256]{3,2,1,0:T(8,128)(2,1)S(1)}, u32[]{:S(2)}, u32[]{:S(2)}) %collective-permute-start.7) | collective-permute-done | bytes 163872 | tf_op jit(solution)/shard_map/ppermute | solution.py:256
  84.7 3.0 %copy-done.3 = bf16[1,27,256,512]{3,2,1,0:T(8,128)(2,1)S(1)} copy-done((bf16[1,27,256,512]{3,2,1,0:T(8,128)(2,1)S(1)}, bf16[1,27,256,512]{3,2,1,0:T(8,128)(2,1)}, u32[]{:S(2)}) %copy-start.3) | copy-done | bytes 7077912
  87.7 2.4 %shard_map.54 = bf16[320,512]{1,0:T(8,128)(2,1)S(1)} custom-call(bf16[2,4,40,256]{3,2,1,0:T(8,128)(2,1)S(1)} %collective-permute-done.7.cur_ref.later_ref, bf16[2,4,40,256]{3,2,1,0:T(8,128)(2,1)S(1)} %collective-permute-done.5.cur_ref.later_ref, bf16[27,256,512]{2,1,0:T(8,128)(2,1)S(1)} %bitcast.174), custom_call_target="tpu_custom_call" | custom-call | flops 2264924160 | bytes 7077888 | tf_op jit(solution)/shard_map/pallas_call | solution.py:47
  90.4 1.4 collective-permute-done.8
  93.7 3.0 %copy-done.4 = bf16[1,27,256,512]{3,2,1,0:T(8,128)(2,1)S(1)} copy-done((bf16[1,27,256,512]{3,2,1,0:T(8,128)(2,1)S(1)}, bf16[1,27,256,512]{3,2,1,0:T(8,128)(2,1)}, u32[]{:S(2)}) %copy-start.4) | copy-done | bytes 7077912
  96.7 2.4 %shard_map.55 = bf16[320,512]{1,0:T(8,128)(2,1)S(1)} custom-call(bf16[2,4,40,256]{3,2,1,0:T(8,128)(2,1)S(1)} %collective-permute-done.9.cur_ref.later_ref, bf16[2,4,40,256]{3,2,1,0:T(8,128)(2,1)S(1)} %collective-permute-done.7.cur_ref.later_ref, bf16[27,256,512]{2,1,0:T(8,128)(2,1)S(1)} %bitcast.175), custom_call_target="tpu_custom_call" | custom-call | flops 2264924160 | bytes 7077888 | tf_op jit(solution)/shard_map/pallas_call | solution.py:47
  102.5 3.0 %copy-done.5 = bf16[1,27,256,512]{3,2,1,0:T(8,128)(2,1)S(1)} copy-done((bf16[1,27,256,512]{3,2,1,0:T(8,128)(2,1)S(1)}, bf16[1,27,256,512]{3,2,1,0:T(8,128)(2,1)}, u32[]{:S(2)}) %copy-start.5) | copy-done | bytes 7077912
  105.5 2.4 %shard_map.56 = bf16[320,512]{1,0:T(8,128)(2,1)S(1)} custom-call(bf16[2,4,40,256]{3,2,1,0:T(8,128)(2,1)S(1)} %collective-permute-done.11.cur_ref, bf16[2,4,40,256]{3,2,1,0:T(8,128)(2,1)S(1)} %collective-permute-done.9.cur_ref.later_ref, bf16[27,256,512]{2,1,0:T(8,128)(2,1)S(1)} %bitcast.176), custom_call_target="tpu_custom_call" | custom-call | flops 2264924160 | bytes 7077888 | tf_op jit(solution)/shard_map/pallas_call | solution.py:47
  108.0 13.7 %all-gather.5.cloned.1.call-done.refs_0_ = bf16[4,4,4,32,256]{4,3,2,1,0:T(8,128)(2,1)} async-done(((bf16[1,4,4,32,256]{4,3,2,1,0:T(8,128)(2,1)}), bf16[4,4,4,32,256]{4,3,2,1,0:T(8,128)(2,1)}) %all-gather.5.cloned.1.call-update) | async-done | bytes 1048592 | tf_op jit(solution)/shard_map/all_gather | solution.py:232
  121.7 20.7 %shard_map.57.refs_2_ = bf16[27,256,512]{2,1,0:T(8,128)(2,1)} custom-call(bf16[4,4,4,32,256]{4,3,2,1,0:T(8,128)(2,1)} %all-gather.5.cloned.1.call-done.refs_0_, bf16[4,2,1,1024,256]{4,3,2,1,0:T(8,128)(2,1)} %bitcast.198), custom_call_target="tpu_custom_call" | custom-call | flops 14495514624 | bytes 21233664 | tf_op jit(solution)/shard_map/pallas_call | solution.py:154
  143.6 10.3 %all-gather.7.cloned.1.call-done.refs_0_ = bf16[4,4,4,32,256]{4,3,2,1,0:T(8,128)(2,1)} async-done(((bf16[1,4,4,32,256]{4,3,2,1,0:T(8,128)(2,1)}), bf16[4,4,4,32,256]{4,3,2,1,0:T(8,128)(2,1)}) %all-gather.7.cloned.1.call-update) | async-done | bytes 1048592 | tf_op jit(solution)/shard_map/all_gather | solution.py:232
  153.9 3.7 %all-to-all-start.2 = ((bf16[4,8,1,32,256]{4,3,1,2,0:T(8,128)(2,1)}), bf16[4,8,1,32,256]{4,3,1,2,0:T(8,128)(2,1)S(1)}, u32[]{:S(2)}, u32[]{:S(2)}) async-start(bf16[4,8,1,32,256]{4,3,1,2,0:T(8,128)(2,1)} %copy_bitcast_fusion), calls=%async_computation.2 | async-start | bytes 1048576 | tf_op jit(solution)/shard_map/all_to_all | solution.py:267
  157.6 19.8 %shard_map.58 = bf16[27,256,512]{2,1,0:T(8,128)(2,1)} custom-call(bf16[4,4,4,32,256]{4,3,2,1,0:T(8,128)(2,1)} %all-gather.7.cloned.1.call-done.refs_0_, bf16[4,2,1,1024,256]{4,3,2,1,0:T(8,128)(2,1)} %bitcast.199, bf16[27,256,512]{2,1,0:T(8,128)(2,1)} %shard_map.57.refs_2_), custom_call_target="tpu_custom_call" | custom-call | flops 14495514624 | bytes 21233664 | tf_op jit(solution)/shard_map/pallas_call | solution.py:154
  (102 shorter events, 17.9 us)
Async XLA Ops:
  7.2 1.4 copy-start
  9.9 16.6 %all-to-all-start = ((bf16[4,2,2,1,40,256]{5,4,2,3,1,0:T(8,128)(2,1)}), bf16[4,2,2,1,40,256]{5,4,2,3,1,0:T(8,128)(2,1)S(1)}, u32[]{:S(2)}, u32[]{:S(2)}) async-start(bf16[4,2,2,1,40,256]{5,4,2,3,1,0:T(8,128)(2,1)} %pad_maximum_fusion.2), calls=%async_computation | async-start | bytes 655360 | tf_op jit(solution)/shard_map/all_to_all | solution.py:194
  26.5 15.6 %all-to-all-start.1 = ((bf16[4,6,1,40,256]{4,3,1,2,0:T(8,128)(2,1)}), bf16[4,6,1,40,256]{4,3,1,2,0:T(8,128)(2,1)S(1)}, u32[]{:S(2)}, u32[]{:S(2)}) async-start(bf16[4,6,1,40,256]{4,3,1,2,0:T(8,128)(2,1)} %pad_maximum_fusion.1), calls=%async_computation.1 | async-start | bytes 983040 | tf_op jit(solution)/shard_map/all_to_all | solution.py:194
  30.0 63.7 %all-gather.9.cloned.1.call-start = ((), (), s32[]{:S(2)}) async-start(), calls=%async_computation.5 | async-start | bytes 4718592 | tf_op jit(solution)/shard_map/all_gather | solution.py:222
  30.1 3.0 %copy-start.1 = (bf16[1,27,256,512]{3,2,1,0:T(8,128)(2,1)S(1)}, bf16[1,27,256,512]{3,2,1,0:T(8,128)(2,1)}, u32[]{:S(2)}) copy-start(bf16[1,27,256,512]{3,2,1,0:T(8,128)(2,1)} %param.5) | copy-start | bytes 21233668
  35.6 1.5 collective-permute-start
  37.4 8.2 %collective-permute-start.1 = (bf16[2,4,40,256]{3,2,1,0:T(8,128)(2,1)S(1)}, bf16[2,4,40,256]{3,2,1,0:T(8,128)(2,1)S(1)}, u32[]{:S(2)}, u32[]{:S(2)}) collective-permute-start(bf16[2,4,40,256]{3,2,1,0:T(8,128)(2,1)S(1)} %get-tuple-element.44), channel_id=1, source_target_pairs={{0,8},{8,0},{1,9},{9,1},{2,10},{10,2},{3,11},{11,3},{4,12},{12,4},... | collective-permute-start | bytes 491528 | tf_op jit(solution)/shard_map/ppermute | solution.py:256
  45.6 76.0 %all-gather.5.cloned.1.call-start = ((), (), s32[]{:S(2)}) async-start(), calls=%async_computation.3 | async-start | bytes 1310720 | tf_op jit(solution)/shard_map/all_gather | solution.py:232
  45.8 3.0 %copy-start.2 = (bf16[1,27,256,512]{3,2,1,0:T(8,128)(2,1)S(1)}, bf16[1,27,256,512]{3,2,1,0:T(8,128)(2,1)}, u32[]{:S(2)}) copy-start(bf16[1,27,256,512]{3,2,1,0:T(8,128)(2,1)} %param.5) | copy-start | bytes 21233668
  51.3 1.5 collective-permute-start.2
  53.1 8.1 %collective-permute-start.3 = (bf16[2,4,40,256]{3,2,1,0:T(8,128)(2,1)S(1)}, bf16[2,4,40,256]{3,2,1,0:T(8,128)(2,1)S(1)}, u32[]{:S(2)}, u32[]{:S(2)}) collective-permute-start(bf16[2,4,40,256]{3,2,1,0:T(8,128)(2,1)S(1)} %get-tuple-element.42), channel_id=1, source_target_pairs={{0,8},{8,16},{16,0},{1,9},{9,17},{17,1},{2,10},{10,18},{18,2},{3,1... | collective-permute-start | bytes 491528 | tf_op jit(solution)/shard_map/ppermute | solution.py:256
  63.7 1.5 collective-permute-start.4
  65.5 7.2 %collective-permute-start.5 = (bf16[2,4,40,256]{3,2,1,0:T(8,128)(2,1)S(1)}, bf16[2,4,40,256]{3,2,1,0:T(8,128)(2,1)S(1)}, u32[]{:S(2)}, u32[]{:S(2)}) collective-permute-start(bf16[2,4,40,256]{3,2,1,0:T(8,128)(2,1)S(1)} %get-tuple-element.40), channel_id=1, source_target_pairs={{0,8},{8,16},{16,24},{24,0},{1,9},{9,17},{17,25},{25,1},{2,10},{10... | collective-permute-start | bytes 491528 | tf_op jit(solution)/shard_map/ppermute | solution.py:256
  75.1 1.5 collective-permute-start.6
  75.3 7.9 %copy-start.6 = (bf16[7,2,4,32,256]{4,3,2,1,0:T(8,128)(2,1)}, bf16[7,2,4,32,256]{4,3,2,1,0:T(8,128)(2,1)S(1)}, u32[]{:S(2)}) copy-start(bf16[7,2,4,32,256]{4,3,2,1,0:T(8,128)(2,1)S(1)} %fusion.76) | copy-start | bytes 2752516
  76.8 6.2 %collective-permute-start.7 = (bf16[2,4,40,256]{3,2,1,0:T(8,128)(2,1)S(1)}, bf16[2,4,40,256]{3,2,1,0:T(8,128)(2,1)S(1)}, u32[]{:S(2)}, u32[]{:S(2)}) collective-permute-start(bf16[2,4,40,256]{3,2,1,0:T(8,128)(2,1)S(1)} %fusion.39), channel_id=1, source_target_pairs={{0,8},{8,16},{16,24},{1,9},{9,17},{17,25},{2,10},{10,18},{18,26},{... | collective-permute-start | bytes 491528 | tf_op jit(solution)/shard_map/ppermute | solution.py:256
  83.1 0.8 copy-start.8
  84.0 6.3 %copy-start.7 = (bf16[7,2,4,32,256]{4,3,2,1,0:T(8,128)(2,1)S(1)}, bf16[7,2,4,32,256]{4,3,2,1,0:T(8,128)(2,1)}, u32[]{:S(2)}) copy-start(bf16[7,2,4,32,256]{4,3,2,1,0:T(8,128)(2,1)} %copy-done.6) | copy-start | bytes 2752516
  84.7 3.0 %copy-start.3 = (bf16[1,27,256,512]{3,2,1,0:T(8,128)(2,1)S(1)}, bf16[1,27,256,512]{3,2,1,0:T(8,128)(2,1)}, u32[]{:S(2)}) copy-start(bf16[1,27,256,512]{3,2,1,0:T(8,128)(2,1)} %param.5) | copy-start | bytes 21233668
  90.2 1.6 collective-permute-start.8
  90.4 63.6 %all-gather.7.cloned.1.call-start = ((), (), s32[]{:S(2)}) async-start(), calls=%async_computation.4 | async-start | bytes 1310720 | tf_op jit(solution)/shard_map/all_gather | solution.py:232
  92.9 0.7 collective-permute-start.9
  93.7 3.0 %copy-start.4 = (bf16[1,27,256,512]{3,2,1,0:T(8,128)(2,1)S(1)}, bf16[1,27,256,512]{3,2,1,0:T(8,128)(2,1)}, u32[]{:S(2)}) copy-start(bf16[1,27,256,512]{3,2,1,0:T(8,128)(2,1)} %param.5) | copy-start | bytes 21233668
  96.7 2.7 %copy-start.9 = (bf16[5,2,4,32,256]{4,3,2,1,0:T(8,128)(2,1)S(1)}, bf16[5,2,4,32,256]{4,3,2,1,0:T(8,128)(2,1)}, u32[]{:S(2)}) copy-start(bf16[5,2,4,32,256]{4,3,2,1,0:T(8,128)(2,1)} %copy-done.8) | copy-start | bytes 1966084
  99.2 1.5 collective-permute-start.10
  101.0 0.7 collective-permute-start.11
  102.5 3.0 %copy-start.5 = (bf16[1,27,256,512]{3,2,1,0:T(8,128)(2,1)S(1)}, bf16[1,27,256,512]{3,2,1,0:T(8,128)(2,1)}, u32[]{:S(2)}) copy-start(bf16[1,27,256,512]{3,2,1,0:T(8,128)(2,1)} %param.5) | copy-start | bytes 21233668
  121.7 20.8 %collective-permute-start.12 = (bf16[320,256]{1,0:T(8,128)(2,1)S(1)}, bf16[320,256]{1,0:T(8,128)(2,1)S(1)}, u32[]{:S(2)}, u32[]{:S(2)}) collective-permute-start(bf16[320,256]{1,0:T(8,128)(2,1)S(1)} %constant_dynamic-slice_fusion.1), channel_id=1, source_target_pairs={{0,1},{1,0},{2,3},{3,2},{4,5},{5,4},{6,7},{7,6},{8,9},{9,8},{10,11... | collective-permute-start | bytes 491528 | tf_op jit(solution)/shard_map/ppermute | solution.py:240
  153.9 23.5 %all-to-all-start.2 = ((bf16[4,8,1,32,256]{4,3,1,2,0:T(8,128)(2,1)}), bf16[4,8,1,32,256]{4,3,1,2,0:T(8,128)(2,1)S(1)}, u32[]{:S(2)}, u32[]{:S(2)}) async-start(bf16[4,8,1,32,256]{4,3,1,2,0:T(8,128)(2,1)} %copy_bitcast_fusion), calls=%async_computation.2 | async-start | bytes 1048576 | tf_op jit(solution)/shard_map/all_to_all | solution.py:267
Sparse Core Ops, SparseCore 0:
  45.7 47.5 all-gather.8
  94.9 26.6 all-gather.4
  123.8 30.0 all-gather.6
where the time goes:
time: 186 us; the launch traced here: 185 us
  waiting for transfers between devices  58.6 us (32%)
  Pallas kernels  57.6 us (31%)
  starting transfers between devices  26.6 us (14%)
  local copies, waits for them, and re-layouts  22.3 us (12%)
  between operations  14.4 us (8%)
  other arithmetic  5.58 us (3%)
    pallas_call x2, Pallas kernels, kernel_gradient(): pl.pallas_call(functools.partial(tap_kernel, first, f_first, has_sum), gr...  40.5 us
    all_gather x2, waiting for transfers between devices, body(): lax.all_gather(taken.reshape(half, rows_n, own, group), 'frame')  24 us
    unnamed x33, local copies, waits for them, and re-layouts  17.4 us
    ppermute x6, waiting for transfers between devices, body(): current = lax.ppermute(updated, 'section', pairs)  17.1 us
    pallas_call x7, Pallas kernels, back_block(): pl.pallas_call(back_kernel, in_specs=[held, held, held], out_specs=held,...  17.1 us
    ppermute x6, starting transfers between devices, body(): current = lax.ppermute(updated, 'section', pairs)  12.4 us
    all_to_all x2, waiting for transfers between devices, to_columns(): pieces = lax.all_to_all(pieces, 'frame', 0, 0)  10.6 us
    all_to_all x2, starting transfers between devices, to_columns(): pieces = lax.all_to_all(pieces, 'frame', 0, 0)  9.79 us
  transfers between devices with their start and end apart: 19, of which 14 were waited for; matrix products, arithmetic and copies ran while one was open for 4% of the time, Pallas kernels for 31%

commit v1 on v0

--- a/solution.py
+++ b/solution.py
@@ -68,20 +68,19 @@
     pieces_n, frames_n, rows_n, own, group = grad_ref.shape
     rings, chans, rows_l, _, width_c = parts_ref.shape
     width_n = pieces_n * own
-    held_n = feature_ref.shape[1] // width_n
+    held_n = feature_ref.shape[2] // width_n
 
     @pl.when(step == 0)
     def _():
         g_copies, f_copies = [], []
         for piece in range(pieces_n):
-            columns = pl.ds(piece * own, own)
-            g_copies.append(pltpu.make_async_copy(grad_ref.at[piece], cells_ref.at[:, :, columns], g_here.at[piece]))
+            g_copies.append(pltpu.make_async_copy(grad_ref.at[piece], cells_ref.at[piece], g_here.at[piece]))
         for ring in range(rings):
             for chan in range(chans):
                 f_copies.append(
                     pltpu.make_async_copy(
                         parts_ref.at[ring, chan, :, pl.ds(f_first * width_n, held_n * width_n)],
-                        feature_ref.at[pl.ds(ring * rows_l, rows_l), :, pl.ds(chan * width_c, width_c)],
+                        feature_ref.at[chan, pl.ds(ring * rows_l, rows_l)],
                         f_here.at[ring * chans + chan],
                     )
                 )
@@ -99,9 +98,10 @@
         for copy in g_copies:
             copy.wait()
         for frame in range(frames_n):
+            joined = [cells_ref[piece, frame, row] for row in range(rows_n) for piece in range(pieces_n)]
             turned = lax.dot_general(
                 identity,
-                cells_ref[frame].reshape(rows_n * width_n, group),
+                jnp.concatenate(joined, axis=0),
                 (((1,), (1,)), ((), ())),
                 preferred_element_type=F32,
             ).astype(BF16)
@@ -123,22 +123,24 @@
             skipped = max(0, lag - first)
             span = (frames_n - skipped) * width_n
             low = (first + skipped - lag - f_first) * width_n
-            for row in range(rows_n):
-                start = ((row + offset) * frames_n + skipped) * width_n
-                part = jnp.dot(
-                    sides[:, pl.ds(pl.multiple_of(start, 128), span)],
-                    feature_ref[row, low : low + span],
-                    preferred_element_type=F32,
-                )
-                if row == 0:
-                    total[...] = part
-                elif row < rows_n - 1:
-                    total[...] += part
-                else:
-                    whole = (total[...] + part).reshape(out_ref.shape)
-                    if has_sum:
-                        whole = whole + sum_ref[...].astype(F32)
-                    out_ref[...] = whole.astype(out_ref.dtype)
+            for chan in range(chans):
+                lanes = slice(chan * width_c, (chan + 1) * width_c)
+                for row in range(rows_n):
+                    start = ((row + offset) * frames_n + skipped) * width_n
+                    part = jnp.dot(
+                        sides[:, pl.ds(pl.multiple_of(start, 128), span)],
+                        feature_ref[chan, row, low : low + span],
+                        preferred_element_type=F32,
+                    )
+                    if row == 0:
+                        total[...] = part
+                    elif row < rows_n - 1:
+                        total[...] += part
+                    else:
+                        whole = (total[...] + part).reshape(3, group, width_c)
+                        if has_sum:
+                            whole = whole + sum_ref[:, :, lanes].astype(F32)
+                        out_ref[:, :, lanes] = whole.astype(out_ref.dtype)
 
 
 def kernel_gradient(first, grads, parts, known):
@@ -158,10 +160,10 @@
         out_specs=out_spec,
         out_shape=jax.ShapeDtypeStruct((27, group, channels), BF16),
         scratch_shapes=[
-            pltpu.VMEM((frames_n, rows_n, width_n, group), BF16),
+            pltpu.VMEM(grads.shape, BF16),
             pltpu.VMEM((3 * group, (rows_n + 2) * frames_n * width_n), BF16),
-            pltpu.VMEM((rows_n, held_n * width_n, channels), BF16),
-            pltpu.VMEM((3 * group, channels), F32),
+            pltpu.VMEM((chans, rows_n, held_n * width_n, width_c), BF16),
+            pltpu.VMEM((3 * group, width_c), F32),
             pltpu.SemaphoreType.DMA((pieces_n,)),
             pltpu.SemaphoreType.DMA((rings * chans,)),
         ],
@@ -218,7 +220,6 @@
     held, gathered, results = [], [], []
     for tick in range(ticks):
         if tick == 1:
-            feature_part, current, stored[-1] = lax.optimization_barrier((feature_part, current, stored[-1]))
             feature_all = lax.all_gather(feature_part, ("frame", "chan") if shared else "frame")
             feature_all = feature_all.reshape(rings, chans if shared else 1, *feature_part.shape)
         if tick == ticks - 2:
@@ -246,6 +247,8 @@
         slope = logistic * (1.0 + slot * (1.0 - logistic))
         updated = current.astype(F32) + slope * summed.reshape(current.shape)
         updated = jnp.where(inside, updated, 0.0).astype(BF16)
+        if tick == 0:
+            feature_part, updated = lax.optimization_barrier((feature_part, updated))
         results.append(updated[:, :, halo : halo + own])
         later = current
         if tick + 1 < ticks:

time: 186 us -> 203 us (1.091)
  waiting for transfers between devices: 58.6 us -> 74.5 us
    all_to_all x2, waiting for transfers between devices: 10.6 us -> 32 us  [to_columns(): pieces = lax.all_to_all(pieces, 'frame', 0, 0)]
    ppermute x6, waiting for transfers between devices: 17.1 us -> 14 us  [body(): current = lax.ppermute(updated, 'section', pairs)]
    all_gather x2, waiting for transfers between devices: 24 us -> 21.8 us  [body(): lax.all_gather(taken.reshape(half, rows_n, own, group), 'frame')]
    unnamed x33 -> x31, local copies, waits for them, and re-layouts: 17.4 us -> 18.1 us
  transfers between devices with their start and end apart: 19 -> 19, of which waited for: 14 -> 13; matrix products, arithmetic and copies ran while one was open for 4% -> 5% of each run, Pallas kernels for 31% -> 27%
where the time goes in v1:
time: 203 us; the launch traced here: 202 us
  waiting for transfers between devices  74.5 us (37%)
  Pallas kernels  57.9 us (29%)
  starting transfers between devices  26.5 us (13%)
  local copies, waits for them, and re-layouts  23 us (11%)
  between operations  14.4 us (7%)
  other arithmetic  6.21 us (3%)
    pallas_call x2, Pallas kernels, kernel_gradient(): pl.pallas_call(functools.partial(tap_kernel, first, f_first, has_sum), gr...  40.7 us
    all_to_all x2, waiting for transfers between devices, to_columns(): pieces = lax.all_to_all(pieces, 'frame', 0, 0)  32 us
    all_gather x2, waiting for transfers between devices, body(): lax.all_gather(taken.reshape(half, rows_n, own, group), 'frame')  21.8 us
    unnamed x31, local copies, waits for them, and re-layouts  18.1 us
    pallas_call x7, Pallas kernels, back_block(): pl.pallas_call(back_kernel, in_specs=[held, held, held], out_specs=held,...  17.1 us
    ppermute x6, waiting for transfers between devices, body(): current = lax.ppermute(updated, 'section', pairs)  14 us
    ppermute x6, starting transfers between devices, body(): current = lax.ppermute(updated, 'section', pairs)  12.1 us
    all_to_all x2, starting transfers between devices, to_columns(): pieces = lax.all_to_all(pieces, 'frame', 0, 0)  9.79 us
  transfers between devices with their start and end apart: 19, of which 13 were waited for; matrix products, arithmetic and copies ran while one was open for 5% of the time, Pallas kernels for 27%

profile of v1, /device:TPU:0, one launch (start us, length us, event | category | flops | bytes accessed | tf_op | source)
XLA Modules:
  0.0 202.5 jit_solution(292018609417232712)
XLA Ops:
  7.2 1.3 constant_dynamic-slice_fusion.10
  9.9 6.3 %all-to-all-start = ((bf16[4,2,2,1,40,256]{5,4,2,3,1,0:T(8,128)(2,1)}), bf16[4,2,2,1,40,256]{5,4,2,3,1,0:T(8,128)(2,1)S(1)}, u32[]{:S(2)}, u32[]{:S(2)}) async-start(bf16[4,2,2,1,40,256]{5,4,2,3,1,0:T(8,128)(2,1)} %pad_maximum_fusion.2), calls=%async_computation | async-start | bytes 655360 | tf_op jit(solution)/shard_map/all_to_all | solution.py:196
  16.2 10.3 %all-to-all-done = bf16[4,2,2,1,40,256]{5,4,2,3,1,0:T(8,128)(2,1)S(1)} async-done(((bf16[4,2,2,1,40,256]{5,4,2,3,1,0:T(8,128)(2,1)}), bf16[4,2,2,1,40,256]{5,4,2,3,1,0:T(8,128)(2,1)S(1)}, u32[]{:S(2)}, u32[]{:S(2)}) %all-to-all-start) | async-done | bytes 327712 | tf_op jit(solution)/shard_map/all_to_all | solution.py:196
  26.6 3.0 %copy-done.1 = bf16[1,27,256,512]{3,2,1,0:T(8,128)(2,1)S(1)} copy-done((bf16[1,27,256,512]{3,2,1,0:T(8,128)(2,1)S(1)}, bf16[1,27,256,512]{3,2,1,0:T(8,128)(2,1)}, u32[]{:S(2)}) %copy-start.1) | copy-done | bytes 7077912
  29.6 2.4 %shard_map.50 = bf16[320,512]{1,0:T(8,128)(2,1)S(1)} custom-call(bf16[2,4,40,256]{3,2,1,0:T(8,128)(2,1)S(1)} %broadcast_select_fusion.3.cur_ref.later_ref, bf16[2,4,40,256]{3,2,1,0:T(8,128)(2,1)S(1)} %broadcast_in_dim.44.later_ref, bf16[27,256,512]{2,1,0:T(8,128)(2,1)S(1)} %bitcast.168), custom_call_target="tpu_custom_call" | custom-call | flops 2264924160 | bytes 7077888 | tf_op jit(solution)/shard_map/pallas_call | solution.py:47
  34.9 3.5 %all-to-all-start.1 = ((bf16[4,6,1,40,256]{4,3,1,2,0:T(8,128)(2,1)}), bf16[4,6,1,40,256]{4,3,1,2,0:T(8,128)(2,1)S(1)}, u32[]{:S(2)}, u32[]{:S(2)}) async-start(bf16[4,6,1,40,256]{4,3,1,2,0:T(8,128)(2,1)} %pad_maximum_fusion.1), calls=%async_computation.1 | async-start | bytes 983040 | tf_op jit(solution)/shard_map/all_to_all | solution.py:196
  39.9 3.4 %collective-permute-start.1 = (bf16[2,4,40,256]{3,2,1,0:T(8,128)(2,1)}, bf16[2,4,40,256]{3,2,1,0:T(8,128)(2,1)S(1)}, u32[]{:S(2)}, u32[]{:S(2)}) collective-permute-start(bf16[2,4,40,256]{3,2,1,0:T(8,128)(2,1)} %broadcast_select_fusion.2), channel_id=1, source_target_pairs={{0,8},{8,0},{1,9},{9,1},{2,10},{10,2},{3,11},{11,3},{4,12},{12,4},... | collective-permute-start | bytes 491528 | tf_op jit(solution)/shard_map/ppermute | solution.py:259
  43.3 21.7 %all-to-all-done.1 = bf16[4,6,1,40,256]{4,3,1,2,0:T(8,128)(2,1)S(1)} async-done(((bf16[4,6,1,40,256]{4,3,1,2,0:T(8,128)(2,1)}), bf16[4,6,1,40,256]{4,3,1,2,0:T(8,128)(2,1)S(1)}, u32[]{:S(2)}, u32[]{:S(2)}) %all-to-all-start.1) | async-done | bytes 491552 | tf_op jit(solution)/shard_map/all_to_all | solution.py:196
  65.1 3.1 %copy-done.2 = bf16[1,27,256,512]{3,2,1,0:T(8,128)(2,1)S(1)} copy-done((bf16[1,27,256,512]{3,2,1,0:T(8,128)(2,1)S(1)}, bf16[1,27,256,512]{3,2,1,0:T(8,128)(2,1)}, u32[]{:S(2)}) %copy-start.2) | copy-done | bytes 7077912
  68.1 2.4 %shard_map.51 = bf16[320,512]{1,0:T(8,128)(2,1)S(1)} custom-call(bf16[2,4,40,256]{3,2,1,0:T(8,128)(2,1)S(1)} %collective-permute-done.1.cur_ref.later_ref, bf16[2,4,40,256]{3,2,1,0:T(8,128)(2,1)S(1)} %broadcast_select_fusion.3.cur_ref.later_ref, bf16[27,256,512]{2,1,0:T(8,128)(2,1)S(1)} %bitcast.169), custom_call_target="tpu_custom_call" | custom-call | flops 2264924160 | bytes 7077888 | tf_op jit(solution)/shard_map/pallas_call | solution.py:47
  70.8 1.2 collective-permute-done.2
  72.3 3.4 %collective-permute-start.3 = (bf16[2,4,40,256]{3,2,1,0:T(8,128)(2,1)S(1)}, bf16[2,4,40,256]{3,2,1,0:T(8,128)(2,1)S(1)}, u32[]{:S(2)}, u32[]{:S(2)}) collective-permute-start(bf16[2,4,40,256]{3,2,1,0:T(8,128)(2,1)S(1)} %get-tuple-element.40), channel_id=1, source_target_pairs={{0,8},{8,16},{16,0},{1,9},{9,17},{17,1},{2,10},{10,18},{18,2},{3,1... | collective-permute-start | bytes 491528 | tf_op jit(solution)/shard_map/ppermute | solution.py:259
  75.8 4.7 %collective-permute-done.3.cur_ref.later_ref = bf16[2,4,40,256]{3,2,1,0:T(8,128)(2,1)S(1)} collective-permute-done((bf16[2,4,40,256]{3,2,1,0:T(8,128)(2,1)S(1)}, bf16[2,4,40,256]{3,2,1,0:T(8,128)(2,1)S(1)}, u32[]{:S(2)}, u32[]{:S(2)}) %collective-permute-start.3) | collective-permute-done | bytes 163872 | tf_op jit(solution)/shard_map/ppermute | solution.py:259
  80.5 2.5 %shard_map.52 = bf16[320,512]{1,0:T(8,128)(2,1)S(1)} custom-call(bf16[2,4,40,256]{3,2,1,0:T(8,128)(2,1)S(1)} %collective-permute-done.3.cur_ref.later_ref, bf16[2,4,40,256]{3,2,1,0:T(8,128)(2,1)S(1)} %collective-permute-done.1.cur_ref.later_ref, bf16[27,256,512]{2,1,0:T(8,128)(2,1)S(1)} %bitcast.170), custom_call_target="tpu_custom_call" | custom-call | flops 2264924160 | bytes 7077888 | tf_op jit(solution)/shard_map/pallas_call | solution.py:47
  83.1 1.3 collective-permute-done.4
  84.8 1.5 collective-permute-start.5
  86.3 5.6 %collective-permute-done.5.cur_ref.later_ref = bf16[2,4,40,256]{3,2,1,0:T(8,128)(2,1)S(1)} collective-permute-done((bf16[2,4,40,256]{3,2,1,0:T(8,128)(2,1)S(1)}, bf16[2,4,40,256]{3,2,1,0:T(8,128)(2,1)S(1)}, u32[]{:S(2)}, u32[]{:S(2)}) %collective-permute-start.5) | collective-permute-done | bytes 163872 | tf_op jit(solution)/shard_map/ppermute | solution.py:259
  92.0 2.4 %shard_map.53 = bf16[320,512]{1,0:T(8,128)(2,1)S(1)} custom-call(bf16[2,4,40,256]{3,2,1,0:T(8,128)(2,1)S(1)} %collective-permute-done.5.cur_ref.later_ref, bf16[2,4,40,256]{3,2,1,0:T(8,128)(2,1)S(1)} %collective-permute-done.3.cur_ref.later_ref, bf16[27,256,512]{2,1,0:T(8,128)(2,1)S(1)} %bitcast.171), custom_call_target="tpu_custom_call" | custom-call | flops 2264924160 | bytes 7077888 | tf_op jit(solution)/shard_map/pallas_call | solution.py:47
  94.6 1.3 collective-permute-done.6
  96.1 2.5 %collective-permute-start.7 = (bf16[2,4,40,256]{3,2,1,0:T(8,128)(2,1)S(1)}, bf16[2,4,40,256]{3,2,1,0:T(8,128)(2,1)S(1)}, u32[]{:S(2)}, u32[]{:S(2)}) collective-permute-start(bf16[2,4,40,256]{3,2,1,0:T(8,128)(2,1)S(1)} %fusion.39), channel_id=1, source_target_pairs={{0,8},{8,16},{16,24},{1,9},{9,17},{17,25},{2,10},{10,18},{18,26},{... | collective-permute-start | bytes 491528 | tf_op jit(solution)/shard_map/ppermute | solution.py:259
  98.7 3.7 %collective-permute-done.7.cur_ref.later_ref = bf16[2,4,40,256]{3,2,1,0:T(8,128)(2,1)S(1)} collective-permute-done((bf16[2,4,40,256]{3,2,1,0:T(8,128)(2,1)S(1)}, bf16[2,4,40,256]{3,2,1,0:T(8,128)(2,1)S(1)}, u32[]{:S(2)}, u32[]{:S(2)}) %collective-permute-start.7) | collective-permute-done | bytes 163872 | tf_op jit(solution)/shard_map/ppermute | solution.py:259
  104.0 3.0 %copy-done.3 = bf16[1,27,256,512]{3,2,1,0:T(8,128)(2,1)S(1)} copy-done((bf16[1,27,256,512]{3,2,1,0:T(8,128)(2,1)S(1)}, bf16[1,27,256,512]{3,2,1,0:T(8,128)(2,1)}, u32[]{:S(2)}) %copy-start.3) | copy-done | bytes 7077912
  107.0 2.4 %shard_map.54 = bf16[320,512]{1,0:T(8,128)(2,1)S(1)} custom-call(bf16[2,4,40,256]{3,2,1,0:T(8,128)(2,1)S(1)} %collective-permute-done.7.cur_ref.later_ref, bf16[2,4,40,256]{3,2,1,0:T(8,128)(2,1)S(1)} %collective-permute-done.5.cur_ref.later_ref, bf16[27,256,512]{2,1,0:T(8,128)(2,1)S(1)} %bitcast.172), custom_call_target="tpu_custom_call" | custom-call | flops 2264924160 | bytes 7077888 | tf_op jit(solution)/shard_map/pallas_call | solution.py:47
  113.0 3.0 %copy-done.4 = bf16[1,27,256,512]{3,2,1,0:T(8,128)(2,1)S(1)} copy-done((bf16[1,27,256,512]{3,2,1,0:T(8,128)(2,1)S(1)}, bf16[1,27,256,512]{3,2,1,0:T(8,128)(2,1)}, u32[]{:S(2)}) %copy-start.4) | copy-done | bytes 7077912
  116.0 2.4 %shard_map.55 = bf16[320,512]{1,0:T(8,128)(2,1)S(1)} custom-call(bf16[2,4,40,256]{3,2,1,0:T(8,128)(2,1)S(1)} %collective-permute-done.9.cur_ref.later_ref, bf16[2,4,40,256]{3,2,1,0:T(8,128)(2,1)S(1)} %collective-permute-done.7.cur_ref.later_ref, bf16[27,256,512]{2,1,0:T(8,128)(2,1)S(1)} %bitcast.173), custom_call_target="tpu_custom_call" | custom-call | flops 2264924160 | bytes 7077888 | tf_op jit(solution)/shard_map/pallas_call | solution.py:47
  121.8 3.0 %copy-done.5 = bf16[1,27,256,512]{3,2,1,0:T(8,128)(2,1)S(1)} copy-done((bf16[1,27,256,512]{3,2,1,0:T(8,128)(2,1)S(1)}, bf16[1,27,256,512]{3,2,1,0:T(8,128)(2,1)}, u32[]{:S(2)}) %copy-start.5) | copy-done | bytes 7077912
  124.8 2.5 %shard_map.56 = bf16[320,512]{1,0:T(8,128)(2,1)S(1)} custom-call(bf16[2,4,40,256]{3,2,1,0:T(8,128)(2,1)S(1)} %collective-permute-done.11.cur_ref, bf16[2,4,40,256]{3,2,1,0:T(8,128)(2,1)S(1)} %collective-permute-done.9.cur_ref.later_ref, bf16[27,256,512]{2,1,0:T(8,128)(2,1)S(1)} %bitcast.174), custom_call_target="tpu_custom_call" | custom-call | flops 2264924160 | bytes 7077888 | tf_op jit(solution)/shard_map/pallas_call | solution.py:47
  127.3 11.6 %all-gather.5.cloned.1.call-done.refs_0_ = bf16[4,4,4,32,256]{4,3,2,1,0:T(8,128)(2,1)} async-done(((bf16[1,4,4,32,256]{4,3,2,1,0:T(8,128)(2,1)}), bf16[4,4,4,32,256]{4,3,2,1,0:T(8,128)(2,1)}) %all-gather.5.cloned.1.call-update) | async-done | bytes 1048592 | tf_op jit(solution)/shard_map/all_gather | solution.py:233
  139.0 20.9 %shard_map.57.refs_2_ = bf16[27,256,512]{2,1,0:T(8,128)(2,1)} custom-call(bf16[4,4,4,32,256]{4,3,2,1,0:T(8,128)(2,1)} %all-gather.5.cloned.1.call-done.refs_0_, bf16[4,2,1,1024,256]{4,3,2,1,0:T(8,128)(2,1)} %bitcast.196), custom_call_target="tpu_custom_call" | custom-call | flops 14495514624 | bytes 21233664 | tf_op jit(solution)/shard_map/pallas_call | solution.py:156
  161.1 10.2 %all-gather.7.cloned.1.call-done.refs_0_ = bf16[4,4,4,32,256]{4,3,2,1,0:T(8,128)(2,1)} async-done(((bf16[1,4,4,32,256]{4,3,2,1,0:T(8,128)(2,1)}), bf16[4,4,4,32,256]{4,3,2,1,0:T(8,128)(2,1)}) %all-gather.7.cloned.1.call-update) | async-done | bytes 1048592 | tf_op jit(solution)/shard_map/all_gather | solution.py:233
  171.2 3.7 %all-to-all-start.2 = ((bf16[4,8,1,32,256]{4,3,1,2,0:T(8,128)(2,1)}), bf16[4,8,1,32,256]{4,3,1,2,0:T(8,128)(2,1)S(1)}, u32[]{:S(2)}, u32[]{:S(2)}) async-start(bf16[4,8,1,32,256]{4,3,1,2,0:T(8,128)(2,1)} %copy_bitcast_fusion), calls=%async_computation.2 | async-start | bytes 1048576 | tf_op jit(solution)/shard_map/all_to_all | solution.py:270
  174.9 19.9 %shard_map.58 = bf16[27,256,512]{2,1,0:T(8,128)(2,1)} custom-call(bf16[4,4,4,32,256]{4,3,2,1,0:T(8,128)(2,1)} %all-gather.7.cloned.1.call-done.refs_0_, bf16[4,2,1,1024,256]{4,3,2,1,0:T(8,128)(2,1)} %bitcast.197, bf16[27,256,512]{2,1,0:T(8,128)(2,1)} %shard_map.57.refs_2_), custom_call_target="tpu_custom_call" | custom-call | flops 14495514624 | bytes 21233664 | tf_op jit(solution)/shard_map/pallas_call | solution.py:156
  (101 shorter events, 17.9 us)
Async XLA Ops:
  7.2 1.4 copy-start
  9.9 16.6 %all-to-all-start = ((bf16[4,2,2,1,40,256]{5,4,2,3,1,0:T(8,128)(2,1)}), bf16[4,2,2,1,40,256]{5,4,2,3,1,0:T(8,128)(2,1)S(1)}, u32[]{:S(2)}, u32[]{:S(2)}) async-start(bf16[4,2,2,1,40,256]{5,4,2,3,1,0:T(8,128)(2,1)} %pad_maximum_fusion.2), calls=%async_computation | async-start | bytes 655360 | tf_op jit(solution)/shard_map/all_to_all | solution.py:196
  16.2 96.8 %all-gather.9.cloned.1.call-start = ((), (), s32[]{:S(2)}) async-start(), calls=%async_computation.5 | async-start | bytes 4718592 | tf_op jit(solution)/shard_map/all_gather | solution.py:223
  26.6 3.0 %copy-start.1 = (bf16[1,27,256,512]{3,2,1,0:T(8,128)(2,1)S(1)}, bf16[1,27,256,512]{3,2,1,0:T(8,128)(2,1)}, u32[]{:S(2)}) copy-start(bf16[1,27,256,512]{3,2,1,0:T(8,128)(2,1)} %param.5) | copy-start | bytes 21233668
  32.1 1.5 collective-permute-start
  34.9 30.1 %all-to-all-start.1 = ((bf16[4,6,1,40,256]{4,3,1,2,0:T(8,128)(2,1)}), bf16[4,6,1,40,256]{4,3,1,2,0:T(8,128)(2,1)S(1)}, u32[]{:S(2)}, u32[]{:S(2)}) async-start(bf16[4,6,1,40,256]{4,3,1,2,0:T(8,128)(2,1)} %pad_maximum_fusion.1), calls=%async_computation.1 | async-start | bytes 983040 | tf_op jit(solution)/shard_map/all_to_all | solution.py:196
  38.4 100.6 %all-gather.5.cloned.1.call-start = ((), (), s32[]{:S(2)}) async-start(), calls=%async_computation.3 | async-start | bytes 1310720 | tf_op jit(solution)/shard_map/all_gather | solution.py:233
  39.9 25.1 %collective-permute-start.1 = (bf16[2,4,40,256]{3,2,1,0:T(8,128)(2,1)}, bf16[2,4,40,256]{3,2,1,0:T(8,128)(2,1)S(1)}, u32[]{:S(2)}, u32[]{:S(2)}) collective-permute-start(bf16[2,4,40,256]{3,2,1,0:T(8,128)(2,1)} %broadcast_select_fusion.2), channel_id=1, source_target_pairs={{0,8},{8,0},{1,9},{9,1},{2,10},{10,2},{3,11},{11,3},{4,12},{12,4},... | collective-permute-start | bytes 491528 | tf_op jit(solution)/shard_map/ppermute | solution.py:259
  65.0 10.8 %copy-start.8 = (bf16[5,2,4,32,256]{4,3,2,1,0:T(8,128)(2,1)S(1)}, bf16[5,2,4,32,256]{4,3,2,1,0:T(8,128)(2,1)}, u32[]{:S(2)}) copy-start(bf16[5,2,4,32,256]{4,3,2,1,0:T(8,128)(2,1)} %fusion.75) | copy-start | bytes 1966084
  65.0 3.1 %copy-start.2 = (bf16[1,27,256,512]{3,2,1,0:T(8,128)(2,1)S(1)}, bf16[1,27,256,512]{3,2,1,0:T(8,128)(2,1)}, u32[]{:S(2)}) copy-start(bf16[1,27,256,512]{3,2,1,0:T(8,128)(2,1)} %param.5) | copy-start | bytes 21233668
  70.6 1.5 collective-permute-start.2
  72.3 8.1 %collective-permute-start.3 = (bf16[2,4,40,256]{3,2,1,0:T(8,128)(2,1)S(1)}, bf16[2,4,40,256]{3,2,1,0:T(8,128)(2,1)S(1)}, u32[]{:S(2)}, u32[]{:S(2)}) collective-permute-start(bf16[2,4,40,256]{3,2,1,0:T(8,128)(2,1)S(1)} %get-tuple-element.40), channel_id=1, source_target_pairs={{0,8},{8,16},{16,0},{1,9},{9,17},{17,1},{2,10},{10,18},{18,2},{3,1... | collective-permute-start | bytes 491528 | tf_op jit(solution)/shard_map/ppermute | solution.py:259
  83.0 1.5 collective-permute-start.4
  84.8 7.2 %collective-permute-start.5 = (bf16[2,4,40,256]{3,2,1,0:T(8,128)(2,1)S(1)}, bf16[2,4,40,256]{3,2,1,0:T(8,128)(2,1)S(1)}, u32[]{:S(2)}, u32[]{:S(2)}) collective-permute-start(bf16[2,4,40,256]{3,2,1,0:T(8,128)(2,1)S(1)} %get-tuple-element.38), channel_id=1, source_target_pairs={{0,8},{8,16},{16,24},{24,0},{1,9},{9,17},{17,25},{25,1},{2,10},{10... | collective-permute-start | bytes 491528 | tf_op jit(solution)/shard_map/ppermute | solution.py:259
  94.5 1.5 collective-permute-start.6
  96.1 6.2 %collective-permute-start.7 = (bf16[2,4,40,256]{3,2,1,0:T(8,128)(2,1)S(1)}, bf16[2,4,40,256]{3,2,1,0:T(8,128)(2,1)S(1)}, u32[]{:S(2)}, u32[]{:S(2)}) collective-permute-start(bf16[2,4,40,256]{3,2,1,0:T(8,128)(2,1)S(1)} %fusion.39), channel_id=1, source_target_pairs={{0,8},{8,16},{16,24},{1,9},{9,17},{17,25},{2,10},{10,18},{18,26},{... | collective-permute-start | bytes 491528 | tf_op jit(solution)/shard_map/ppermute | solution.py:259
  102.4 0.8 copy-start.6
  104.0 3.0 %copy-start.3 = (bf16[1,27,256,512]{3,2,1,0:T(8,128)(2,1)S(1)}, bf16[1,27,256,512]{3,2,1,0:T(8,128)(2,1)}, u32[]{:S(2)}) copy-start(bf16[1,27,256,512]{3,2,1,0:T(8,128)(2,1)} %param.5) | copy-start | bytes 21233668
  109.5 1.6 collective-permute-start.8
  109.6 61.6 %all-gather.7.cloned.1.call-start = ((), (), s32[]{:S(2)}) async-start(), calls=%async_computation.4 | async-start | bytes 1310720 | tf_op jit(solution)/shard_map/all_gather | solution.py:233
  112.2 0.7 collective-permute-start.9
  113.0 3.0 %copy-start.4 = (bf16[1,27,256,512]{3,2,1,0:T(8,128)(2,1)S(1)}, bf16[1,27,256,512]{3,2,1,0:T(8,128)(2,1)}, u32[]{:S(2)}) copy-start(bf16[1,27,256,512]{3,2,1,0:T(8,128)(2,1)} %param.5) | copy-start | bytes 21233668
  116.0 2.7 %copy-start.7 = (bf16[5,2,4,32,256]{4,3,2,1,0:T(8,128)(2,1)S(1)}, bf16[5,2,4,32,256]{4,3,2,1,0:T(8,128)(2,1)}, u32[]{:S(2)}) copy-start(bf16[5,2,4,32,256]{4,3,2,1,0:T(8,128)(2,1)} %copy-done.6) | copy-start | bytes 1966084
  118.5 1.5 collective-permute-start.10
  120.3 0.7 collective-permute-start.11
  121.8 3.0 %copy-start.5 = (bf16[1,27,256,512]{3,2,1,0:T(8,128)(2,1)S(1)}, bf16[1,27,256,512]{3,2,1,0:T(8,128)(2,1)}, u32[]{:S(2)}) copy-start(bf16[1,27,256,512]{3,2,1,0:T(8,128)(2,1)} %param.5) | copy-start | bytes 21233668
  138.9 21.0 %collective-permute-start.12 = (bf16[320,256]{1,0:T(8,128)(2,1)S(1)}, bf16[320,256]{1,0:T(8,128)(2,1)S(1)}, u32[]{:S(2)}, u32[]{:S(2)}) collective-permute-start(bf16[320,256]{1,0:T(8,128)(2,1)S(1)} %constant_dynamic-slice_fusion.1), channel_id=1, source_target_pairs={{0,1},{1,0},{2,3},{3,2},{4,5},{5,4},{6,7},{7,6},{8,9},{9,8},{10,11... | collective-permute-start | bytes 491528 | tf_op jit(solution)/shard_map/ppermute | solution.py:241
  171.2 23.6 %all-to-all-start.2 = ((bf16[4,8,1,32,256]{4,3,1,2,0:T(8,128)(2,1)}), bf16[4,8,1,32,256]{4,3,1,2,0:T(8,128)(2,1)S(1)}, u32[]{:S(2)}, u32[]{:S(2)}) async-start(bf16[4,8,1,32,256]{4,3,1,2,0:T(8,128)(2,1)} %copy_bitcast_fusion), calls=%async_computation.2 | async-start | bytes 1048576 | tf_op jit(solution)/shard_map/all_to_all | solution.py:270
Sparse Core Ops, SparseCore 0:
  33.9 54.4 all-gather.8
  109.8 29.1 all-gather.4
  141.1 30.1 all-gather.6

commit v2 on v1

--- a/solution.py
+++ b/solution.py
@@ -61,11 +61,12 @@
 
 
 def tap_kernel(first, f_first, has_sum, *refs):
-    grad_ref, parts_ref, *refs = refs
+    ring_ref, parts_ref, *refs = refs
     sum_ref = refs.pop(0) if has_sum else None
-    out_ref, cells_ref, sides, feature_ref, total, g_here, f_here = refs
+    out_ref, cells_ref, sides, feature_ref, total, g_here, f_here = refs[-7:]
+    grad_refs = refs[:-7]
     step = pl.program_id(0)
-    pieces_n, frames_n, rows_n, own, group = grad_ref.shape
+    pieces_n, frames_n, rows_n, own, group = cells_ref.shape
     rings, chans, rows_l, _, width_c = parts_ref.shape
     width_n = pieces_n * own
     held_n = feature_ref.shape[2] // width_n
@@ -74,7 +75,11 @@
     def _():
         g_copies, f_copies = [], []
         for piece in range(pieces_n):
-            g_copies.append(pltpu.make_async_copy(grad_ref.at[piece], cells_ref.at[piece], g_here.at[piece]))
+            if len(grad_refs) == 1:
+                source, target = grad_refs[0].at[piece], cells_ref.at[piece]
+            else:
+                source, target = grad_refs[piece], cells_ref.at[lax.rem(ring_ref[0] + pieces_n - piece, pieces_n)]
+            g_copies.append(pltpu.make_async_copy(source, target, g_here.at[piece]))
         for ring in range(rings):
             for chan in range(chans):
                 f_copies.append(
@@ -123,12 +128,21 @@
             skipped = max(0, lag - first)
             span = (frames_n - skipped) * width_n
             low = (first + skipped - lag - f_first) * width_n
+            starts = [((row + offset) * frames_n + skipped) * width_n for row in range(rows_n)]
+            lefts = [sides[:, pl.ds(pl.multiple_of(start, 128), span)] for start in starts] if has_sum else None
             for chan in range(chans):
                 lanes = slice(chan * width_c, (chan + 1) * width_c)
+                if has_sum:
+                    rights = [feature_ref[chan, row, low : low + span] for row in range(rows_n)]
+                    whole = jnp.dot(
+                        jnp.concatenate(lefts, axis=1), jnp.concatenate(rights, axis=0), preferred_element_type=F32
+                    ).reshape(3, group, width_c)
+                    whole = whole + sum_ref[:, :, lanes].astype(F32)
+                    out_ref[:, :, lanes] = whole.astype(out_ref.dtype)
+                    continue
                 for row in range(rows_n):
-                    start = ((row + offset) * frames_n + skipped) * width_n
                     part = jnp.dot(
-                        sides[:, pl.ds(pl.multiple_of(start, 128), span)],
+                        sides[:, pl.ds(pl.multiple_of(starts[row], 128), span)],
                         feature_ref[chan, row, low : low + span],
                         preferred_element_type=F32,
                     )
@@ -138,13 +152,12 @@
                         total[...] += part
                     else:
                         whole = (total[...] + part).reshape(3, group, width_c)
-                        if has_sum:
-                            whole = whole + sum_ref[:, :, lanes].astype(F32)
                         out_ref[:, :, lanes] = whole.astype(out_ref.dtype)
 
 
-def kernel_gradient(first, grads, parts, known):
-    pieces_n, frames_n, rows_n, own, group = grads.shape
+def kernel_gradient(first, grads, parts, ring_pos, known):
+    held = grads[0].shape if len(grads) == 1 else (len(grads),) + grads[0].shape
+    pieces_n, frames_n, rows_n, own, group = held
     rings, chans, rows_l, _, width_c = parts.shape
     channels = chans * width_c
     width_n = pieces_n * own
@@ -156,11 +169,11 @@
     return pl.pallas_call(
         functools.partial(tap_kernel, first, f_first, has_sum),
         grid=(9,),
-        in_specs=[far, far] + [out_spec] * has_sum,
+        in_specs=[pl.BlockSpec(memory_space=pltpu.SMEM), far] + [out_spec] * has_sum + [far] * len(grads),
         out_specs=out_spec,
         out_shape=jax.ShapeDtypeStruct((27, group, channels), BF16),
         scratch_shapes=[
-            pltpu.VMEM(grads.shape, BF16),
+            pltpu.VMEM(held, BF16),
             pltpu.VMEM((3 * group, (rows_n + 2) * frames_n * width_n), BF16),
             pltpu.VMEM((chans, rows_n, held_n * width_n, width_c), BF16),
             pltpu.VMEM((3 * group, width_c), F32),
@@ -173,7 +186,7 @@
             bytes_accessed=6 * 27 * group * channels,
             transcendentals=0,
         ),
-    )(*([grads, parts] + [known] * has_sum))
+    )(*([ring_pos.reshape(1), parts] + [known] * has_sum + grads))
 
 
 def body(upstream, acts, weights):
@@ -220,6 +233,7 @@
     held, gathered, results = [], [], []
     for tick in range(ticks):
         if tick == 1:
+            feature_part, current, stored[-1] = lax.optimization_barrier((feature_part, current, stored[-1]))
             feature_all = lax.all_gather(feature_part, ("frame", "chan") if shared else "frame")
             feature_all = feature_all.reshape(rings, chans if shared else 1, *feature_part.shape)
         if tick == ticks - 2:
@@ -230,10 +244,17 @@
             taken = jnp.stack(held[begin:])
             taken = lax.dynamic_slice_in_dim(taken, section_pos, blocks_n // 2, 0)[::-1]
             taken, current = lax.optimization_barrier((taken, current))
-            gathered.append(lax.all_gather(taken.reshape(half, rows_n, own, group), "frame"))
+            taken = taken.reshape(half, rows_n, own, group)
+            if not begin:
+                gathered.append([lax.all_gather(taken, "frame")])
         partial = back_block(current, later, kernels)
         if tick == ticks - 1:
-            partial, gathered[0] = lax.optimization_barrier((partial, gathered[0]))
+            partial, gathered[0], taken = lax.optimization_barrier((partial, gathered[0], taken))
+            if rings <= 4:
+                pairs = [[(i, (i + step) % rings) for i in range(rings)] for step in range(1, rings)]
+                gathered.append([taken] + [lax.ppermute(taken, "frame", pair) for pair in pairs])
+            else:
+                gathered.append([lax.all_gather(taken, "frame")])
         summed = lax.dynamic_slice_in_dim(partial, chan_pos * group, group, 1).astype(F32)
         for step in range(1, chans):
             there = lax.rem(chan_pos + step, chans)
@@ -247,8 +268,6 @@
         slope = logistic * (1.0 + slot * (1.0 - logistic))
         updated = current.astype(F32) + slope * summed.reshape(current.shape)
         updated = jnp.where(inside, updated, 0.0).astype(BF16)
-        if tick == 0:
-            feature_part, updated = lax.optimization_barrier((feature_part, updated))
         results.append(updated[:, :, halo : halo + own])
         later = current
         if tick + 1 < ticks:
@@ -258,17 +277,17 @@
                 pairs.append((tick + 1, 0))
             current = lax.ppermute(updated, "section", pairs)
 
-    if own % 16:
+    if own % 16 and rings > 4:
         gathered = [
-            block.transpose(1, 2, 0, 3, 4).reshape(1, half, rows_n, width_n, group) for block in gathered
+            [block.transpose(1, 2, 0, 3, 4).reshape(1, half, rows_n, width_n, group)] for (block,) in gathered
         ]
-    kernel_sum = kernel_gradient(half, gathered[0], feature_all, None)
+    kernel_sum = kernel_gradient(half, gathered[0], feature_all, ring_pos, None)
 
     outs = lax.dynamic_slice_in_dim(jnp.stack(results), section_pos, blocks_n, 0)[::-1]
     outs = outs.reshape(frames_all, rings, rows_l, own, group).transpose(1, 0, 2, 3, 4)
     outs, gathered[1], kernel_sum = lax.optimization_barrier((outs, gathered[1], kernel_sum))
     outs = lax.all_to_all(outs, "frame", 0, 0)
-    kernel_total = kernel_gradient(0, gathered[1], feature_all, kernel_sum)
+    kernel_total = kernel_gradient(0, gathered[1], feature_all, ring_pos, kernel_sum)
     outs, kernel_total = lax.optimization_barrier((outs, kernel_total))
     outs = outs.transpose(4, 1, 2, 0, 3).reshape(group, frames_all, rows_l, width_n)
     return (outs[None], kernel_total[None])

time: 203 us -> 183 us (0.901)
  the two profiles are of different devices: /device:TPU:0 before, /device:TPU:15 now
where the time goes in v2:
time: 183 us; the launch traced here: 182 us
  Pallas kernels  56.7 us (31%)
  starting transfers between devices  46.4 us (25%)
  waiting for transfers between devices  36.2 us (20%)
  local copies, waits for them, and re-layouts  22.4 us (12%)
  between operations  14.6 us (8%)
  other arithmetic  5.59 us (3%)
    pallas_call x2, Pallas kernels, kernel_gradient(): pl.pallas_call(functools.partial(tap_kernel, first, f_first, has_sum), gr...  39.5 us
    ppermute x6, waiting for transfers between devices, body(): current = lax.ppermute(updated, 'section', pairs)  25.1 us
    ppermute x6, starting transfers between devices, body(): current = lax.ppermute(updated, 'section', pairs)  19 us
    unnamed x33, local copies, waits for them, and re-layouts  17.4 us
    pallas_call x7, Pallas kernels, back_block(): pl.pallas_call(back_kernel, in_specs=[held, held, held], out_specs=held,...  17.1 us
    all_to_all x2, starting transfers between devices, to_columns(): pieces = lax.all_to_all(pieces, 'frame', 0, 0)  9.77 us
    ppermute x7, starting transfers between devices, body(): lax.ppermute(piece, 'chan', [(i, (i + step) % chans) for i in range(chans)])  9.35 us
    all_to_all x2, waiting for transfers between devices, to_columns(): pieces = lax.all_to_all(pieces, 'frame', 0, 0)  5.99 us
  transfers between devices with their start and end apart: 21, of which 10 were waited for; matrix products, arithmetic and copies ran while one was open for 5% of the time, Pallas kernels for 31%

profile of v2, /device:TPU:15, one launch (start us, length us, event | category | flops | bytes accessed | tf_op | source)
XLA Modules:
  0.0 181.9 jit_solution(219471753322093759)
XLA Ops:
  7.2 1.3 constant_dynamic-slice_fusion.11
  9.9 4.8 %all-to-all-start = ((bf16[4,2,2,1,40,256]{5,4,2,3,1,0:T(8,128)(2,1)}), bf16[4,2,2,1,40,256]{5,4,2,3,1,0:T(8,128)(2,1)S(1)}, u32[]{:S(2)}, u32[]{:S(2)}) async-start(bf16[4,2,2,1,40,256]{5,4,2,3,1,0:T(8,128)(2,1)} %pad_maximum_fusion.2), calls=%async_computation | async-start | bytes 655360 | tf_op jit(solution)/shard_map/all_to_all | solution.py:209
  15.7 6.0 %all-to-all-done = bf16[4,2,2,1,40,256]{5,4,2,3,1,0:T(8,128)(2,1)S(1)} async-done(((bf16[4,2,2,1,40,256]{5,4,2,3,1,0:T(8,128)(2,1)}), bf16[4,2,2,1,40,256]{5,4,2,3,1,0:T(8,128)(2,1)S(1)}, u32[]{:S(2)}, u32[]{:S(2)}) %all-to-all-start) | async-done | bytes 327712 | tf_op jit(solution)/shard_map/all_to_all | solution.py:209
  21.7 5.0 %all-to-all-start.1 = ((bf16[4,6,1,40,256]{4,3,1,2,0:T(8,128)(2,1)}), bf16[4,6,1,40,256]{4,3,1,2,0:T(8,128)(2,1)S(1)}, u32[]{:S(2)}, u32[]{:S(2)}) async-start(bf16[4,6,1,40,256]{4,3,1,2,0:T(8,128)(2,1)} %pad_maximum_fusion.1), calls=%async_computation.1 | async-start | bytes 983040 | tf_op jit(solution)/shard_map/all_to_all | solution.py:209
  26.8 3.0 %copy-done.1 = bf16[1,27,256,512]{3,2,1,0:T(8,128)(2,1)S(1)} copy-done((bf16[1,27,256,512]{3,2,1,0:T(8,128)(2,1)S(1)}, bf16[1,27,256,512]{3,2,1,0:T(8,128)(2,1)}, u32[]{:S(2)}) %copy-start.1) | copy-done | bytes 7077912
  29.8 2.4 %shard_map.50 = bf16[320,512]{1,0:T(8,128)(2,1)S(1)} custom-call(bf16[2,4,40,256]{3,2,1,0:T(8,128)(2,1)S(1)} %broadcast_select_fusion.3.cur_ref.later_ref, bf16[2,4,40,256]{3,2,1,0:T(8,128)(2,1)S(1)} %broadcast_in_dim.44.later_ref, bf16[27,256,512]{2,1,0:T(8,128)(2,1)S(1)} %bitcast.171), custom_call_target="tpu_custom_call" | custom-call | flops 2264924160 | bytes 7077888 | tf_op jit(solution)/shard_map/pallas_call | solution.py:47
  32.3 3.0 %collective-permute-start = (bf16[320,256]{1,0:T(8,128)(2,1)S(1)}, bf16[320,256]{1,0:T(8,128)(2,1)S(1)}, u32[]{:S(2)}, u32[]{:S(2)}) collective-permute-start(bf16[320,256]{1,0:T(8,128)(2,1)S(1)} %constant_dynamic-slice_fusion.9), channel_id=1, source_target_pairs={{0,1},{1,0},{2,3},{3,2},{4,5},{5,4},{6,7},{7,6},{8,9},{9,8},{10,11... | collective-permute-start | bytes 491528 | tf_op jit(solution)/shard_map/ppermute | solution.py:262
  37.7 3.0 %copy-done.2 = bf16[1,27,256,512]{3,2,1,0:T(8,128)(2,1)S(1)} copy-done((bf16[1,27,256,512]{3,2,1,0:T(8,128)(2,1)S(1)}, bf16[1,27,256,512]{3,2,1,0:T(8,128)(2,1)}, u32[]{:S(2)}) %copy-start.2) | copy-done | bytes 7077912
  40.7 2.5 %shard_map.51 = bf16[320,512]{1,0:T(8,128)(2,1)S(1)} custom-call(bf16[2,4,40,256]{3,2,1,0:T(8,128)(2,1)S(1)} %collective-permute-done.1.cur_ref.later_ref, bf16[2,4,40,256]{3,2,1,0:T(8,128)(2,1)S(1)} %broadcast_select_fusion.3.cur_ref.later_ref, bf16[27,256,512]{2,1,0:T(8,128)(2,1)S(1)} %bitcast.172), custom_call_target="tpu_custom_call" | custom-call | flops 2264924160 | bytes 7077888 | tf_op jit(solution)/shard_map/pallas_call | solution.py:47
  43.2 1.7 collective-permute-start.2
  47.0 2.4 %shard_map.52 = bf16[320,512]{1,0:T(8,128)(2,1)S(1)} custom-call(bf16[2,4,40,256]{3,2,1,0:T(8,128)(2,1)S(1)} %collective-permute-done.3.cur_ref.later_ref, bf16[2,4,40,256]{3,2,1,0:T(8,128)(2,1)S(1)} %collective-permute-done.1.cur_ref.later_ref, bf16[27,256,512]{2,1,0:T(8,128)(2,1)S(1)} %bitcast.173), custom_call_target="tpu_custom_call" | custom-call | flops 2264924160 | bytes 7077888 | tf_op jit(solution)/shard_map/pallas_call | solution.py:47
  51.3 13.6 %collective-permute-start.5 = (bf16[2,4,40,256]{3,2,1,0:T(8,128)(2,1)S(1)}, bf16[2,4,40,256]{3,2,1,0:T(8,128)(2,1)S(1)}, u32[]{:S(2)}, u32[]{:S(2)}) collective-permute-start(bf16[2,4,40,256]{3,2,1,0:T(8,128)(2,1)S(1)} %get-tuple-element.48), channel_id=1, source_target_pairs={{0,8},{8,16},{16,24},{24,0},{1,9},{9,17},{17,25},{25,1},{2,10},{10... | collective-permute-start | bytes 491528 | tf_op jit(solution)/shard_map/ppermute | solution.py:278
  65.0 4.1 %collective-permute-done.5.cur_ref.later_ref = bf16[2,4,40,256]{3,2,1,0:T(8,128)(2,1)S(1)} collective-permute-done((bf16[2,4,40,256]{3,2,1,0:T(8,128)(2,1)S(1)}, bf16[2,4,40,256]{3,2,1,0:T(8,128)(2,1)S(1)}, u32[]{:S(2)}, u32[]{:S(2)}) %collective-permute-start.5) | collective-permute-done | bytes 163872 | tf_op jit(solution)/shard_map/ppermute | solution.py:278
  69.1 2.5 %shard_map.53 = bf16[320,512]{1,0:T(8,128)(2,1)S(1)} custom-call(bf16[2,4,40,256]{3,2,1,0:T(8,128)(2,1)S(1)} %collective-permute-done.5.cur_ref.later_ref, bf16[2,4,40,256]{3,2,1,0:T(8,128)(2,1)S(1)} %collective-permute-done.3.cur_ref.later_ref, bf16[27,256,512]{2,1,0:T(8,128)(2,1)S(1)} %bitcast.174), custom_call_target="tpu_custom_call" | custom-call | flops 2264924160 | bytes 7077888 | tf_op jit(solution)/shard_map/pallas_call | solution.py:47
  73.7 1.5 collective-permute-start.7
  75.2 7.1 %collective-permute-done.7.cur_ref.later_ref = bf16[2,4,40,256]{3,2,1,0:T(8,128)(2,1)S(1)} collective-permute-done((bf16[2,4,40,256]{3,2,1,0:T(8,128)(2,1)S(1)}, bf16[2,4,40,256]{3,2,1,0:T(8,128)(2,1)S(1)}, u32[]{:S(2)}, u32[]{:S(2)}) %collective-permute-start.7) | collective-permute-done | bytes 163872 | tf_op jit(solution)/shard_map/ppermute | solution.py:278
  83.9 3.0 %copy-done.3 = bf16[1,27,256,512]{3,2,1,0:T(8,128)(2,1)S(1)} copy-done((bf16[1,27,256,512]{3,2,1,0:T(8,128)(2,1)S(1)}, bf16[1,27,256,512]{3,2,1,0:T(8,128)(2,1)}, u32[]{:S(2)}) %copy-start.3) | copy-done | bytes 7077912
  87.0 2.5 %shard_map.54 = bf16[320,512]{1,0:T(8,128)(2,1)S(1)} custom-call(bf16[2,4,40,256]{3,2,1,0:T(8,128)(2,1)S(1)} %collective-permute-done.7.cur_ref.later_ref, bf16[2,4,40,256]{3,2,1,0:T(8,128)(2,1)S(1)} %collective-permute-done.5.cur_ref.later_ref, bf16[27,256,512]{2,1,0:T(8,128)(2,1)S(1)} %bitcast.175), custom_call_target="tpu_custom_call" | custom-call | flops 2264924160 | bytes 7077888 | tf_op jit(solution)/shard_map/pallas_call | solution.py:47
  92.6 1.3 collective-permute-start.9
  93.9 7.2 %collective-permute-done.9.cur_ref.later_ref = bf16[2,4,40,256]{3,2,1,0:T(8,128)(2,1)S(1)} collective-permute-done((bf16[2,4,40,256]{3,2,1,0:T(8,128)(2,1)S(1)}, bf16[2,4,40,256]{3,2,1,0:T(8,128)(2,1)S(1)}, u32[]{:S(2)}, u32[]{:S(2)}) %collective-permute-start.9) | collective-permute-done | bytes 163872 | tf_op jit(solution)/shard_map/ppermute | solution.py:278
  101.1 3.0 %copy-done.4 = bf16[1,27,256,512]{3,2,1,0:T(8,128)(2,1)S(1)} copy-done((bf16[1,27,256,512]{3,2,1,0:T(8,128)(2,1)S(1)}, bf16[1,27,256,512]{3,2,1,0:T(8,128)(2,1)}, u32[]{:S(2)}) %copy-start.4) | copy-done | bytes 7077912
  104.1 2.4 %shard_map.55 = bf16[320,512]{1,0:T(8,128)(2,1)S(1)} custom-call(bf16[2,4,40,256]{3,2,1,0:T(8,128)(2,1)S(1)} %collective-permute-done.9.cur_ref.later_ref, bf16[2,4,40,256]{3,2,1,0:T(8,128)(2,1)S(1)} %collective-permute-done.7.cur_ref.later_ref, bf16[27,256,512]{2,1,0:T(8,128)(2,1)S(1)} %bitcast.176), custom_call_target="tpu_custom_call" | custom-call | flops 2264924160 | bytes 7077888 | tf_op jit(solution)/shard_map/pallas_call | solution.py:47
  108.9 1.3 collective-permute-start.11
  110.3 6.7 %collective-permute-done.11.cur_ref = bf16[2,4,40,256]{3,2,1,0:T(8,128)(2,1)S(1)} collective-permute-done((bf16[2,4,40,256]{3,2,1,0:T(8,128)(2,1)S(1)}, bf16[2,4,40,256]{3,2,1,0:T(8,128)(2,1)S(1)}, u32[]{:S(2)}, u32[]{:S(2)}) %collective-permute-start.11) | collective-permute-done | bytes 163872 | tf_op jit(solution)/shard_map/ppermute | solution.py:278
  117.8 3.0 %copy-done.5 = bf16[1,27,256,512]{3,2,1,0:T(8,128)(2,1)S(1)} copy-done((bf16[1,27,256,512]{3,2,1,0:T(8,128)(2,1)S(1)}, bf16[1,27,256,512]{3,2,1,0:T(8,128)(2,1)}, u32[]{:S(2)}) %copy-start.5) | copy-done | bytes 7077912
  120.8 2.4 %shard_map.56 = bf16[320,512]{1,0:T(8,128)(2,1)S(1)} custom-call(bf16[2,4,40,256]{3,2,1,0:T(8,128)(2,1)S(1)} %collective-permute-done.11.cur_ref, bf16[2,4,40,256]{3,2,1,0:T(8,128)(2,1)S(1)} %collective-permute-done.9.cur_ref.later_ref, bf16[27,256,512]{2,1,0:T(8,128)(2,1)S(1)} %bitcast.177), custom_call_target="tpu_custom_call" | custom-call | flops 2264924160 | bytes 7077888 | tf_op jit(solution)/shard_map/pallas_call | solution.py:47
  123.3 2.3 %collective-permute-start.14 = (bf16[4,4,32,256]{3,2,1,0:T(8,128)(2,1)}, bf16[4,4,32,256]{3,2,1,0:T(8,128)(2,1)}, u32[]{:S(2)}, u32[]{:S(2)}) collective-permute-start(bf16[4,4,32,256]{3,2,1,0:T(8,128)(2,1)} %bitcast.199), channel_id=1, source_target_pairs={{0,4},{2,6},{4,0},{6,2},{1,5},{3,7},{5,1},{7,3},{8,12},{10,14},{12... | collective-permute-start | bytes 786440 | tf_op jit(solution)/shard_map/ppermute | solution.py:255
  125.7 2.1 %collective-permute-start.13 = (bf16[4,4,32,256]{3,2,1,0:T(8,128)(2,1)}, bf16[4,4,32,256]{3,2,1,0:T(8,128)(2,1)}, u32[]{:S(2)}, u32[]{:S(2)}) collective-permute-start(bf16[4,4,32,256]{3,2,1,0:T(8,128)(2,1)} %bitcast.200), channel_id=1, source_target_pairs={{0,2},{2,4},{4,6},{6,0},{1,3},{3,5},{5,7},{7,1},{8,10},{10,12},{12... | collective-permute-start | bytes 786440 | tf_op jit(solution)/shard_map/ppermute | solution.py:255
  127.8 1.7 collective-permute-start.12
  129.5 20.9 %shard_map.57.refs_2_ = bf16[27,256,512]{2,1,0:T(8,128)(2,1)} custom-call(s32[1]{0:T(128)} %bitcast.67.refs_0_, bf16[4,2,1,1024,256]{4,3,2,1,0:T(8,128)(2,1)} %bitcast.202, bf16[4,4,4,32,256]{4,3,2,1,0:T(8,128)(2,1)} %all-gather.4.cloned.1.call-done.refs_2_), custom_call_target="tpu_custom_call" | custom-call | flops 14495514624 | bytes 21233664 | tf_op jit(solution)/shard_map/pallas_call | solution.py:169
  151.6 3.7 %all-to-all-start.2 = ((bf16[4,8,1,32,256]{4,3,1,2,0:T(8,128)(2,1)}), bf16[4,8,1,32,256]{4,3,1,2,0:T(8,128)(2,1)S(1)}, u32[]{:S(2)}, u32[]{:S(2)}) async-start(bf16[4,8,1,32,256]{4,3,1,2,0:T(8,128)(2,1)} %copy_bitcast_fusion), calls=%async_computation.2 | async-start | bytes 1048576 | tf_op jit(solution)/shard_map/all_to_all | solution.py:289
  155.3 18.7 %shard_map.58 = bf16[27,256,512]{2,1,0:T(8,128)(2,1)} custom-call(s32[1]{0:T(128)} %bitcast.67.refs_0_, bf16[4,2,1,1024,256]{4,3,2,1,0:T(8,128)(2,1)} %bitcast.203, bf16[27,256,512]{2,1,0:T(8,128)(2,1)} %shard_map.57.refs_2_, bf16[4,4,32,256]{3,2,1,0:T(8,128)(2,1)} %bitcast.201, bf16[4,4,32,256]{3,2,1,0:T(8,128)(2,1)} %collective-permute-done.13.refs_4_, ...), custom_call_target="tpu_custom_call" | custom-call | flops 14495514624 | bytes 21233664 | tf_op jit(solution)/shard_map/pallas_call | solution.py:169
  (105 shorter events, 21.2 us)
Async XLA Ops:
  7.2 1.4 copy-start
  9.9 11.8 %all-to-all-start = ((bf16[4,2,2,1,40,256]{5,4,2,3,1,0:T(8,128)(2,1)}), bf16[4,2,2,1,40,256]{5,4,2,3,1,0:T(8,128)(2,1)S(1)}, u32[]{:S(2)}, u32[]{:S(2)}) async-start(bf16[4,2,2,1,40,256]{5,4,2,3,1,0:T(8,128)(2,1)} %pad_maximum_fusion.2), calls=%async_computation | async-start | bytes 655360 | tf_op jit(solution)/shard_map/all_to_all | solution.py:209
  21.7 15.6 %all-to-all-start.1 = ((bf16[4,6,1,40,256]{4,3,1,2,0:T(8,128)(2,1)}), bf16[4,6,1,40,256]{4,3,1,2,0:T(8,128)(2,1)S(1)}, u32[]{:S(2)}, u32[]{:S(2)}) async-start(bf16[4,6,1,40,256]{4,3,1,2,0:T(8,128)(2,1)} %pad_maximum_fusion.1), calls=%async_computation.1 | async-start | bytes 983040 | tf_op jit(solution)/shard_map/all_to_all | solution.py:209
  26.7 74.4 %all-gather.6.cloned.1.call-start = ((), (), s32[]{:S(2)}) async-start(), calls=%async_computation.4 | async-start | bytes 4718592 | tf_op jit(solution)/shard_map/all_gather | solution.py:237
  26.8 3.0 %copy-start.1 = (bf16[1,27,256,512]{3,2,1,0:T(8,128)(2,1)S(1)}, bf16[1,27,256,512]{3,2,1,0:T(8,128)(2,1)}, u32[]{:S(2)}) copy-start(bf16[1,27,256,512]{3,2,1,0:T(8,128)(2,1)} %param.5) | copy-start | bytes 21233668
  32.3 4.1 %collective-permute-start = (bf16[320,256]{1,0:T(8,128)(2,1)S(1)}, bf16[320,256]{1,0:T(8,128)(2,1)S(1)}, u32[]{:S(2)}, u32[]{:S(2)}) collective-permute-start(bf16[320,256]{1,0:T(8,128)(2,1)S(1)} %constant_dynamic-slice_fusion.9), channel_id=1, source_target_pairs={{0,1},{1,0},{2,3},{3,2},{4,5},{5,4},{6,7},{7,6},{8,9},{9,8},{10,11... | collective-permute-start | bytes 491528 | tf_op jit(solution)/shard_map/ppermute | solution.py:262
  36.7 0.8 collective-permute-start.1
  37.5 85.8 %all-gather.4.cloned.1.call-start = ((), (), s32[]{:S(2)}) async-start(), calls=%async_computation.3 | async-start | bytes 1310720 | tf_op jit(solution)/shard_map/all_gather | solution.py:249
  37.7 3.0 %copy-start.2 = (bf16[1,27,256,512]{3,2,1,0:T(8,128)(2,1)S(1)}, bf16[1,27,256,512]{3,2,1,0:T(8,128)(2,1)}, u32[]{:S(2)}) copy-start(bf16[1,27,256,512]{3,2,1,0:T(8,128)(2,1)} %param.5) | copy-start | bytes 21233668
  43.2 2.7 %collective-permute-start.2 = (bf16[320,256]{1,0:T(8,128)(2,1)S(1)}, bf16[320,256]{1,0:T(8,128)(2,1)S(1)}, u32[]{:S(2)}, u32[]{:S(2)}) collective-permute-start(bf16[320,256]{1,0:T(8,128)(2,1)S(1)} %constant_dynamic-slice_fusion.8), channel_id=1, source_target_pairs={{0,1},{1,0},{2,3},{3,2},{4,5},{5,4},{6,7},{7,6},{8,9},{9,8},{10,11... | collective-permute-start | bytes 491528 | tf_op jit(solution)/shard_map/ppermute | solution.py:262
  46.2 0.8 collective-permute-start.3
  49.5 1.5 collective-permute-start.4
  51.3 17.8 %collective-permute-start.5 = (bf16[2,4,40,256]{3,2,1,0:T(8,128)(2,1)S(1)}, bf16[2,4,40,256]{3,2,1,0:T(8,128)(2,1)S(1)}, u32[]{:S(2)}, u32[]{:S(2)}) collective-permute-start(bf16[2,4,40,256]{3,2,1,0:T(8,128)(2,1)S(1)} %get-tuple-element.48), channel_id=1, source_target_pairs={{0,8},{8,16},{16,24},{24,0},{1,9},{9,17},{17,25},{25,1},{2,10},{10... | collective-permute-start | bytes 491528 | tf_op jit(solution)/shard_map/ppermute | solution.py:278
  71.6 1.9 %collective-permute-start.6 = (bf16[320,256]{1,0:T(8,128)(2,1)S(1)}, bf16[320,256]{1,0:T(8,128)(2,1)S(1)}, u32[]{:S(2)}, u32[]{:S(2)}) collective-permute-start(bf16[320,256]{1,0:T(8,128)(2,1)S(1)} %constant_dynamic-slice_fusion.6), channel_id=1, source_target_pairs={{0,1},{1,0},{2,3},{3,2},{4,5},{5,4},{6,7},{7,6},{8,9},{9,8},{10,11... | collective-permute-start | bytes 491528 | tf_op jit(solution)/shard_map/ppermute | solution.py:262
  72.4 9.9 %copy-start.6 = (bf16[7,2,4,32,256]{4,3,2,1,0:T(8,128)(2,1)}, bf16[7,2,4,32,256]{4,3,2,1,0:T(8,128)(2,1)S(1)}, u32[]{:S(2)}) copy-start(bf16[7,2,4,32,256]{4,3,2,1,0:T(8,128)(2,1)S(1)} %fusion.76) | copy-start | bytes 2752516
  73.7 8.6 %collective-permute-start.7 = (bf16[2,4,40,256]{3,2,1,0:T(8,128)(2,1)S(1)}, bf16[2,4,40,256]{3,2,1,0:T(8,128)(2,1)S(1)}, u32[]{:S(2)}, u32[]{:S(2)}) collective-permute-start(bf16[2,4,40,256]{3,2,1,0:T(8,128)(2,1)S(1)} %fusion.39), channel_id=1, source_target_pairs={{0,8},{8,16},{16,24},{1,9},{9,17},{17,25},{2,10},{10,18},{18,26},{... | collective-permute-start | bytes 491528 | tf_op jit(solution)/shard_map/ppermute | solution.py:278
  82.4 0.8 copy-start.8
  83.2 7.1 %copy-start.7 = (bf16[7,2,4,32,256]{4,3,2,1,0:T(8,128)(2,1)S(1)}, bf16[7,2,4,32,256]{4,3,2,1,0:T(8,128)(2,1)}, u32[]{:S(2)}) copy-start(bf16[7,2,4,32,256]{4,3,2,1,0:T(8,128)(2,1)} %copy-done.6) | copy-start | bytes 2752516
  83.9 3.0 %copy-start.3 = (bf16[1,27,256,512]{3,2,1,0:T(8,128)(2,1)S(1)}, bf16[1,27,256,512]{3,2,1,0:T(8,128)(2,1)}, u32[]{:S(2)}) copy-start(bf16[1,27,256,512]{3,2,1,0:T(8,128)(2,1)} %param.5) | copy-start | bytes 21233668
  89.5 1.9 %collective-permute-start.8 = (bf16[320,256]{1,0:T(8,128)(2,1)S(1)}, bf16[320,256]{1,0:T(8,128)(2,1)}, u32[]{:S(2)}, u32[]{:S(2)}) collective-permute-start(bf16[320,256]{1,0:T(8,128)(2,1)S(1)} %constant_dynamic-slice_fusion.4), channel_id=1, source_target_pairs={{0,1},{1,0},{2,3},{3,2},{4,5},{5,4},{6,7},{7,6},{8,9},{9,8},{10,11... | collective-permute-start | bytes 491528 | tf_op jit(solution)/shard_map/ppermute | solution.py:262
  92.6 8.6 %collective-permute-start.9 = (bf16[2,4,40,256]{3,2,1,0:T(8,128)(2,1)S(1)}, bf16[2,4,40,256]{3,2,1,0:T(8,128)(2,1)S(1)}, u32[]{:S(2)}, u32[]{:S(2)}) collective-permute-start(bf16[2,4,40,256]{3,2,1,0:T(8,128)(2,1)S(1)} %fusion.48), channel_id=1, source_target_pairs={{8,16},{16,24},{9,17},{17,25},{10,18},{18,26},{11,19},{19,27},{12,... | collective-permute-start | bytes 491528 | tf_op jit(solution)/shard_map/ppermute | solution.py:278
  101.1 3.0 %copy-start.4 = (bf16[1,27,256,512]{3,2,1,0:T(8,128)(2,1)S(1)}, bf16[1,27,256,512]{3,2,1,0:T(8,128)(2,1)}, u32[]{:S(2)}) copy-start(bf16[1,27,256,512]{3,2,1,0:T(8,128)(2,1)} %param.5) | copy-start | bytes 21233668
  104.1 3.4 %copy-start.9 = (bf16[5,2,4,32,256]{4,3,2,1,0:T(8,128)(2,1)S(1)}, bf16[5,2,4,32,256]{4,3,2,1,0:T(8,128)(2,1)}, u32[]{:S(2)}) copy-start(bf16[5,2,4,32,256]{4,3,2,1,0:T(8,128)(2,1)} %copy-done.8) | copy-start | bytes 1966084
  106.6 2.0 %collective-permute-start.10 = (bf16[320,256]{1,0:T(8,128)(2,1)S(1)}, bf16[320,256]{1,0:T(8,128)(2,1)S(1)}, u32[]{:S(2)}, u32[]{:S(2)}) collective-permute-start(bf16[320,256]{1,0:T(8,128)(2,1)S(1)} %constant_dynamic-slice_fusion.3), channel_id=1, source_target_pairs={{0,1},{1,0},{2,3},{3,2},{4,5},{5,4},{6,7},{7,6},{8,9},{9,8},{10,11... | collective-permute-start | bytes 491528 | tf_op jit(solution)/shard_map/ppermute | solution.py:262
  108.9 8.0 %collective-permute-start.11 = (bf16[2,4,40,256]{3,2,1,0:T(8,128)(2,1)S(1)}, bf16[2,4,40,256]{3,2,1,0:T(8,128)(2,1)S(1)}, u32[]{:S(2)}, u32[]{:S(2)}) collective-permute-start(bf16[2,4,40,256]{3,2,1,0:T(8,128)(2,1)S(1)} %get-tuple-element.56), channel_id=1, source_target_pairs={{16,24},{17,25},{18,26},{19,27},{20,28},{21,29},{22,30},{23,31}} | collective-permute-start | bytes 491528 | tf_op jit(solution)/shard_map/ppermute | solution.py:278
  117.8 3.0 %copy-start.5 = (bf16[1,27,256,512]{3,2,1,0:T(8,128)(2,1)S(1)}, bf16[1,27,256,512]{3,2,1,0:T(8,128)(2,1)}, u32[]{:S(2)}) copy-start(bf16[1,27,256,512]{3,2,1,0:T(8,128)(2,1)} %param.5) | copy-start | bytes 21233668
  123.3 28.3 %collective-permute-start.15 = (bf16[4,4,32,256]{3,2,1,0:T(8,128)(2,1)}, bf16[4,4,32,256]{3,2,1,0:T(8,128)(2,1)}, u32[]{:S(2)}, u32[]{:S(2)}) collective-permute-start(bf16[4,4,32,256]{3,2,1,0:T(8,128)(2,1)} %bitcast.198), channel_id=1, source_target_pairs={{0,6},{2,0},{4,2},{6,4},{1,7},{3,1},{5,3},{7,5},{8,14},{10,8},{12,... | collective-permute-start | bytes 786440 | tf_op jit(solution)/shard_map/ppermute | solution.py:255
  123.3 28.2 %collective-permute-start.14 = (bf16[4,4,32,256]{3,2,1,0:T(8,128)(2,1)}, bf16[4,4,32,256]{3,2,1,0:T(8,128)(2,1)}, u32[]{:S(2)}, u32[]{:S(2)}) collective-permute-start(bf16[4,4,32,256]{3,2,1,0:T(8,128)(2,1)} %bitcast.199), channel_id=1, source_target_pairs={{0,4},{2,6},{4,0},{6,2},{1,5},{3,7},{5,1},{7,3},{8,12},{10,14},{12... | collective-permute-start | bytes 786440 | tf_op jit(solution)/shard_map/ppermute | solution.py:255
  125.7 25.9 %collective-permute-start.13 = (bf16[4,4,32,256]{3,2,1,0:T(8,128)(2,1)}, bf16[4,4,32,256]{3,2,1,0:T(8,128)(2,1)}, u32[]{:S(2)}, u32[]{:S(2)}) collective-permute-start(bf16[4,4,32,256]{3,2,1,0:T(8,128)(2,1)} %bitcast.200), channel_id=1, source_target_pairs={{0,2},{2,4},{4,6},{6,0},{1,3},{3,5},{5,7},{7,1},{8,10},{10,12},{12... | collective-permute-start | bytes 786440 | tf_op jit(solution)/shard_map/ppermute | solution.py:255
  127.8 22.6 %collective-permute-start.12 = (bf16[320,256]{1,0:T(8,128)(2,1)S(1)}, bf16[320,256]{1,0:T(8,128)(2,1)S(1)}, u32[]{:S(2)}, u32[]{:S(2)}) collective-permute-start(bf16[320,256]{1,0:T(8,128)(2,1)S(1)} %constant_dynamic-slice_fusion.1), channel_id=1, source_target_pairs={{0,1},{1,0},{2,3},{3,2},{4,5},{5,4},{6,7},{7,6},{8,9},{9,8},{10,11... | collective-permute-start | bytes 491528 | tf_op jit(solution)/shard_map/ppermute | solution.py:262
  151.6 22.4 %all-to-all-start.2 = ((bf16[4,8,1,32,256]{4,3,1,2,0:T(8,128)(2,1)}), bf16[4,8,1,32,256]{4,3,1,2,0:T(8,128)(2,1)S(1)}, u32[]{:S(2)}, u32[]{:S(2)}) async-start(bf16[4,8,1,32,256]{4,3,1,2,0:T(8,128)(2,1)} %copy_bitcast_fusion), calls=%async_computation.2 | async-start | bytes 1048576 | tf_op jit(solution)/shard_map/all_to_all | solution.py:289
Sparse Core Ops, SparseCore 0:
  37.6 52.9 all-gather.5
  92.2 27.5 all-gather.3

commit v3 on v2

--- a/solution.py
+++ b/solution.py
@@ -103,7 +103,8 @@
         for copy in g_copies:
             copy.wait()
         for frame in range(frames_n):
-            joined = [cells_ref[piece, frame, row] for row in range(rows_n) for piece in range(pieces_n)]
+            held = frames_n - (frame // BLOCK_FRAMES + 1) * BLOCK_FRAMES + frame % BLOCK_FRAMES
+            joined = [cells_ref[piece, held, row] for row in range(rows_n) for piece in range(pieces_n)]
             turned = lax.dot_general(
                 identity,
                 jnp.concatenate(joined, axis=0),
@@ -242,7 +243,7 @@
         if tick in (ticks - 1 - blocks_n // 2, ticks - 1):
             begin = len(gathered) * (blocks_n // 2)
             taken = jnp.stack(held[begin:])
-            taken = lax.dynamic_slice_in_dim(taken, section_pos, blocks_n // 2, 0)[::-1]
+            taken = lax.dynamic_slice_in_dim(taken, section_pos, blocks_n // 2, 0)
             taken, current = lax.optimization_barrier((taken, current))
             taken = taken.reshape(half, rows_n, own, group)
             if not begin:

time: 183 us -> 179 us (0.978)
  the two profiles are of different devices: /device:TPU:15 before, /device:TPU:0 now
where the time goes in v3:
time: 179 us; the launch traced here: 178 us
  Pallas kernels  56.7 us (32%)
  waiting for transfers between devices  54.4 us (30%)
  starting transfers between devices  31 us (17%)
  local copies, waits for them, and re-layouts  17.1 us (10%)
  between operations  14.6 us (8%)
  other arithmetic  4.68 us (3%)
    pallas_call x2, Pallas kernels, kernel_gradient(): pl.pallas_call(functools.partial(tap_kernel, first, f_first, has_sum), gr...  39.6 us
    ppermute x6, waiting for transfers between devices, body(): current = lax.ppermute(updated, 'section', pairs)  17.1 us
    pallas_call x7, Pallas kernels, back_block(): pl.pallas_call(back_kernel, in_specs=[held, held, held], out_specs=held,...  17.1 us
    all_gather x1, waiting for transfers between devices, body(): gathered.append([lax.all_gather(taken, 'frame')])  17 us
    ppermute x6, starting transfers between devices, body(): current = lax.ppermute(updated, 'section', pairs)  12.4 us
    unnamed x29, local copies, waits for them, and re-layouts  12.1 us
    all_to_all x2, waiting for transfers between devices, to_columns(): pieces = lax.all_to_all(pieces, 'frame', 0, 0)  10.6 us
    all_to_all x2, starting transfers between devices, to_columns(): pieces = lax.all_to_all(pieces, 'frame', 0, 0)  9.79 us
  transfers between devices with their start and end apart: 21, of which 14 were waited for; matrix products, arithmetic and copies ran while one was open for 5% of the time, Pallas kernels for 32%

profile of v3, /device:TPU:0, one launch (start us, length us, event | category | flops | bytes accessed | tf_op | source)
XLA Modules:
  0.0 178.4 jit_solution(15179033025995731925)
XLA Ops:
  7.2 1.3 constant_dynamic-slice_fusion.11
  9.9 6.3 %all-to-all-start = ((bf16[4,2,2,1,40,256]{5,4,2,3,1,0:T(8,128)(2,1)}), bf16[4,2,2,1,40,256]{5,4,2,3,1,0:T(8,128)(2,1)S(1)}, u32[]{:S(2)}, u32[]{:S(2)}) async-start(bf16[4,2,2,1,40,256]{5,4,2,3,1,0:T(8,128)(2,1)} %pad_maximum_fusion.2), calls=%async_computation | async-start | bytes 655360 | tf_op jit(solution)/shard_map/all_to_all | solution.py:210
  17.3 9.2 %all-to-all-done = bf16[4,2,2,1,40,256]{5,4,2,3,1,0:T(8,128)(2,1)S(1)} async-done(((bf16[4,2,2,1,40,256]{5,4,2,3,1,0:T(8,128)(2,1)}), bf16[4,2,2,1,40,256]{5,4,2,3,1,0:T(8,128)(2,1)S(1)}, u32[]{:S(2)}, u32[]{:S(2)}) %all-to-all-start) | async-done | bytes 327712 | tf_op jit(solution)/shard_map/all_to_all | solution.py:210
  26.5 3.5 %all-to-all-start.1 = ((bf16[4,6,1,40,256]{4,3,1,2,0:T(8,128)(2,1)}), bf16[4,6,1,40,256]{4,3,1,2,0:T(8,128)(2,1)S(1)}, u32[]{:S(2)}, u32[]{:S(2)}) async-start(bf16[4,6,1,40,256]{4,3,1,2,0:T(8,128)(2,1)} %pad_maximum_fusion.1), calls=%async_computation.1 | async-start | bytes 983040 | tf_op jit(solution)/shard_map/all_to_all | solution.py:210
  30.1 3.0 %copy-done.1 = bf16[1,27,256,512]{3,2,1,0:T(8,128)(2,1)S(1)} copy-done((bf16[1,27,256,512]{3,2,1,0:T(8,128)(2,1)S(1)}, bf16[1,27,256,512]{3,2,1,0:T(8,128)(2,1)}, u32[]{:S(2)}) %copy-start.1) | copy-done | bytes 7077912
  33.1 2.4 %shard_map.50 = bf16[320,512]{1,0:T(8,128)(2,1)S(1)} custom-call(bf16[2,4,40,256]{3,2,1,0:T(8,128)(2,1)S(1)} %broadcast_select_fusion.3.cur_ref.later_ref, bf16[2,4,40,256]{3,2,1,0:T(8,128)(2,1)S(1)} %broadcast_in_dim.44.later_ref, bf16[27,256,512]{2,1,0:T(8,128)(2,1)S(1)} %bitcast.171), custom_call_target="tpu_custom_call" | custom-call | flops 2264924160 | bytes 7077888 | tf_op jit(solution)/shard_map/pallas_call | solution.py:47
  37.4 3.4 %collective-permute-start.1 = (bf16[2,4,40,256]{3,2,1,0:T(8,128)(2,1)S(1)}, bf16[2,4,40,256]{3,2,1,0:T(8,128)(2,1)S(1)}, u32[]{:S(2)}, u32[]{:S(2)}) collective-permute-start(bf16[2,4,40,256]{3,2,1,0:T(8,128)(2,1)S(1)} %get-tuple-element.52), channel_id=1, source_target_pairs={{0,8},{8,0},{1,9},{9,1},{2,10},{10,2},{3,11},{11,3},{4,12},{12,4},... | collective-permute-start | bytes 491528 | tf_op jit(solution)/shard_map/ppermute | solution.py:279
  40.8 1.3 all-to-all-done.1
  42.2 3.4 %collective-permute-done.1.cur_ref.later_ref = bf16[2,4,40,256]{3,2,1,0:T(8,128)(2,1)S(1)} collective-permute-done((bf16[2,4,40,256]{3,2,1,0:T(8,128)(2,1)S(1)}, bf16[2,4,40,256]{3,2,1,0:T(8,128)(2,1)S(1)}, u32[]{:S(2)}, u32[]{:S(2)}) %collective-permute-start.1) | collective-permute-done | bytes 163872 | tf_op jit(solution)/shard_map/ppermute | solution.py:279
  45.8 3.0 %copy-done.2 = bf16[1,27,256,512]{3,2,1,0:T(8,128)(2,1)S(1)} copy-done((bf16[1,27,256,512]{3,2,1,0:T(8,128)(2,1)S(1)}, bf16[1,27,256,512]{3,2,1,0:T(8,128)(2,1)}, u32[]{:S(2)}) %copy-start.2) | copy-done | bytes 7077912
  48.8 2.4 %shard_map.51 = bf16[320,512]{1,0:T(8,128)(2,1)S(1)} custom-call(bf16[2,4,40,256]{3,2,1,0:T(8,128)(2,1)S(1)} %collective-permute-done.1.cur_ref.later_ref, bf16[2,4,40,256]{3,2,1,0:T(8,128)(2,1)S(1)} %broadcast_select_fusion.3.cur_ref.later_ref, bf16[27,256,512]{2,1,0:T(8,128)(2,1)S(1)} %bitcast.172), custom_call_target="tpu_custom_call" | custom-call | flops 2264924160 | bytes 7077888 | tf_op jit(solution)/shard_map/pallas_call | solution.py:47
  51.4 1.3 collective-permute-done.2
  53.1 3.4 %collective-permute-start.3 = (bf16[2,4,40,256]{3,2,1,0:T(8,128)(2,1)S(1)}, bf16[2,4,40,256]{3,2,1,0:T(8,128)(2,1)S(1)}, u32[]{:S(2)}, u32[]{:S(2)}) collective-permute-start(bf16[2,4,40,256]{3,2,1,0:T(8,128)(2,1)S(1)} %get-tuple-element.50), channel_id=1, source_target_pairs={{0,8},{8,16},{16,0},{1,9},{9,17},{17,1},{2,10},{10,18},{18,2},{3,1... | collective-permute-start | bytes 491528 | tf_op jit(solution)/shard_map/ppermute | solution.py:279
  56.6 4.6 %collective-permute-done.3.cur_ref.later_ref = bf16[2,4,40,256]{3,2,1,0:T(8,128)(2,1)S(1)} collective-permute-done((bf16[2,4,40,256]{3,2,1,0:T(8,128)(2,1)S(1)}, bf16[2,4,40,256]{3,2,1,0:T(8,128)(2,1)S(1)}, u32[]{:S(2)}, u32[]{:S(2)}) %collective-permute-start.3) | collective-permute-done | bytes 163872 | tf_op jit(solution)/shard_map/ppermute | solution.py:279
  61.2 2.4 %shard_map.52 = bf16[320,512]{1,0:T(8,128)(2,1)S(1)} custom-call(bf16[2,4,40,256]{3,2,1,0:T(8,128)(2,1)S(1)} %collective-permute-done.3.cur_ref.later_ref, bf16[2,4,40,256]{3,2,1,0:T(8,128)(2,1)S(1)} %collective-permute-done.1.cur_ref.later_ref, bf16[27,256,512]{2,1,0:T(8,128)(2,1)S(1)} %bitcast.173), custom_call_target="tpu_custom_call" | custom-call | flops 2264924160 | bytes 7077888 | tf_op jit(solution)/shard_map/pallas_call | solution.py:47
  63.8 1.3 collective-permute-done.4
  65.5 1.5 collective-permute-start.5
  67.1 5.6 %collective-permute-done.5.cur_ref.later_ref = bf16[2,4,40,256]{3,2,1,0:T(8,128)(2,1)S(1)} collective-permute-done((bf16[2,4,40,256]{3,2,1,0:T(8,128)(2,1)S(1)}, bf16[2,4,40,256]{3,2,1,0:T(8,128)(2,1)S(1)}, u32[]{:S(2)}, u32[]{:S(2)}) %collective-permute-start.5) | collective-permute-done | bytes 163872 | tf_op jit(solution)/shard_map/ppermute | solution.py:279
  72.7 2.4 %shard_map.53 = bf16[320,512]{1,0:T(8,128)(2,1)S(1)} custom-call(bf16[2,4,40,256]{3,2,1,0:T(8,128)(2,1)S(1)} %collective-permute-done.5.cur_ref.later_ref, bf16[2,4,40,256]{3,2,1,0:T(8,128)(2,1)S(1)} %collective-permute-done.3.cur_ref.later_ref, bf16[27,256,512]{2,1,0:T(8,128)(2,1)S(1)} %bitcast.174), custom_call_target="tpu_custom_call" | custom-call | flops 2264924160 | bytes 7077888 | tf_op jit(solution)/shard_map/pallas_call | solution.py:47
  75.3 1.3 collective-permute-done.6
  76.8 2.7 %collective-permute-start.7 = (bf16[2,4,40,256]{3,2,1,0:T(8,128)(2,1)S(1)}, bf16[2,4,40,256]{3,2,1,0:T(8,128)(2,1)S(1)}, u32[]{:S(2)}, u32[]{:S(2)}) collective-permute-start(bf16[2,4,40,256]{3,2,1,0:T(8,128)(2,1)S(1)} %fusion.39), channel_id=1, source_target_pairs={{0,8},{8,16},{16,24},{1,9},{9,17},{17,25},{2,10},{10,18},{18,26},{... | collective-permute-start | bytes 491528 | tf_op jit(solution)/shard_map/ppermute | solution.py:279
  79.6 3.5 %collective-permute-done.7.cur_ref.later_ref = bf16[2,4,40,256]{3,2,1,0:T(8,128)(2,1)S(1)} collective-permute-done((bf16[2,4,40,256]{3,2,1,0:T(8,128)(2,1)S(1)}, bf16[2,4,40,256]{3,2,1,0:T(8,128)(2,1)S(1)}, u32[]{:S(2)}, u32[]{:S(2)}) %collective-permute-start.7) | collective-permute-done | bytes 163872 | tf_op jit(solution)/shard_map/ppermute | solution.py:279
  83.9 2.4 %shard_map.54 = bf16[320,512]{1,0:T(8,128)(2,1)S(1)} custom-call(bf16[2,4,40,256]{3,2,1,0:T(8,128)(2,1)S(1)} %collective-permute-done.7.cur_ref.later_ref, bf16[2,4,40,256]{3,2,1,0:T(8,128)(2,1)S(1)} %collective-permute-done.5.cur_ref.later_ref, bf16[27,256,512]{2,1,0:T(8,128)(2,1)S(1)} %bitcast.175), custom_call_target="tpu_custom_call" | custom-call | flops 2264924160 | bytes 7077888 | tf_op jit(solution)/shard_map/pallas_call | solution.py:47
  89.5 3.9 %all-gather.6.cloned.1.call-done = bf16[8,1024,256]{2,1,0:T(8,128)(2,1)} async-done(((bf16[1,1024,256]{2,1,0:T(8,128)(2,1)}), bf16[8,1024,256]{2,1,0:T(8,128)(2,1)}) %all-gather.6.cloned.1.call-update) | async-done | bytes 4194320 | tf_op jit(solution)/shard_map/all_gather | solution.py:238
  93.3 3.0 %copy-done.3 = bf16[1,27,256,512]{3,2,1,0:T(8,128)(2,1)S(1)} copy-done((bf16[1,27,256,512]{3,2,1,0:T(8,128)(2,1)S(1)}, bf16[1,27,256,512]{3,2,1,0:T(8,128)(2,1)}, u32[]{:S(2)}) %copy-start.3) | copy-done | bytes 7077912
  96.4 2.5 %shard_map.55 = bf16[320,512]{1,0:T(8,128)(2,1)S(1)} custom-call(bf16[2,4,40,256]{3,2,1,0:T(8,128)(2,1)S(1)} %collective-permute-done.9.cur_ref.later_ref, bf16[2,4,40,256]{3,2,1,0:T(8,128)(2,1)S(1)} %collective-permute-done.7.cur_ref.later_ref, bf16[27,256,512]{2,1,0:T(8,128)(2,1)S(1)} %bitcast.176), custom_call_target="tpu_custom_call" | custom-call | flops 2264924160 | bytes 7077888 | tf_op jit(solution)/shard_map/pallas_call | solution.py:47
  102.2 2.4 %shard_map.56 = bf16[320,512]{1,0:T(8,128)(2,1)S(1)} custom-call(bf16[2,4,40,256]{3,2,1,0:T(8,128)(2,1)S(1)} %collective-permute-done.11.cur_ref, bf16[2,4,40,256]{3,2,1,0:T(8,128)(2,1)S(1)} %collective-permute-done.9.cur_ref.later_ref, bf16[27,256,512]{2,1,0:T(8,128)(2,1)S(1)} %bitcast.177), custom_call_target="tpu_custom_call" | custom-call | flops 2264924160 | bytes 7077888 | tf_op jit(solution)/shard_map/pallas_call | solution.py:47
  104.6 17.0 %all-gather.4.cloned.1.call-done.refs_2_ = bf16[4,4,4,32,256]{4,3,2,1,0:T(8,128)(2,1)} async-done(((bf16[1,4,4,32,256]{4,3,2,1,0:T(8,128)(2,1)}), bf16[4,4,4,32,256]{4,3,2,1,0:T(8,128)(2,1)}) %all-gather.4.cloned.1.call-update) | async-done | bytes 1048592 | tf_op jit(solution)/shard_map/all_gather | solution.py:250
  121.6 1.9 %collective-permute-start.15 = (bf16[4,4,32,256]{3,2,1,0:T(8,128)(2,1)}, bf16[4,4,32,256]{3,2,1,0:T(8,128)(2,1)}, u32[]{:S(2)}, u32[]{:S(2)}) collective-permute-start(bf16[4,4,32,256]{3,2,1,0:T(8,128)(2,1)} %bitcast.198), channel_id=1, source_target_pairs={{0,6},{2,0},{4,2},{6,4},{1,7},{3,1},{5,3},{7,5},{8,14},{10,8},{12,... | collective-permute-start | bytes 786440 | tf_op jit(solution)/shard_map/ppermute | solution.py:256
  125.6 20.9 %shard_map.57.refs_2_ = bf16[27,256,512]{2,1,0:T(8,128)(2,1)} custom-call(s32[1]{0:T(128)} %bitcast.67.refs_0_, bf16[4,2,1,1024,256]{4,3,2,1,0:T(8,128)(2,1)} %bitcast.202, bf16[4,4,4,32,256]{4,3,2,1,0:T(8,128)(2,1)} %all-gather.4.cloned.1.call-done.refs_2_), custom_call_target="tpu_custom_call" | custom-call | flops 14495514624 | bytes 21233664 | tf_op jit(solution)/shard_map/pallas_call | solution.py:170
  147.7 4.1 %all-to-all-start.2 = ((bf16[4,8,1,32,256]{4,3,1,2,0:T(8,128)(2,1)}), bf16[4,8,1,32,256]{4,3,1,2,0:T(8,128)(2,1)S(1)}, u32[]{:S(2)}, u32[]{:S(2)}) async-start(bf16[4,8,1,32,256]{4,3,1,2,0:T(8,128)(2,1)} %copy_bitcast_fusion), calls=%async_computation.2 | async-start | bytes 1048576 | tf_op jit(solution)/shard_map/all_to_all | solution.py:290
  151.8 18.7 %shard_map.58 = bf16[27,256,512]{2,1,0:T(8,128)(2,1)} custom-call(s32[1]{0:T(128)} %bitcast.67.refs_0_, bf16[4,2,1,1024,256]{4,3,2,1,0:T(8,128)(2,1)} %bitcast.203, bf16[27,256,512]{2,1,0:T(8,128)(2,1)} %shard_map.57.refs_2_, bf16[4,4,32,256]{3,2,1,0:T(8,128)(2,1)} %bitcast.201, bf16[4,4,32,256]{3,2,1,0:T(8,128)(2,1)} %collective-permute-done.13.refs_4_, ...), custom_call_target="tpu_custom_call" | custom-call | flops 14495514624 | bytes 21233664 | tf_op jit(solution)/shard_map/pallas_call | solution.py:170
  (99 shorter events, 17.5 us)
Async XLA Ops:
  7.2 1.4 copy-start
  9.9 16.6 %all-to-all-start = ((bf16[4,2,2,1,40,256]{5,4,2,3,1,0:T(8,128)(2,1)}), bf16[4,2,2,1,40,256]{5,4,2,3,1,0:T(8,128)(2,1)S(1)}, u32[]{:S(2)}, u32[]{:S(2)}) async-start(bf16[4,2,2,1,40,256]{5,4,2,3,1,0:T(8,128)(2,1)} %pad_maximum_fusion.2), calls=%async_computation | async-start | bytes 655360 | tf_op jit(solution)/shard_map/all_to_all | solution.py:210
  26.5 15.6 %all-to-all-start.1 = ((bf16[4,6,1,40,256]{4,3,1,2,0:T(8,128)(2,1)}), bf16[4,6,1,40,256]{4,3,1,2,0:T(8,128)(2,1)S(1)}, u32[]{:S(2)}, u32[]{:S(2)}) async-start(bf16[4,6,1,40,256]{4,3,1,2,0:T(8,128)(2,1)} %pad_maximum_fusion.1), calls=%async_computation.1 | async-start | bytes 983040 | tf_op jit(solution)/shard_map/all_to_all | solution.py:210
  30.0 63.3 %all-gather.6.cloned.1.call-start = ((), (), s32[]{:S(2)}) async-start(), calls=%async_computation.4 | async-start | bytes 4718592 | tf_op jit(solution)/shard_map/all_gather | solution.py:238
  30.1 3.0 %copy-start.1 = (bf16[1,27,256,512]{3,2,1,0:T(8,128)(2,1)S(1)}, bf16[1,27,256,512]{3,2,1,0:T(8,128)(2,1)}, u32[]{:S(2)}) copy-start(bf16[1,27,256,512]{3,2,1,0:T(8,128)(2,1)} %param.5) | copy-start | bytes 21233668
  35.6 1.5 collective-permute-start
  37.4 8.2 %collective-permute-start.1 = (bf16[2,4,40,256]{3,2,1,0:T(8,128)(2,1)S(1)}, bf16[2,4,40,256]{3,2,1,0:T(8,128)(2,1)S(1)}, u32[]{:S(2)}, u32[]{:S(2)}) collective-permute-start(bf16[2,4,40,256]{3,2,1,0:T(8,128)(2,1)S(1)} %get-tuple-element.52), channel_id=1, source_target_pairs={{0,8},{8,0},{1,9},{9,1},{2,10},{10,2},{3,11},{11,3},{4,12},{12,4},... | collective-permute-start | bytes 491528 | tf_op jit(solution)/shard_map/ppermute | solution.py:279
  45.6 76.0 %all-gather.4.cloned.1.call-start = ((), (), s32[]{:S(2)}) async-start(), calls=%async_computation.3 | async-start | bytes 1310720 | tf_op jit(solution)/shard_map/all_gather | solution.py:250
  45.8 3.0 %copy-start.2 = (bf16[1,27,256,512]{3,2,1,0:T(8,128)(2,1)S(1)}, bf16[1,27,256,512]{3,2,1,0:T(8,128)(2,1)}, u32[]{:S(2)}) copy-start(bf16[1,27,256,512]{3,2,1,0:T(8,128)(2,1)} %param.5) | copy-start | bytes 21233668
  51.3 1.5 collective-permute-start.2
  53.1 8.1 %collective-permute-start.3 = (bf16[2,4,40,256]{3,2,1,0:T(8,128)(2,1)S(1)}, bf16[2,4,40,256]{3,2,1,0:T(8,128)(2,1)S(1)}, u32[]{:S(2)}, u32[]{:S(2)}) collective-permute-start(bf16[2,4,40,256]{3,2,1,0:T(8,128)(2,1)S(1)} %get-tuple-element.50), channel_id=1, source_target_pairs={{0,8},{8,16},{16,0},{1,9},{9,17},{17,1},{2,10},{10,18},{18,2},{3,1... | collective-permute-start | bytes 491528 | tf_op jit(solution)/shard_map/ppermute | solution.py:279
  63.7 1.5 collective-permute-start.4
  65.5 7.2 %collective-permute-start.5 = (bf16[2,4,40,256]{3,2,1,0:T(8,128)(2,1)S(1)}, bf16[2,4,40,256]{3,2,1,0:T(8,128)(2,1)S(1)}, u32[]{:S(2)}, u32[]{:S(2)}) collective-permute-start(bf16[2,4,40,256]{3,2,1,0:T(8,128)(2,1)S(1)} %get-tuple-element.48), channel_id=1, source_target_pairs={{0,8},{8,16},{16,24},{24,0},{1,9},{9,17},{17,25},{25,1},{2,10},{10... | collective-permute-start | bytes 491528 | tf_op jit(solution)/shard_map/ppermute | solution.py:279
  75.1 1.5 collective-permute-start.6
  76.8 6.2 %collective-permute-start.7 = (bf16[2,4,40,256]{3,2,1,0:T(8,128)(2,1)S(1)}, bf16[2,4,40,256]{3,2,1,0:T(8,128)(2,1)S(1)}, u32[]{:S(2)}, u32[]{:S(2)}) collective-permute-start(bf16[2,4,40,256]{3,2,1,0:T(8,128)(2,1)S(1)} %fusion.39), channel_id=1, source_target_pairs={{0,8},{8,16},{16,24},{1,9},{9,17},{17,25},{2,10},{10,18},{18,26},{... | collective-permute-start | bytes 491528 | tf_op jit(solution)/shard_map/ppermute | solution.py:279
  83.1 3.4 %copy-start.6 = (bf16[5,2,4,32,256]{4,3,2,1,0:T(8,128)(2,1)}, bf16[5,2,4,32,256]{4,3,2,1,0:T(8,128)(2,1)S(1)}, u32[]{:S(2)}) copy-start(bf16[5,2,4,32,256]{4,3,2,1,0:T(8,128)(2,1)S(1)} %get-tuple-element.68) | copy-start | bytes 1966084
  86.4 1.5 collective-permute-start.8
  86.5 0.9 copy-start.4
  88.1 1.4 collective-permute-start.9
  93.3 3.0 %copy-start.3 = (bf16[1,27,256,512]{3,2,1,0:T(8,128)(2,1)S(1)}, bf16[1,27,256,512]{3,2,1,0:T(8,128)(2,1)}, u32[]{:S(2)}) copy-start(bf16[1,27,256,512]{3,2,1,0:T(8,128)(2,1)} %param.5) | copy-start | bytes 21233668
  96.4 2.8 %copy-start.7 = (bf16[5,2,4,32,256]{4,3,2,1,0:T(8,128)(2,1)S(1)}, bf16[5,2,4,32,256]{4,3,2,1,0:T(8,128)(2,1)}, u32[]{:S(2)}) copy-start(bf16[5,2,4,32,256]{4,3,2,1,0:T(8,128)(2,1)} %copy-done.6) | copy-start | bytes 1966084
  96.4 5.0 %copy-start.5 = (bf16[7,2,4,32,256]{4,3,2,1,0:T(8,128)(2,1)S(1)}, bf16[7,2,4,32,256]{4,3,2,1,0:T(8,128)(2,1)}, u32[]{:S(2)}) copy-start(bf16[7,2,4,32,256]{4,3,2,1,0:T(8,128)(2,1)} %fusion.73) | copy-start | bytes 2752516
  98.8 1.5 collective-permute-start.10
  100.6 0.7 collective-permute-start.11
  121.6 26.1 %collective-permute-start.15 = (bf16[4,4,32,256]{3,2,1,0:T(8,128)(2,1)}, bf16[4,4,32,256]{3,2,1,0:T(8,128)(2,1)}, u32[]{:S(2)}, u32[]{:S(2)}) collective-permute-start(bf16[4,4,32,256]{3,2,1,0:T(8,128)(2,1)} %bitcast.198), channel_id=1, source_target_pairs={{0,6},{2,0},{4,2},{6,4},{1,7},{3,1},{5,3},{7,5},{8,14},{10,8},{12,... | collective-permute-start | bytes 786440 | tf_op jit(solution)/shard_map/ppermute | solution.py:256
  123.5 24.2 %collective-permute-start.14 = (bf16[4,4,32,256]{3,2,1,0:T(8,128)(2,1)}, bf16[4,4,32,256]{3,2,1,0:T(8,128)(2,1)}, u32[]{:S(2)}, u32[]{:S(2)}) collective-permute-start(bf16[4,4,32,256]{3,2,1,0:T(8,128)(2,1)} %bitcast.199), channel_id=1, source_target_pairs={{0,4},{2,6},{4,0},{6,2},{1,5},{3,7},{5,1},{7,3},{8,12},{10,14},{12... | collective-permute-start | bytes 786440 | tf_op jit(solution)/shard_map/ppermute | solution.py:256
  124.5 23.2 %collective-permute-start.13 = (bf16[4,4,32,256]{3,2,1,0:T(8,128)(2,1)}, bf16[4,4,32,256]{3,2,1,0:T(8,128)(2,1)}, u32[]{:S(2)}, u32[]{:S(2)}) collective-permute-start(bf16[4,4,32,256]{3,2,1,0:T(8,128)(2,1)} %bitcast.200), channel_id=1, source_target_pairs={{0,2},{2,4},{4,6},{6,0},{1,3},{3,5},{5,7},{7,1},{8,10},{10,12},{12... | collective-permute-start | bytes 786440 | tf_op jit(solution)/shard_map/ppermute | solution.py:256
  125.5 21.0 %collective-permute-start.12 = (bf16[320,256]{1,0:T(8,128)(2,1)S(1)}, bf16[320,256]{1,0:T(8,128)(2,1)S(1)}, u32[]{:S(2)}, u32[]{:S(2)}) collective-permute-start(bf16[320,256]{1,0:T(8,128)(2,1)S(1)} %constant_dynamic-slice_fusion.1), channel_id=1, source_target_pairs={{0,1},{1,0},{2,3},{3,2},{4,5},{5,4},{6,7},{7,6},{8,9},{9,8},{10,11... | collective-permute-start | bytes 491528 | tf_op jit(solution)/shard_map/ppermute | solution.py:263
  147.7 22.7 %all-to-all-start.2 = ((bf16[4,8,1,32,256]{4,3,1,2,0:T(8,128)(2,1)}), bf16[4,8,1,32,256]{4,3,1,2,0:T(8,128)(2,1)S(1)}, u32[]{:S(2)}, u32[]{:S(2)}) async-start(bf16[4,8,1,32,256]{4,3,1,2,0:T(8,128)(2,1)} %copy_bitcast_fusion), calls=%async_computation.2 | async-start | bytes 1048576 | tf_op jit(solution)/shard_map/all_to_all | solution.py:290
Sparse Core Ops, SparseCore 0:
  45.7 47.5 all-gather.5
  94.9 26.6 all-gather.3

commit v4 on v3

--- a/solution.py
+++ b/solution.py
@@ -89,8 +89,10 @@
                         f_here.at[ring * chans + chan],
                     )
                 )
-        for copy in g_copies + f_copies:
+        for copy in g_copies:
             copy.start()
+        for copy in f_copies:
+            copy.start(priority=1)
         same = lax.broadcasted_iota(jnp.int32, (group, group), 0) == lax.broadcasted_iota(jnp.int32, (group, group), 1)
         identity = jnp.where(same, 1.0, 0.0).astype(BF16)
         source = lax.broadcasted_iota(jnp.int32, (width_n, 2 * width_n), 0)

time: 179 us -> 178 us (level)
  transfers between devices with their start and end apart: 21 -> 21, of which waited for: 14 -> 15; matrix products, arithmetic and copies ran while one was open for 5% -> 5% of each run, Pallas kernels for 32% -> 31%
where the time goes in v4:
time: 178 us; the launch traced here: 177 us
  Pallas kernels  55.5 us (31%)
  waiting for transfers between devices  54.8 us (31%)
  starting transfers between devices  30.6 us (17%)
  local copies, waits for them, and re-layouts  17.1 us (10%)
  between operations  14.6 us (8%)
  other arithmetic  4.68 us (3%)
    pallas_call x2, Pallas kernels, kernel_gradient(): pl.pallas_call(functools.partial(tap_kernel, first, f_first, has_sum), gr...  38.4 us
    ppermute x6, waiting for transfers between devices, body(): current = lax.ppermute(updated, 'section', pairs)  17.1 us
    pallas_call x7, Pallas kernels, back_block(): pl.pallas_call(back_kernel, in_specs=[held, held, held], out_specs=held,...  17.1 us
    all_gather x1, waiting for transfers between devices, body(): gathered.append([lax.all_gather(taken, 'frame')])  17 us
    ppermute x6, starting transfers between devices, body(): current = lax.ppermute(updated, 'section', pairs)  12.4 us
    unnamed x29, local copies, waits for them, and re-layouts  12.1 us
    all_to_all x2, waiting for transfers between devices, to_columns(): pieces = lax.all_to_all(pieces, 'frame', 0, 0)  10.6 us
    all_to_all x2, starting transfers between devices, to_columns(): pieces = lax.all_to_all(pieces, 'frame', 0, 0)  9.79 us
  transfers between devices with their start and end apart: 21, of which 15 were waited for; matrix products, arithmetic and copies ran while one was open for 5% of the time, Pallas kernels for 31%

profile of v4, /device:TPU:0, one launch (start us, length us, event | category | flops | bytes accessed | tf_op | source)
XLA Modules:
  0.0 177.3 jit_solution(9588557553192822927)
XLA Ops:
  7.2 1.3 constant_dynamic-slice_fusion.11
  9.9 6.3 %all-to-all-start = ((bf16[4,2,2,1,40,256]{5,4,2,3,1,0:T(8,128)(2,1)}), bf16[4,2,2,1,40,256]{5,4,2,3,1,0:T(8,128)(2,1)S(1)}, u32[]{:S(2)}, u32[]{:S(2)}) async-start(bf16[4,2,2,1,40,256]{5,4,2,3,1,0:T(8,128)(2,1)} %pad_maximum_fusion.2), calls=%async_computation | async-start | bytes 655360 | tf_op jit(solution)/shard_map/all_to_all | solution.py:212
  17.3 9.2 %all-to-all-done = bf16[4,2,2,1,40,256]{5,4,2,3,1,0:T(8,128)(2,1)S(1)} async-done(((bf16[4,2,2,1,40,256]{5,4,2,3,1,0:T(8,128)(2,1)}), bf16[4,2,2,1,40,256]{5,4,2,3,1,0:T(8,128)(2,1)S(1)}, u32[]{:S(2)}, u32[]{:S(2)}) %all-to-all-start) | async-done | bytes 327712 | tf_op jit(solution)/shard_map/all_to_all | solution.py:212
  26.5 3.5 %all-to-all-start.1 = ((bf16[4,6,1,40,256]{4,3,1,2,0:T(8,128)(2,1)}), bf16[4,6,1,40,256]{4,3,1,2,0:T(8,128)(2,1)S(1)}, u32[]{:S(2)}, u32[]{:S(2)}) async-start(bf16[4,6,1,40,256]{4,3,1,2,0:T(8,128)(2,1)} %pad_maximum_fusion.1), calls=%async_computation.1 | async-start | bytes 983040 | tf_op jit(solution)/shard_map/all_to_all | solution.py:212
  30.1 3.0 %copy-done.1 = bf16[1,27,256,512]{3,2,1,0:T(8,128)(2,1)S(1)} copy-done((bf16[1,27,256,512]{3,2,1,0:T(8,128)(2,1)S(1)}, bf16[1,27,256,512]{3,2,1,0:T(8,128)(2,1)}, u32[]{:S(2)}) %copy-start.1) | copy-done | bytes 7077912
  33.1 2.4 %shard_map.50 = bf16[320,512]{1,0:T(8,128)(2,1)S(1)} custom-call(bf16[2,4,40,256]{3,2,1,0:T(8,128)(2,1)S(1)} %broadcast_select_fusion.3.cur_ref.later_ref, bf16[2,4,40,256]{3,2,1,0:T(8,128)(2,1)S(1)} %broadcast_in_dim.44.later_ref, bf16[27,256,512]{2,1,0:T(8,128)(2,1)S(1)} %bitcast.171), custom_call_target="tpu_custom_call" | custom-call | flops 2264924160 | bytes 7077888 | tf_op jit(solution)/shard_map/pallas_call | solution.py:47
  37.4 3.4 %collective-permute-start.1 = (bf16[2,4,40,256]{3,2,1,0:T(8,128)(2,1)S(1)}, bf16[2,4,40,256]{3,2,1,0:T(8,128)(2,1)S(1)}, u32[]{:S(2)}, u32[]{:S(2)}) collective-permute-start(bf16[2,4,40,256]{3,2,1,0:T(8,128)(2,1)S(1)} %get-tuple-element.52), channel_id=1, source_target_pairs={{0,8},{8,0},{1,9},{9,1},{2,10},{10,2},{3,11},{11,3},{4,12},{12,4},... | collective-permute-start | bytes 491528 | tf_op jit(solution)/shard_map/ppermute | solution.py:281
  40.8 1.3 all-to-all-done.1
  42.2 3.4 %collective-permute-done.1.cur_ref.later_ref = bf16[2,4,40,256]{3,2,1,0:T(8,128)(2,1)S(1)} collective-permute-done((bf16[2,4,40,256]{3,2,1,0:T(8,128)(2,1)S(1)}, bf16[2,4,40,256]{3,2,1,0:T(8,128)(2,1)S(1)}, u32[]{:S(2)}, u32[]{:S(2)}) %collective-permute-start.1) | collective-permute-done | bytes 163872 | tf_op jit(solution)/shard_map/ppermute | solution.py:281
  45.8 3.0 %copy-done.2 = bf16[1,27,256,512]{3,2,1,0:T(8,128)(2,1)S(1)} copy-done((bf16[1,27,256,512]{3,2,1,0:T(8,128)(2,1)S(1)}, bf16[1,27,256,512]{3,2,1,0:T(8,128)(2,1)}, u32[]{:S(2)}) %copy-start.2) | copy-done | bytes 7077912
  48.8 2.4 %shard_map.51 = bf16[320,512]{1,0:T(8,128)(2,1)S(1)} custom-call(bf16[2,4,40,256]{3,2,1,0:T(8,128)(2,1)S(1)} %collective-permute-done.1.cur_ref.later_ref, bf16[2,4,40,256]{3,2,1,0:T(8,128)(2,1)S(1)} %broadcast_select_fusion.3.cur_ref.later_ref, bf16[27,256,512]{2,1,0:T(8,128)(2,1)S(1)} %bitcast.172), custom_call_target="tpu_custom_call" | custom-call | flops 2264924160 | bytes 7077888 | tf_op jit(solution)/shard_map/pallas_call | solution.py:47
  51.4 1.3 collective-permute-done.2
  53.1 3.4 %collective-permute-start.3 = (bf16[2,4,40,256]{3,2,1,0:T(8,128)(2,1)S(1)}, bf16[2,4,40,256]{3,2,1,0:T(8,128)(2,1)S(1)}, u32[]{:S(2)}, u32[]{:S(2)}) collective-permute-start(bf16[2,4,40,256]{3,2,1,0:T(8,128)(2,1)S(1)} %get-tuple-element.50), channel_id=1, source_target_pairs={{0,8},{8,16},{16,0},{1,9},{9,17},{17,1},{2,10},{10,18},{18,2},{3,1... | collective-permute-start | bytes 491528 | tf_op jit(solution)/shard_map/ppermute | solution.py:281
  56.6 4.6 %collective-permute-done.3.cur_ref.later_ref = bf16[2,4,40,256]{3,2,1,0:T(8,128)(2,1)S(1)} collective-permute-done((bf16[2,4,40,256]{3,2,1,0:T(8,128)(2,1)S(1)}, bf16[2,4,40,256]{3,2,1,0:T(8,128)(2,1)S(1)}, u32[]{:S(2)}, u32[]{:S(2)}) %collective-permute-start.3) | collective-permute-done | bytes 163872 | tf_op jit(solution)/shard_map/ppermute | solution.py:281
  61.2 2.4 %shard_map.52 = bf16[320,512]{1,0:T(8,128)(2,1)S(1)} custom-call(bf16[2,4,40,256]{3,2,1,0:T(8,128)(2,1)S(1)} %collective-permute-done.3.cur_ref.later_ref, bf16[2,4,40,256]{3,2,1,0:T(8,128)(2,1)S(1)} %collective-permute-done.1.cur_ref.later_ref, bf16[27,256,512]{2,1,0:T(8,128)(2,1)S(1)} %bitcast.173), custom_call_target="tpu_custom_call" | custom-call | flops 2264924160 | bytes 7077888 | tf_op jit(solution)/shard_map/pallas_call | solution.py:47
  63.8 1.3 collective-permute-done.4
  65.5 1.5 collective-permute-start.5
  67.1 5.6 %collective-permute-done.5.cur_ref.later_ref = bf16[2,4,40,256]{3,2,1,0:T(8,128)(2,1)S(1)} collective-permute-done((bf16[2,4,40,256]{3,2,1,0:T(8,128)(2,1)S(1)}, bf16[2,4,40,256]{3,2,1,0:T(8,128)(2,1)S(1)}, u32[]{:S(2)}, u32[]{:S(2)}) %collective-permute-start.5) | collective-permute-done | bytes 163872 | tf_op jit(solution)/shard_map/ppermute | solution.py:281
  72.7 2.4 %shard_map.53 = bf16[320,512]{1,0:T(8,128)(2,1)S(1)} custom-call(bf16[2,4,40,256]{3,2,1,0:T(8,128)(2,1)S(1)} %collective-permute-done.5.cur_ref.later_ref, bf16[2,4,40,256]{3,2,1,0:T(8,128)(2,1)S(1)} %collective-permute-done.3.cur_ref.later_ref, bf16[27,256,512]{2,1,0:T(8,128)(2,1)S(1)} %bitcast.174), custom_call_target="tpu_custom_call" | custom-call | flops 2264924160 | bytes 7077888 | tf_op jit(solution)/shard_map/pallas_call | solution.py:47
  75.3 1.3 collective-permute-done.6
  76.8 2.7 %collective-permute-start.7 = (bf16[2,4,40,256]{3,2,1,0:T(8,128)(2,1)S(1)}, bf16[2,4,40,256]{3,2,1,0:T(8,128)(2,1)S(1)}, u32[]{:S(2)}, u32[]{:S(2)}) collective-permute-start(bf16[2,4,40,256]{3,2,1,0:T(8,128)(2,1)S(1)} %fusion.39), channel_id=1, source_target_pairs={{0,8},{8,16},{16,24},{1,9},{9,17},{17,25},{2,10},{10,18},{18,26},{... | collective-permute-start | bytes 491528 | tf_op jit(solution)/shard_map/ppermute | solution.py:281
  79.6 3.5 %collective-permute-done.7.cur_ref.later_ref = bf16[2,4,40,256]{3,2,1,0:T(8,128)(2,1)S(1)} collective-permute-done((bf16[2,4,40,256]{3,2,1,0:T(8,128)(2,1)S(1)}, bf16[2,4,40,256]{3,2,1,0:T(8,128)(2,1)S(1)}, u32[]{:S(2)}, u32[]{:S(2)}) %collective-permute-start.7) | collective-permute-done | bytes 163872 | tf_op jit(solution)/shard_map/ppermute | solution.py:281
  83.9 2.4 %shard_map.54 = bf16[320,512]{1,0:T(8,128)(2,1)S(1)} custom-call(bf16[2,4,40,256]{3,2,1,0:T(8,128)(2,1)S(1)} %collective-permute-done.7.cur_ref.later_ref, bf16[2,4,40,256]{3,2,1,0:T(8,128)(2,1)S(1)} %collective-permute-done.5.cur_ref.later_ref, bf16[27,256,512]{2,1,0:T(8,128)(2,1)S(1)} %bitcast.175), custom_call_target="tpu_custom_call" | custom-call | flops 2264924160 | bytes 7077888 | tf_op jit(solution)/shard_map/pallas_call | solution.py:47
  89.5 3.9 %all-gather.6.cloned.1.call-done = bf16[8,1024,256]{2,1,0:T(8,128)(2,1)} async-done(((bf16[1,1024,256]{2,1,0:T(8,128)(2,1)}), bf16[8,1024,256]{2,1,0:T(8,128)(2,1)}) %all-gather.6.cloned.1.call-update) | async-done | bytes 4194320 | tf_op jit(solution)/shard_map/all_gather | solution.py:240
  93.3 3.0 %copy-done.3 = bf16[1,27,256,512]{3,2,1,0:T(8,128)(2,1)S(1)} copy-done((bf16[1,27,256,512]{3,2,1,0:T(8,128)(2,1)S(1)}, bf16[1,27,256,512]{3,2,1,0:T(8,128)(2,1)}, u32[]{:S(2)}) %copy-start.3) | copy-done | bytes 7077912
  96.4 2.5 %shard_map.55 = bf16[320,512]{1,0:T(8,128)(2,1)S(1)} custom-call(bf16[2,4,40,256]{3,2,1,0:T(8,128)(2,1)S(1)} %collective-permute-done.9.cur_ref.later_ref, bf16[2,4,40,256]{3,2,1,0:T(8,128)(2,1)S(1)} %collective-permute-done.7.cur_ref.later_ref, bf16[27,256,512]{2,1,0:T(8,128)(2,1)S(1)} %bitcast.176), custom_call_target="tpu_custom_call" | custom-call | flops 2264924160 | bytes 7077888 | tf_op jit(solution)/shard_map/pallas_call | solution.py:47
  102.2 2.4 %shard_map.56 = bf16[320,512]{1,0:T(8,128)(2,1)S(1)} custom-call(bf16[2,4,40,256]{3,2,1,0:T(8,128)(2,1)S(1)} %collective-permute-done.11.cur_ref, bf16[2,4,40,256]{3,2,1,0:T(8,128)(2,1)S(1)} %collective-permute-done.9.cur_ref.later_ref, bf16[27,256,512]{2,1,0:T(8,128)(2,1)S(1)} %bitcast.177), custom_call_target="tpu_custom_call" | custom-call | flops 2264924160 | bytes 7077888 | tf_op jit(solution)/shard_map/pallas_call | solution.py:47
  104.6 17.0 %all-gather.4.cloned.1.call-done.refs_2_ = bf16[4,4,4,32,256]{4,3,2,1,0:T(8,128)(2,1)} async-done(((bf16[1,4,4,32,256]{4,3,2,1,0:T(8,128)(2,1)}), bf16[4,4,4,32,256]{4,3,2,1,0:T(8,128)(2,1)}) %all-gather.4.cloned.1.call-update) | async-done | bytes 1048592 | tf_op jit(solution)/shard_map/all_gather | solution.py:252
  121.6 1.9 %collective-permute-start.15 = (bf16[4,4,32,256]{3,2,1,0:T(8,128)(2,1)}, bf16[4,4,32,256]{3,2,1,0:T(8,128)(2,1)}, u32[]{:S(2)}, u32[]{:S(2)}) collective-permute-start(bf16[4,4,32,256]{3,2,1,0:T(8,128)(2,1)} %bitcast.198), channel_id=1, source_target_pairs={{0,6},{2,0},{4,2},{6,4},{1,7},{3,1},{5,3},{7,5},{8,14},{10,8},{12,... | collective-permute-start | bytes 786440 | tf_op jit(solution)/shard_map/ppermute | solution.py:258
  125.6 20.2 %shard_map.57.refs_2_ = bf16[27,256,512]{2,1,0:T(8,128)(2,1)} custom-call(s32[1]{0:T(128)} %bitcast.67.refs_0_, bf16[4,2,1,1024,256]{4,3,2,1,0:T(8,128)(2,1)} %bitcast.202, bf16[4,4,4,32,256]{4,3,2,1,0:T(8,128)(2,1)} %all-gather.4.cloned.1.call-done.refs_2_), custom_call_target="tpu_custom_call" | custom-call | flops 14495514624 | bytes 21233664 | tf_op jit(solution)/shard_map/pallas_call | solution.py:172
  147.5 3.7 %all-to-all-start.2 = ((bf16[4,8,1,32,256]{4,3,1,2,0:T(8,128)(2,1)}), bf16[4,8,1,32,256]{4,3,1,2,0:T(8,128)(2,1)S(1)}, u32[]{:S(2)}, u32[]{:S(2)}) async-start(bf16[4,8,1,32,256]{4,3,1,2,0:T(8,128)(2,1)} %copy_bitcast_fusion), calls=%async_computation.2 | async-start | bytes 1048576 | tf_op jit(solution)/shard_map/all_to_all | solution.py:292
  151.2 18.2 %shard_map.58 = bf16[27,256,512]{2,1,0:T(8,128)(2,1)} custom-call(s32[1]{0:T(128)} %bitcast.67.refs_0_, bf16[4,2,1,1024,256]{4,3,2,1,0:T(8,128)(2,1)} %bitcast.203, bf16[27,256,512]{2,1,0:T(8,128)(2,1)} %shard_map.57.refs_2_, bf16[4,4,32,256]{3,2,1,0:T(8,128)(2,1)} %bitcast.201, bf16[4,4,32,256]{3,2,1,0:T(8,128)(2,1)} %collective-permute-done.13.refs_4_, ...), custom_call_target="tpu_custom_call" | custom-call | flops 14495514624 | bytes 21233664 | tf_op jit(solution)/shard_map/pallas_call | solution.py:172
  (99 shorter events, 18.0 us)
Async XLA Ops:
  7.2 1.4 copy-start
  9.9 16.6 %all-to-all-start = ((bf16[4,2,2,1,40,256]{5,4,2,3,1,0:T(8,128)(2,1)}), bf16[4,2,2,1,40,256]{5,4,2,3,1,0:T(8,128)(2,1)S(1)}, u32[]{:S(2)}, u32[]{:S(2)}) async-start(bf16[4,2,2,1,40,256]{5,4,2,3,1,0:T(8,128)(2,1)} %pad_maximum_fusion.2), calls=%async_computation | async-start | bytes 655360 | tf_op jit(solution)/shard_map/all_to_all | solution.py:212
  26.5 15.6 %all-to-all-start.1 = ((bf16[4,6,1,40,256]{4,3,1,2,0:T(8,128)(2,1)}), bf16[4,6,1,40,256]{4,3,1,2,0:T(8,128)(2,1)S(1)}, u32[]{:S(2)}, u32[]{:S(2)}) async-start(bf16[4,6,1,40,256]{4,3,1,2,0:T(8,128)(2,1)} %pad_maximum_fusion.1), calls=%async_computation.1 | async-start | bytes 983040 | tf_op jit(solution)/shard_map/all_to_all | solution.py:212
  30.0 63.3 %all-gather.6.cloned.1.call-start = ((), (), s32[]{:S(2)}) async-start(), calls=%async_computation.4 | async-start | bytes 4718592 | tf_op jit(solution)/shard_map/all_gather | solution.py:240
  30.1 3.0 %copy-start.1 = (bf16[1,27,256,512]{3,2,1,0:T(8,128)(2,1)S(1)}, bf16[1,27,256,512]{3,2,1,0:T(8,128)(2,1)}, u32[]{:S(2)}) copy-start(bf16[1,27,256,512]{3,2,1,0:T(8,128)(2,1)} %param.5) | copy-start | bytes 21233668
  35.6 1.5 collective-permute-start
  37.4 8.2 %collective-permute-start.1 = (bf16[2,4,40,256]{3,2,1,0:T(8,128)(2,1)S(1)}, bf16[2,4,40,256]{3,2,1,0:T(8,128)(2,1)S(1)}, u32[]{:S(2)}, u32[]{:S(2)}) collective-permute-start(bf16[2,4,40,256]{3,2,1,0:T(8,128)(2,1)S(1)} %get-tuple-element.52), channel_id=1, source_target_pairs={{0,8},{8,0},{1,9},{9,1},{2,10},{10,2},{3,11},{11,3},{4,12},{12,4},... | collective-permute-start | bytes 491528 | tf_op jit(solution)/shard_map/ppermute | solution.py:281
  45.6 76.0 %all-gather.4.cloned.1.call-start = ((), (), s32[]{:S(2)}) async-start(), calls=%async_computation.3 | async-start | bytes 1310720 | tf_op jit(solution)/shard_map/all_gather | solution.py:252
  45.8 3.0 %copy-start.2 = (bf16[1,27,256,512]{3,2,1,0:T(8,128)(2,1)S(1)}, bf16[1,27,256,512]{3,2,1,0:T(8,128)(2,1)}, u32[]{:S(2)}) copy-start(bf16[1,27,256,512]{3,2,1,0:T(8,128)(2,1)} %param.5) | copy-start | bytes 21233668
  51.3 1.5 collective-permute-start.2
  53.1 8.1 %collective-permute-start.3 = (bf16[2,4,40,256]{3,2,1,0:T(8,128)(2,1)S(1)}, bf16[2,4,40,256]{3,2,1,0:T(8,128)(2,1)S(1)}, u32[]{:S(2)}, u32[]{:S(2)}) collective-permute-start(bf16[2,4,40,256]{3,2,1,0:T(8,128)(2,1)S(1)} %get-tuple-element.50), channel_id=1, source_target_pairs={{0,8},{8,16},{16,0},{1,9},{9,17},{17,1},{2,10},{10,18},{18,2},{3,1... | collective-permute-start | bytes 491528 | tf_op jit(solution)/shard_map/ppermute | solution.py:281
  63.7 1.5 collective-permute-start.4
  65.5 7.2 %collective-permute-start.5 = (bf16[2,4,40,256]{3,2,1,0:T(8,128)(2,1)S(1)}, bf16[2,4,40,256]{3,2,1,0:T(8,128)(2,1)S(1)}, u32[]{:S(2)}, u32[]{:S(2)}) collective-permute-start(bf16[2,4,40,256]{3,2,1,0:T(8,128)(2,1)S(1)} %get-tuple-element.48), channel_id=1, source_target_pairs={{0,8},{8,16},{16,24},{24,0},{1,9},{9,17},{17,25},{25,1},{2,10},{10... | collective-permute-start | bytes 491528 | tf_op jit(solution)/shard_map/ppermute | solution.py:281
  75.1 1.5 collective-permute-start.6
  76.8 6.2 %collective-permute-start.7 = (bf16[2,4,40,256]{3,2,1,0:T(8,128)(2,1)S(1)}, bf16[2,4,40,256]{3,2,1,0:T(8,128)(2,1)S(1)}, u32[]{:S(2)}, u32[]{:S(2)}) collective-permute-start(bf16[2,4,40,256]{3,2,1,0:T(8,128)(2,1)S(1)} %fusion.39), channel_id=1, source_target_pairs={{0,8},{8,16},{16,24},{1,9},{9,17},{17,25},{2,10},{10,18},{18,26},{... | collective-permute-start | bytes 491528 | tf_op jit(solution)/shard_map/ppermute | solution.py:281
  83.1 3.4 %copy-start.6 = (bf16[5,2,4,32,256]{4,3,2,1,0:T(8,128)(2,1)}, bf16[5,2,4,32,256]{4,3,2,1,0:T(8,128)(2,1)S(1)}, u32[]{:S(2)}) copy-start(bf16[5,2,4,32,256]{4,3,2,1,0:T(8,128)(2,1)S(1)} %get-tuple-element.68) | copy-start | bytes 1966084
  86.4 1.5 collective-permute-start.8
  86.5 0.9 copy-start.4
  88.1 1.4 collective-permute-start.9
  93.3 3.0 %copy-start.3 = (bf16[1,27,256,512]{3,2,1,0:T(8,128)(2,1)S(1)}, bf16[1,27,256,512]{3,2,1,0:T(8,128)(2,1)}, u32[]{:S(2)}) copy-start(bf16[1,27,256,512]{3,2,1,0:T(8,128)(2,1)} %param.5) | copy-start | bytes 21233668
  96.4 2.8 %copy-start.7 = (bf16[5,2,4,32,256]{4,3,2,1,0:T(8,128)(2,1)S(1)}, bf16[5,2,4,32,256]{4,3,2,1,0:T(8,128)(2,1)}, u32[]{:S(2)}) copy-start(bf16[5,2,4,32,256]{4,3,2,1,0:T(8,128)(2,1)} %copy-done.6) | copy-start | bytes 1966084
  96.4 5.0 %copy-start.5 = (bf16[7,2,4,32,256]{4,3,2,1,0:T(8,128)(2,1)S(1)}, bf16[7,2,4,32,256]{4,3,2,1,0:T(8,128)(2,1)}, u32[]{:S(2)}) copy-start(bf16[7,2,4,32,256]{4,3,2,1,0:T(8,128)(2,1)} %fusion.73) | copy-start | bytes 2752516
  98.8 1.5 collective-permute-start.10
  100.6 0.7 collective-permute-start.11
  121.6 25.4 %collective-permute-start.15 = (bf16[4,4,32,256]{3,2,1,0:T(8,128)(2,1)}, bf16[4,4,32,256]{3,2,1,0:T(8,128)(2,1)}, u32[]{:S(2)}, u32[]{:S(2)}) collective-permute-start(bf16[4,4,32,256]{3,2,1,0:T(8,128)(2,1)} %bitcast.198), channel_id=1, source_target_pairs={{0,6},{2,0},{4,2},{6,4},{1,7},{3,1},{5,3},{7,5},{8,14},{10,8},{12,... | collective-permute-start | bytes 786440 | tf_op jit(solution)/shard_map/ppermute | solution.py:258
  123.5 24.0 %collective-permute-start.14 = (bf16[4,4,32,256]{3,2,1,0:T(8,128)(2,1)}, bf16[4,4,32,256]{3,2,1,0:T(8,128)(2,1)}, u32[]{:S(2)}, u32[]{:S(2)}) collective-permute-start(bf16[4,4,32,256]{3,2,1,0:T(8,128)(2,1)} %bitcast.199), channel_id=1, source_target_pairs={{0,4},{2,6},{4,0},{6,2},{1,5},{3,7},{5,1},{7,3},{8,12},{10,14},{12... | collective-permute-start | bytes 786440 | tf_op jit(solution)/shard_map/ppermute | solution.py:258
  124.5 23.0 %collective-permute-start.13 = (bf16[4,4,32,256]{3,2,1,0:T(8,128)(2,1)}, bf16[4,4,32,256]{3,2,1,0:T(8,128)(2,1)}, u32[]{:S(2)}, u32[]{:S(2)}) collective-permute-start(bf16[4,4,32,256]{3,2,1,0:T(8,128)(2,1)} %bitcast.200), channel_id=1, source_target_pairs={{0,2},{2,4},{4,6},{6,0},{1,3},{3,5},{5,7},{7,1},{8,10},{10,12},{12... | collective-permute-start | bytes 786440 | tf_op jit(solution)/shard_map/ppermute | solution.py:258
  125.5 20.3 %collective-permute-start.12 = (bf16[320,256]{1,0:T(8,128)(2,1)S(1)}, bf16[320,256]{1,0:T(8,128)(2,1)S(1)}, u32[]{:S(2)}, u32[]{:S(2)}) collective-permute-start(bf16[320,256]{1,0:T(8,128)(2,1)S(1)} %constant_dynamic-slice_fusion.1), channel_id=1, source_target_pairs={{0,1},{1,0},{2,3},{3,2},{4,5},{5,4},{6,7},{7,6},{8,9},{9,8},{10,11... | collective-permute-start | bytes 491528 | tf_op jit(solution)/shard_map/ppermute | solution.py:265
  147.5 21.9 %all-to-all-start.2 = ((bf16[4,8,1,32,256]{4,3,1,2,0:T(8,128)(2,1)}), bf16[4,8,1,32,256]{4,3,1,2,0:T(8,128)(2,1)S(1)}, u32[]{:S(2)}, u32[]{:S(2)}) async-start(bf16[4,8,1,32,256]{4,3,1,2,0:T(8,128)(2,1)} %copy_bitcast_fusion), calls=%async_computation.2 | async-start | bytes 1048576 | tf_op jit(solution)/shard_map/all_to_all | solution.py:292
Sparse Core Ops, SparseCore 0:
  45.7 47.5 all-gather.5
  94.9 26.6 all-gather.3

commit v5 on v3

--- a/solution.py
+++ b/solution.py
@@ -89,8 +89,8 @@
                         f_here.at[ring * chans + chan],
                     )
                 )
-        for copy in g_copies + f_copies:
-            copy.start()
+        for index, copy in enumerate(g_copies + f_copies):
+            copy.start(priority=index % 2)
         same = lax.broadcasted_iota(jnp.int32, (group, group), 0) == lax.broadcasted_iota(jnp.int32, (group, group), 1)
         identity = jnp.where(same, 1.0, 0.0).astype(BF16)
         source = lax.broadcasted_iota(jnp.int32, (width_n, 2 * width_n), 0)
@@ -124,7 +124,7 @@
     offset = 2 - step % 3
     for lag in range(3):
 
-        @pl.when(step // 3 == lag)
+        @pl.when(step // 3 == (2 - lag if has_sum else lag))
         def _():
             skipped = max(0, lag - first)
             span = (frames_n - skipped) * width_n
@@ -165,8 +165,10 @@
     f_first = max(0, first - 2)
     held_n = first + frames_n - f_first
     far = pl.BlockSpec(memory_space=pltpu.HBM)
-    out_spec = pl.BlockSpec((3, group, channels), lambda step: (step, 0, 0))
     has_sum = known is not None
+    out_spec = pl.BlockSpec(
+        (3, group, channels), lambda step: ((2 - step // 3) * 3 + step % 3 if has_sum else step, 0, 0)
+    )
     return pl.pallas_call(
         functools.partial(tap_kernel, first, f_first, has_sum),
         grid=(9,),

time: 179 us -> 179 us (level)
  no operation moved by 1% of the time
where the time goes in v5:
time: 179 us
  Pallas kernels  56.7 us (32%)
  waiting for transfers between devices  54.4 us (30%)
  starting transfers between devices  31 us (17%)
  local copies, waits for them, and re-layouts  17.1 us (10%)
  between operations  14.6 us (8%)
  other arithmetic  4.68 us (3%)
    pallas_call x2, Pallas kernels, kernel_gradient(): pl.pallas_call(functools.partial(tap_kernel, first, f_first, has_sum), gr...  39.6 us
    ppermute x6, waiting for transfers between devices, body(): current = lax.ppermute(updated, 'section', pairs)  17.1 us
    pallas_call x7, Pallas kernels, back_block(): pl.pallas_call(back_kernel, in_specs=[held, held, held], out_specs=held,...  17.1 us
    all_gather x1, waiting for transfers between devices, body(): gathered.append([lax.all_gather(taken, 'frame')])  17 us
    ppermute x6, starting transfers between devices, body(): current = lax.ppermute(updated, 'section', pairs)  12.4 us
    unnamed x29, local copies, waits for them, and re-layouts  12.1 us
    all_to_all x2, waiting for transfers between devices, to_columns(): pieces = lax.all_to_all(pieces, 'frame', 0, 0)  10.6 us
    all_to_all x2, starting transfers between devices, to_columns(): pieces = lax.all_to_all(pieces, 'frame', 0, 0)  9.79 us
  transfers between devices with their start and end apart: 21, of which 14 were waited for; matrix products, arithmetic and copies ran while one was open for 5% of the time, Pallas kernels for 32%

profile of v5, /device:TPU:0, one launch (start us, length us, event | category | flops | bytes accessed | tf_op | source)
XLA Modules:
  0.0 178.5 jit_solution(6311500562951709183)
XLA Ops:
  7.2 1.3 constant_dynamic-slice_fusion.11
  9.9 6.3 %all-to-all-start = ((bf16[4,2,2,1,40,256]{5,4,2,3,1,0:T(8,128)(2,1)}), bf16[4,2,2,1,40,256]{5,4,2,3,1,0:T(8,128)(2,1)S(1)}, u32[]{:S(2)}, u32[]{:S(2)}) async-start(bf16[4,2,2,1,40,256]{5,4,2,3,1,0:T(8,128)(2,1)} %pad_maximum_fusion.2), calls=%async_computation | async-start | bytes 655360 | tf_op jit(solution)/shard_map/all_to_all | solution.py:212
  17.3 9.2 %all-to-all-done = bf16[4,2,2,1,40,256]{5,4,2,3,1,0:T(8,128)(2,1)S(1)} async-done(((bf16[4,2,2,1,40,256]{5,4,2,3,1,0:T(8,128)(2,1)}), bf16[4,2,2,1,40,256]{5,4,2,3,1,0:T(8,128)(2,1)S(1)}, u32[]{:S(2)}, u32[]{:S(2)}) %all-to-all-start) | async-done | bytes 327712 | tf_op jit(solution)/shard_map/all_to_all | solution.py:212
  26.5 3.5 %all-to-all-start.1 = ((bf16[4,6,1,40,256]{4,3,1,2,0:T(8,128)(2,1)}), bf16[4,6,1,40,256]{4,3,1,2,0:T(8,128)(2,1)S(1)}, u32[]{:S(2)}, u32[]{:S(2)}) async-start(bf16[4,6,1,40,256]{4,3,1,2,0:T(8,128)(2,1)} %pad_maximum_fusion.1), calls=%async_computation.1 | async-start | bytes 983040 | tf_op jit(solution)/shard_map/all_to_all | solution.py:212
  30.1 3.0 %copy-done.1 = bf16[1,27,256,512]{3,2,1,0:T(8,128)(2,1)S(1)} copy-done((bf16[1,27,256,512]{3,2,1,0:T(8,128)(2,1)S(1)}, bf16[1,27,256,512]{3,2,1,0:T(8,128)(2,1)}, u32[]{:S(2)}) %copy-start.1) | copy-done | bytes 7077912
  33.1 2.4 %shard_map.50 = bf16[320,512]{1,0:T(8,128)(2,1)S(1)} custom-call(bf16[2,4,40,256]{3,2,1,0:T(8,128)(2,1)S(1)} %broadcast_select_fusion.3.cur_ref.later_ref, bf16[2,4,40,256]{3,2,1,0:T(8,128)(2,1)S(1)} %broadcast_in_dim.44.later_ref, bf16[27,256,512]{2,1,0:T(8,128)(2,1)S(1)} %bitcast.171), custom_call_target="tpu_custom_call" | custom-call | flops 2264924160 | bytes 7077888 | tf_op jit(solution)/shard_map/pallas_call | solution.py:47
  37.4 3.4 %collective-permute-start.1 = (bf16[2,4,40,256]{3,2,1,0:T(8,128)(2,1)S(1)}, bf16[2,4,40,256]{3,2,1,0:T(8,128)(2,1)S(1)}, u32[]{:S(2)}, u32[]{:S(2)}) collective-permute-start(bf16[2,4,40,256]{3,2,1,0:T(8,128)(2,1)S(1)} %get-tuple-element.52), channel_id=1, source_target_pairs={{0,8},{8,0},{1,9},{9,1},{2,10},{10,2},{3,11},{11,3},{4,12},{12,4},... | collective-permute-start | bytes 491528 | tf_op jit(solution)/shard_map/ppermute | solution.py:281
  40.8 1.3 all-to-all-done.1
  42.2 3.4 %collective-permute-done.1.cur_ref.later_ref = bf16[2,4,40,256]{3,2,1,0:T(8,128)(2,1)S(1)} collective-permute-done((bf16[2,4,40,256]{3,2,1,0:T(8,128)(2,1)S(1)}, bf16[2,4,40,256]{3,2,1,0:T(8,128)(2,1)S(1)}, u32[]{:S(2)}, u32[]{:S(2)}) %collective-permute-start.1) | collective-permute-done | bytes 163872 | tf_op jit(solution)/shard_map/ppermute | solution.py:281
  45.8 3.0 %copy-done.2 = bf16[1,27,256,512]{3,2,1,0:T(8,128)(2,1)S(1)} copy-done((bf16[1,27,256,512]{3,2,1,0:T(8,128)(2,1)S(1)}, bf16[1,27,256,512]{3,2,1,0:T(8,128)(2,1)}, u32[]{:S(2)}) %copy-start.2) | copy-done | bytes 7077912
  48.8 2.4 %shard_map.51 = bf16[320,512]{1,0:T(8,128)(2,1)S(1)} custom-call(bf16[2,4,40,256]{3,2,1,0:T(8,128)(2,1)S(1)} %collective-permute-done.1.cur_ref.later_ref, bf16[2,4,40,256]{3,2,1,0:T(8,128)(2,1)S(1)} %broadcast_select_fusion.3.cur_ref.later_ref, bf16[27,256,512]{2,1,0:T(8,128)(2,1)S(1)} %bitcast.172), custom_call_target="tpu_custom_call" | custom-call | flops 2264924160 | bytes 7077888 | tf_op jit(solution)/shard_map/pallas_call | solution.py:47
  51.4 1.3 collective-permute-done.2
  53.1 3.4 %collective-permute-start.3 = (bf16[2,4,40,256]{3,2,1,0:T(8,128)(2,1)S(1)}, bf16[2,4,40,256]{3,2,1,0:T(8,128)(2,1)S(1)}, u32[]{:S(2)}, u32[]{:S(2)}) collective-permute-start(bf16[2,4,40,256]{3,2,1,0:T(8,128)(2,1)S(1)} %get-tuple-element.50), channel_id=1, source_target_pairs={{0,8},{8,16},{16,0},{1,9},{9,17},{17,1},{2,10},{10,18},{18,2},{3,1... | collective-permute-start | bytes 491528 | tf_op jit(solution)/shard_map/ppermute | solution.py:281
  56.6 4.6 %collective-permute-done.3.cur_ref.later_ref = bf16[2,4,40,256]{3,2,1,0:T(8,128)(2,1)S(1)} collective-permute-done((bf16[2,4,40,256]{3,2,1,0:T(8,128)(2,1)S(1)}, bf16[2,4,40,256]{3,2,1,0:T(8,128)(2,1)S(1)}, u32[]{:S(2)}, u32[]{:S(2)}) %collective-permute-start.3) | collective-permute-done | bytes 163872 | tf_op jit(solution)/shard_map/ppermute | solution.py:281
  61.2 2.4 %shard_map.52 = bf16[320,512]{1,0:T(8,128)(2,1)S(1)} custom-call(bf16[2,4,40,256]{3,2,1,0:T(8,128)(2,1)S(1)} %collective-permute-done.3.cur_ref.later_ref, bf16[2,4,40,256]{3,2,1,0:T(8,128)(2,1)S(1)} %collective-permute-done.1.cur_ref.later_ref, bf16[27,256,512]{2,1,0:T(8,128)(2,1)S(1)} %bitcast.173), custom_call_target="tpu_custom_call" | custom-call | flops 2264924160 | bytes 7077888 | tf_op jit(solution)/shard_map/pallas_call | solution.py:47
  63.8 1.3 collective-permute-done.4
  65.5 1.5 collective-permute-start.5
  67.1 5.6 %collective-permute-done.5.cur_ref.later_ref = bf16[2,4,40,256]{3,2,1,0:T(8,128)(2,1)S(1)} collective-permute-done((bf16[2,4,40,256]{3,2,1,0:T(8,128)(2,1)S(1)}, bf16[2,4,40,256]{3,2,1,0:T(8,128)(2,1)S(1)}, u32[]{:S(2)}, u32[]{:S(2)}) %collective-permute-start.5) | collective-permute-done | bytes 163872 | tf_op jit(solution)/shard_map/ppermute | solution.py:281
  72.7 2.4 %shard_map.53 = bf16[320,512]{1,0:T(8,128)(2,1)S(1)} custom-call(bf16[2,4,40,256]{3,2,1,0:T(8,128)(2,1)S(1)} %collective-permute-done.5.cur_ref.later_ref, bf16[2,4,40,256]{3,2,1,0:T(8,128)(2,1)S(1)} %collective-permute-done.3.cur_ref.later_ref, bf16[27,256,512]{2,1,0:T(8,128)(2,1)S(1)} %bitcast.174), custom_call_target="tpu_custom_call" | custom-call | flops 2264924160 | bytes 7077888 | tf_op jit(solution)/shard_map/pallas_call | solution.py:47
  75.3 1.3 collective-permute-done.6
  76.8 2.7 %collective-permute-start.7 = (bf16[2,4,40,256]{3,2,1,0:T(8,128)(2,1)S(1)}, bf16[2,4,40,256]{3,2,1,0:T(8,128)(2,1)S(1)}, u32[]{:S(2)}, u32[]{:S(2)}) collective-permute-start(bf16[2,4,40,256]{3,2,1,0:T(8,128)(2,1)S(1)} %fusion.39), channel_id=1, source_target_pairs={{0,8},{8,16},{16,24},{1,9},{9,17},{17,25},{2,10},{10,18},{18,26},{... | collective-permute-start | bytes 491528 | tf_op jit(solution)/shard_map/ppermute | solution.py:281
  79.6 3.5 %collective-permute-done.7.cur_ref.later_ref = bf16[2,4,40,256]{3,2,1,0:T(8,128)(2,1)S(1)} collective-permute-done((bf16[2,4,40,256]{3,2,1,0:T(8,128)(2,1)S(1)}, bf16[2,4,40,256]{3,2,1,0:T(8,128)(2,1)S(1)}, u32[]{:S(2)}, u32[]{:S(2)}) %collective-permute-start.7) | collective-permute-done | bytes 163872 | tf_op jit(solution)/shard_map/ppermute | solution.py:281
  83.9 2.4 %shard_map.54 = bf16[320,512]{1,0:T(8,128)(2,1)S(1)} custom-call(bf16[2,4,40,256]{3,2,1,0:T(8,128)(2,1)S(1)} %collective-permute-done.7.cur_ref.later_ref, bf16[2,4,40,256]{3,2,1,0:T(8,128)(2,1)S(1)} %collective-permute-done.5.cur_ref.later_ref, bf16[27,256,512]{2,1,0:T(8,128)(2,1)S(1)} %bitcast.175), custom_call_target="tpu_custom_call" | custom-call | flops 2264924160 | bytes 7077888 | tf_op jit(solution)/shard_map/pallas_call | solution.py:47
  89.5 3.9 %all-gather.6.cloned.1.call-done = bf16[8,1024,256]{2,1,0:T(8,128)(2,1)} async-done(((bf16[1,1024,256]{2,1,0:T(8,128)(2,1)}), bf16[8,1024,256]{2,1,0:T(8,128)(2,1)}) %all-gather.6.cloned.1.call-update) | async-done | bytes 4194320 | tf_op jit(solution)/shard_map/all_gather | solution.py:240
  93.3 3.0 %copy-done.3 = bf16[1,27,256,512]{3,2,1,0:T(8,128)(2,1)S(1)} copy-done((bf16[1,27,256,512]{3,2,1,0:T(8,128)(2,1)S(1)}, bf16[1,27,256,512]{3,2,1,0:T(8,128)(2,1)}, u32[]{:S(2)}) %copy-start.3) | copy-done | bytes 7077912
  96.4 2.5 %shard_map.55 = bf16[320,512]{1,0:T(8,128)(2,1)S(1)} custom-call(bf16[2,4,40,256]{3,2,1,0:T(8,128)(2,1)S(1)} %collective-permute-done.9.cur_ref.later_ref, bf16[2,4,40,256]{3,2,1,0:T(8,128)(2,1)S(1)} %collective-permute-done.7.cur_ref.later_ref, bf16[27,256,512]{2,1,0:T(8,128)(2,1)S(1)} %bitcast.176), custom_call_target="tpu_custom_call" | custom-call | flops 2264924160 | bytes 7077888 | tf_op jit(solution)/shard_map/pallas_call | solution.py:47
  102.2 2.4 %shard_map.56 = bf16[320,512]{1,0:T(8,128)(2,1)S(1)} custom-call(bf16[2,4,40,256]{3,2,1,0:T(8,128)(2,1)S(1)} %collective-permute-done.11.cur_ref, bf16[2,4,40,256]{3,2,1,0:T(8,128)(2,1)S(1)} %collective-permute-done.9.cur_ref.later_ref, bf16[27,256,512]{2,1,0:T(8,128)(2,1)S(1)} %bitcast.177), custom_call_target="tpu_custom_call" | custom-call | flops 2264924160 | bytes 7077888 | tf_op jit(solution)/shard_map/pallas_call | solution.py:47
  104.6 17.0 %all-gather.4.cloned.1.call-done.refs_2_ = bf16[4,4,4,32,256]{4,3,2,1,0:T(8,128)(2,1)} async-done(((bf16[1,4,4,32,256]{4,3,2,1,0:T(8,128)(2,1)}), bf16[4,4,4,32,256]{4,3,2,1,0:T(8,128)(2,1)}) %all-gather.4.cloned.1.call-update) | async-done | bytes 1048592 | tf_op jit(solution)/shard_map/all_gather | solution.py:252
  121.6 1.9 %collective-permute-start.15 = (bf16[4,4,32,256]{3,2,1,0:T(8,128)(2,1)}, bf16[4,4,32,256]{3,2,1,0:T(8,128)(2,1)}, u32[]{:S(2)}, u32[]{:S(2)}) collective-permute-start(bf16[4,4,32,256]{3,2,1,0:T(8,128)(2,1)} %bitcast.198), channel_id=1, source_target_pairs={{0,6},{2,0},{4,2},{6,4},{1,7},{3,1},{5,3},{7,5},{8,14},{10,8},{12,... | collective-permute-start | bytes 786440 | tf_op jit(solution)/shard_map/ppermute | solution.py:258
  125.6 20.9 %shard_map.57.refs_2_ = bf16[27,256,512]{2,1,0:T(8,128)(2,1)} custom-call(s32[1]{0:T(128)} %bitcast.67.refs_0_, bf16[4,2,1,1024,256]{4,3,2,1,0:T(8,128)(2,1)} %bitcast.202, bf16[4,4,4,32,256]{4,3,2,1,0:T(8,128)(2,1)} %all-gather.4.cloned.1.call-done.refs_2_), custom_call_target="tpu_custom_call" | custom-call | flops 14495514624 | bytes 21233664 | tf_op jit(solution)/shard_map/pallas_call | solution.py:172
  147.7 4.1 %all-to-all-start.2 = ((bf16[4,8,1,32,256]{4,3,1,2,0:T(8,128)(2,1)}), bf16[4,8,1,32,256]{4,3,1,2,0:T(8,128)(2,1)S(1)}, u32[]{:S(2)}, u32[]{:S(2)}) async-start(bf16[4,8,1,32,256]{4,3,1,2,0:T(8,128)(2,1)} %copy_bitcast_fusion), calls=%async_computation.2 | async-start | bytes 1048576 | tf_op jit(solution)/shard_map/all_to_all | solution.py:292
  151.8 18.7 %shard_map.58 = bf16[27,256,512]{2,1,0:T(8,128)(2,1)} custom-call(s32[1]{0:T(128)} %bitcast.67.refs_0_, bf16[4,2,1,1024,256]{4,3,2,1,0:T(8,128)(2,1)} %bitcast.203, bf16[27,256,512]{2,1,0:T(8,128)(2,1)} %shard_map.57.refs_2_, bf16[4,4,32,256]{3,2,1,0:T(8,128)(2,1)} %bitcast.201, bf16[4,4,32,256]{3,2,1,0:T(8,128)(2,1)} %collective-permute-done.13.refs_4_, ...), custom_call_target="tpu_custom_call" | custom-call | flops 14495514624 | bytes 21233664 | tf_op jit(solution)/shard_map/pallas_call | solution.py:172
  (99 shorter events, 17.5 us)
Async XLA Ops:
  7.2 1.4 copy-start
  9.9 16.6 %all-to-all-start = ((bf16[4,2,2,1,40,256]{5,4,2,3,1,0:T(8,128)(2,1)}), bf16[4,2,2,1,40,256]{5,4,2,3,1,0:T(8,128)(2,1)S(1)}, u32[]{:S(2)}, u32[]{:S(2)}) async-start(bf16[4,2,2,1,40,256]{5,4,2,3,1,0:T(8,128)(2,1)} %pad_maximum_fusion.2), calls=%async_computation | async-start | bytes 655360 | tf_op jit(solution)/shard_map/all_to_all | solution.py:212
  26.5 15.6 %all-to-all-start.1 = ((bf16[4,6,1,40,256]{4,3,1,2,0:T(8,128)(2,1)}), bf16[4,6,1,40,256]{4,3,1,2,0:T(8,128)(2,1)S(1)}, u32[]{:S(2)}, u32[]{:S(2)}) async-start(bf16[4,6,1,40,256]{4,3,1,2,0:T(8,128)(2,1)} %pad_maximum_fusion.1), calls=%async_computation.1 | async-start | bytes 983040 | tf_op jit(solution)/shard_map/all_to_all | solution.py:212
  30.0 63.3 %all-gather.6.cloned.1.call-start = ((), (), s32[]{:S(2)}) async-start(), calls=%async_computation.4 | async-start | bytes 4718592 | tf_op jit(solution)/shard_map/all_gather | solution.py:240
  30.1 3.0 %copy-start.1 = (bf16[1,27,256,512]{3,2,1,0:T(8,128)(2,1)S(1)}, bf16[1,27,256,512]{3,2,1,0:T(8,128)(2,1)}, u32[]{:S(2)}) copy-start(bf16[1,27,256,512]{3,2,1,0:T(8,128)(2,1)} %param.5) | copy-start | bytes 21233668
  35.6 1.5 collective-permute-start
  37.4 8.2 %collective-permute-start.1 = (bf16[2,4,40,256]{3,2,1,0:T(8,128)(2,1)S(1)}, bf16[2,4,40,256]{3,2,1,0:T(8,128)(2,1)S(1)}, u32[]{:S(2)}, u32[]{:S(2)}) collective-permute-start(bf16[2,4,40,256]{3,2,1,0:T(8,128)(2,1)S(1)} %get-tuple-element.52), channel_id=1, source_target_pairs={{0,8},{8,0},{1,9},{9,1},{2,10},{10,2},{3,11},{11,3},{4,12},{12,4},... | collective-permute-start | bytes 491528 | tf_op jit(solution)/shard_map/ppermute | solution.py:281
  45.6 76.0 %all-gather.4.cloned.1.call-start = ((), (), s32[]{:S(2)}) async-start(), calls=%async_computation.3 | async-start | bytes 1310720 | tf_op jit(solution)/shard_map/all_gather | solution.py:252
  45.8 3.0 %copy-start.2 = (bf16[1,27,256,512]{3,2,1,0:T(8,128)(2,1)S(1)}, bf16[1,27,256,512]{3,2,1,0:T(8,128)(2,1)}, u32[]{:S(2)}) copy-start(bf16[1,27,256,512]{3,2,1,0:T(8,128)(2,1)} %param.5) | copy-start | bytes 21233668
  51.3 1.5 collective-permute-start.2
  53.1 8.1 %collective-permute-start.3 = (bf16[2,4,40,256]{3,2,1,0:T(8,128)(2,1)S(1)}, bf16[2,4,40,256]{3,2,1,0:T(8,128)(2,1)S(1)}, u32[]{:S(2)}, u32[]{:S(2)}) collective-permute-start(bf16[2,4,40,256]{3,2,1,0:T(8,128)(2,1)S(1)} %get-tuple-element.50), channel_id=1, source_target_pairs={{0,8},{8,16},{16,0},{1,9},{9,17},{17,1},{2,10},{10,18},{18,2},{3,1... | collective-permute-start | bytes 491528 | tf_op jit(solution)/shard_map/ppermute | solution.py:281
  63.7 1.5 collective-permute-start.4
  65.5 7.2 %collective-permute-start.5 = (bf16[2,4,40,256]{3,2,1,0:T(8,128)(2,1)S(1)}, bf16[2,4,40,256]{3,2,1,0:T(8,128)(2,1)S(1)}, u32[]{:S(2)}, u32[]{:S(2)}) collective-permute-start(bf16[2,4,40,256]{3,2,1,0:T(8,128)(2,1)S(1)} %get-tuple-element.48), channel_id=1, source_target_pairs={{0,8},{8,16},{16,24},{24,0},{1,9},{9,17},{17,25},{25,1},{2,10},{10... | collective-permute-start | bytes 491528 | tf_op jit(solution)/shard_map/ppermute | solution.py:281
  75.1 1.5 collective-permute-start.6
  76.8 6.2 %collective-permute-start.7 = (bf16[2,4,40,256]{3,2,1,0:T(8,128)(2,1)S(1)}, bf16[2,4,40,256]{3,2,1,0:T(8,128)(2,1)S(1)}, u32[]{:S(2)}, u32[]{:S(2)}) collective-permute-start(bf16[2,4,40,256]{3,2,1,0:T(8,128)(2,1)S(1)} %fusion.39), channel_id=1, source_target_pairs={{0,8},{8,16},{16,24},{1,9},{9,17},{17,25},{2,10},{10,18},{18,26},{... | collective-permute-start | bytes 491528 | tf_op jit(solution)/shard_map/ppermute | solution.py:281
  83.1 3.4 %copy-start.6 = (bf16[5,2,4,32,256]{4,3,2,1,0:T(8,128)(2,1)}, bf16[5,2,4,32,256]{4,3,2,1,0:T(8,128)(2,1)S(1)}, u32[]{:S(2)}) copy-start(bf16[5,2,4,32,256]{4,3,2,1,0:T(8,128)(2,1)S(1)} %get-tuple-element.68) | copy-start | bytes 1966084
  86.4 1.5 collective-permute-start.8
  86.5 0.9 copy-start.4
  88.1 1.4 collective-permute-start.9
  93.3 3.0 %copy-start.3 = (bf16[1,27,256,512]{3,2,1,0:T(8,128)(2,1)S(1)}, bf16[1,27,256,512]{3,2,1,0:T(8,128)(2,1)}, u32[]{:S(2)}) copy-start(bf16[1,27,256,512]{3,2,1,0:T(8,128)(2,1)} %param.5) | copy-start | bytes 21233668
  96.4 2.8 %copy-start.7 = (bf16[5,2,4,32,256]{4,3,2,1,0:T(8,128)(2,1)S(1)}, bf16[5,2,4,32,256]{4,3,2,1,0:T(8,128)(2,1)}, u32[]{:S(2)}) copy-start(bf16[5,2,4,32,256]{4,3,2,1,0:T(8,128)(2,1)} %copy-done.6) | copy-start | bytes 1966084
  96.4 5.0 %copy-start.5 = (bf16[7,2,4,32,256]{4,3,2,1,0:T(8,128)(2,1)S(1)}, bf16[7,2,4,32,256]{4,3,2,1,0:T(8,128)(2,1)}, u32[]{:S(2)}) copy-start(bf16[7,2,4,32,256]{4,3,2,1,0:T(8,128)(2,1)} %fusion.73) | copy-start | bytes 2752516
  98.8 1.5 collective-permute-start.10
  100.6 0.7 collective-permute-start.11
  121.6 26.1 %collective-permute-start.15 = (bf16[4,4,32,256]{3,2,1,0:T(8,128)(2,1)}, bf16[4,4,32,256]{3,2,1,0:T(8,128)(2,1)}, u32[]{:S(2)}, u32[]{:S(2)}) collective-permute-start(bf16[4,4,32,256]{3,2,1,0:T(8,128)(2,1)} %bitcast.198), channel_id=1, source_target_pairs={{0,6},{2,0},{4,2},{6,4},{1,7},{3,1},{5,3},{7,5},{8,14},{10,8},{12,... | collective-permute-start | bytes 786440 | tf_op jit(solution)/shard_map/ppermute | solution.py:258
  123.5 24.2 %collective-permute-start.14 = (bf16[4,4,32,256]{3,2,1,0:T(8,128)(2,1)}, bf16[4,4,32,256]{3,2,1,0:T(8,128)(2,1)}, u32[]{:S(2)}, u32[]{:S(2)}) collective-permute-start(bf16[4,4,32,256]{3,2,1,0:T(8,128)(2,1)} %bitcast.199), channel_id=1, source_target_pairs={{0,4},{2,6},{4,0},{6,2},{1,5},{3,7},{5,1},{7,3},{8,12},{10,14},{12... | collective-permute-start | bytes 786440 | tf_op jit(solution)/shard_map/ppermute | solution.py:258
  124.5 23.2 %collective-permute-start.13 = (bf16[4,4,32,256]{3,2,1,0:T(8,128)(2,1)}, bf16[4,4,32,256]{3,2,1,0:T(8,128)(2,1)}, u32[]{:S(2)}, u32[]{:S(2)}) collective-permute-start(bf16[4,4,32,256]{3,2,1,0:T(8,128)(2,1)} %bitcast.200), channel_id=1, source_target_pairs={{0,2},{2,4},{4,6},{6,0},{1,3},{3,5},{5,7},{7,1},{8,10},{10,12},{12... | collective-permute-start | bytes 786440 | tf_op jit(solution)/shard_map/ppermute | solution.py:258
  125.5 21.0 %collective-permute-start.12 = (bf16[320,256]{1,0:T(8,128)(2,1)S(1)}, bf16[320,256]{1,0:T(8,128)(2,1)S(1)}, u32[]{:S(2)}, u32[]{:S(2)}) collective-permute-start(bf16[320,256]{1,0:T(8,128)(2,1)S(1)} %constant_dynamic-slice_fusion.1), channel_id=1, source_target_pairs={{0,1},{1,0},{2,3},{3,2},{4,5},{5,4},{6,7},{7,6},{8,9},{9,8},{10,11... | collective-permute-start | bytes 491528 | tf_op jit(solution)/shard_map/ppermute | solution.py:265
  147.7 22.8 %all-to-all-start.2 = ((bf16[4,8,1,32,256]{4,3,1,2,0:T(8,128)(2,1)}), bf16[4,8,1,32,256]{4,3,1,2,0:T(8,128)(2,1)S(1)}, u32[]{:S(2)}, u32[]{:S(2)}) async-start(bf16[4,8,1,32,256]{4,3,1,2,0:T(8,128)(2,1)} %copy_bitcast_fusion), calls=%async_computation.2 | async-start | bytes 1048576 | tf_op jit(solution)/shard_map/all_to_all | solution.py:292
Sparse Core Ops, SparseCore 0:
  45.7 47.5 all-gather.5
  94.9 26.6 all-gather.3

commit v6 on v5

--- a/solution.py
+++ b/solution.py
@@ -71,26 +71,40 @@
     width_n = pieces_n * own
     held_n = feature_ref.shape[2] // width_n
 
+    lags = (2, 1, 0) if has_sum else (0, 1, 2)
+
+    def feature_copies(phase):
+        needed = []
+        for lag in lags[: phase + 1]:
+            skipped = max(0, lag - first)
+            low = first + skipped - lag - f_first
+            needed.append(set(range(low, low + frames_n - skipped)))
+        fresh = sorted(needed[-1].difference(*needed[:-1]))
+        begin, cells = fresh[0] * width_n, len(fresh) * width_n
+        return [
+            pltpu.make_async_copy(
+                parts_ref.at[ring, chan, :, pl.ds(f_first * width_n + begin, cells)],
+                feature_ref.at[chan, pl.ds(ring * rows_l, rows_l), pl.ds(begin, cells)],
+                f_here.at[(phase * rings + ring) * chans + chan],
+            )
+            for ring in range(rings)
+            for chan in range(chans)
+        ]
+
     @pl.when(step == 0)
     def _():
-        g_copies, f_copies = [], []
+        g_copies = []
         for piece in range(pieces_n):
             if len(grad_refs) == 1:
                 source, target = grad_refs[0].at[piece], cells_ref.at[piece]
             else:
                 source, target = grad_refs[piece], cells_ref.at[lax.rem(ring_ref[0] + pieces_n - piece, pieces_n)]
             g_copies.append(pltpu.make_async_copy(source, target, g_here.at[piece]))
-        for ring in range(rings):
-            for chan in range(chans):
-                f_copies.append(
-                    pltpu.make_async_copy(
-                        parts_ref.at[ring, chan, :, pl.ds(f_first * width_n, held_n * width_n)],
-                        feature_ref.at[chan, pl.ds(ring * rows_l, rows_l)],
-                        f_here.at[ring * chans + chan],
-                    )
-                )
-        for index, copy in enumerate(g_copies + f_copies):
-            copy.start(priority=index % 2)
+        for copy in g_copies:
+            copy.start()
+        for phase in range(3):
+            for copy in feature_copies(phase):
+                copy.start(priority=1)
         same = lax.broadcasted_iota(jnp.int32, (group, group), 0) == lax.broadcasted_iota(jnp.int32, (group, group), 1)
         identity = jnp.where(same, 1.0, 0.0).astype(BF16)
         source = lax.broadcasted_iota(jnp.int32, (width_n, 2 * width_n), 0)
@@ -118,13 +132,18 @@
                 sides[0:group, start : start + width_n] = both[:, :width_n]
                 sides[group : 2 * group, start : start + width_n] = cells
                 sides[2 * group : 3 * group, start : start + width_n] = both[:, width_n:]
-        for copy in f_copies:
-            copy.wait()
+
+    for phase in range(3):
+
+        @pl.when(step == 3 * phase)
+        def _():
+            for copy in feature_copies(phase):
+                copy.wait()
 
     offset = 2 - step % 3
     for lag in range(3):
 
-        @pl.when(step // 3 == (2 - lag if has_sum else lag))
+        @pl.when(step // 3 == lags.index(lag))
         def _():
             skipped = max(0, lag - first)
             span = (frames_n - skipped) * width_n
@@ -181,7 +200,7 @@
             pltpu.VMEM((chans, rows_n, held_n * width_n, width_c), BF16),
             pltpu.VMEM((3 * group, width_c), F32),
             pltpu.SemaphoreType.DMA((pieces_n,)),
-            pltpu.SemaphoreType.DMA((rings * chans,)),
+            pltpu.SemaphoreType.DMA((3 * rings * chans,)),
         ],
         compiler_params=pltpu.CompilerParams(vmem_limit_bytes=58 * 2**20),
         cost_estimate=pl.CostEstimate(

time: 179 us -> 179 us (level)
  transfers between devices with their start and end apart: 21 -> 21, of which waited for: 14 -> 15; matrix products, arithmetic and copies ran while one was open for 5% -> 5% of each run, Pallas kernels for 32% -> 32%
where the time goes in v6:
time: 179 us; the launch traced here: 178 us
  Pallas kernels  56.3 us (31%)
  waiting for transfers between devices  54.5 us (30%)
  starting transfers between devices  30.9 us (17%)
  local copies, waits for them, and re-layouts  17.1 us (10%)
  between operations  14.6 us (8%)
  other arithmetic  4.68 us (3%)
    pallas_call x2, Pallas kernels, kernel_gradient(): pl.pallas_call(functools.partial(tap_kernel, first, f_first, has_sum), gr...  39.1 us
    ppermute x6, waiting for transfers between devices, body(): current = lax.ppermute(updated, 'section', pairs)  17.1 us
    pallas_call x7, Pallas kernels, back_block(): pl.pallas_call(back_kernel, in_specs=[held, held, held], out_specs=held,...  17.1 us
    all_gather x1, waiting for transfers between devices, body(): gathered.append([lax.all_gather(taken, 'frame')])  17 us
    ppermute x6, starting transfers between devices, body(): current = lax.ppermute(updated, 'section', pairs)  12.4 us
    unnamed x29, local copies, waits for them, and re-layouts  12.1 us
    all_to_all x2, waiting for transfers between devices, to_columns(): pieces = lax.all_to_all(pieces, 'frame', 0, 0)  10.6 us
    all_to_all x2, starting transfers between devices, to_columns(): pieces = lax.all_to_all(pieces, 'frame', 0, 0)  9.79 us
  transfers between devices with their start and end apart: 21, of which 15 were waited for; matrix products, arithmetic and copies ran while one was open for 5% of the time, Pallas kernels for 32%

profile of v6, /device:TPU:0, one launch (start us, length us, event | category | flops | bytes accessed | tf_op | source)
XLA Modules:
  0.0 178.0 jit_solution(6549966238392999043)
XLA Ops:
  7.2 1.3 constant_dynamic-slice_fusion.11
  9.9 6.3 %all-to-all-start = ((bf16[4,2,2,1,40,256]{5,4,2,3,1,0:T(8,128)(2,1)}), bf16[4,2,2,1,40,256]{5,4,2,3,1,0:T(8,128)(2,1)S(1)}, u32[]{:S(2)}, u32[]{:S(2)}) async-start(bf16[4,2,2,1,40,256]{5,4,2,3,1,0:T(8,128)(2,1)} %pad_maximum_fusion.2), calls=%async_computation | async-start | bytes 655360 | tf_op jit(solution)/shard_map/all_to_all | solution.py:231
  17.3 9.2 %all-to-all-done = bf16[4,2,2,1,40,256]{5,4,2,3,1,0:T(8,128)(2,1)S(1)} async-done(((bf16[4,2,2,1,40,256]{5,4,2,3,1,0:T(8,128)(2,1)}), bf16[4,2,2,1,40,256]{5,4,2,3,1,0:T(8,128)(2,1)S(1)}, u32[]{:S(2)}, u32[]{:S(2)}) %all-to-all-start) | async-done | bytes 327712 | tf_op jit(solution)/shard_map/all_to_all | solution.py:231
  26.5 3.5 %all-to-all-start.1 = ((bf16[4,6,1,40,256]{4,3,1,2,0:T(8,128)(2,1)}), bf16[4,6,1,40,256]{4,3,1,2,0:T(8,128)(2,1)S(1)}, u32[]{:S(2)}, u32[]{:S(2)}) async-start(bf16[4,6,1,40,256]{4,3,1,2,0:T(8,128)(2,1)} %pad_maximum_fusion.1), calls=%async_computation.1 | async-start | bytes 983040 | tf_op jit(solution)/shard_map/all_to_all | solution.py:231
  30.1 3.0 %copy-done.1 = bf16[1,27,256,512]{3,2,1,0:T(8,128)(2,1)S(1)} copy-done((bf16[1,27,256,512]{3,2,1,0:T(8,128)(2,1)S(1)}, bf16[1,27,256,512]{3,2,1,0:T(8,128)(2,1)}, u32[]{:S(2)}) %copy-start.1) | copy-done | bytes 7077912
  33.1 2.4 %shard_map.50 = bf16[320,512]{1,0:T(8,128)(2,1)S(1)} custom-call(bf16[2,4,40,256]{3,2,1,0:T(8,128)(2,1)S(1)} %broadcast_select_fusion.3.cur_ref.later_ref, bf16[2,4,40,256]{3,2,1,0:T(8,128)(2,1)S(1)} %broadcast_in_dim.44.later_ref, bf16[27,256,512]{2,1,0:T(8,128)(2,1)S(1)} %bitcast.171), custom_call_target="tpu_custom_call" | custom-call | flops 2264924160 | bytes 7077888 | tf_op jit(solution)/shard_map/pallas_call | solution.py:47
  37.4 3.4 %collective-permute-start.1 = (bf16[2,4,40,256]{3,2,1,0:T(8,128)(2,1)S(1)}, bf16[2,4,40,256]{3,2,1,0:T(8,128)(2,1)S(1)}, u32[]{:S(2)}, u32[]{:S(2)}) collective-permute-start(bf16[2,4,40,256]{3,2,1,0:T(8,128)(2,1)S(1)} %get-tuple-element.52), channel_id=1, source_target_pairs={{0,8},{8,0},{1,9},{9,1},{2,10},{10,2},{3,11},{11,3},{4,12},{12,4},... | collective-permute-start | bytes 491528 | tf_op jit(solution)/shard_map/ppermute | solution.py:300
  40.8 1.3 all-to-all-done.1
  42.2 3.4 %collective-permute-done.1.cur_ref.later_ref = bf16[2,4,40,256]{3,2,1,0:T(8,128)(2,1)S(1)} collective-permute-done((bf16[2,4,40,256]{3,2,1,0:T(8,128)(2,1)S(1)}, bf16[2,4,40,256]{3,2,1,0:T(8,128)(2,1)S(1)}, u32[]{:S(2)}, u32[]{:S(2)}) %collective-permute-start.1) | collective-permute-done | bytes 163872 | tf_op jit(solution)/shard_map/ppermute | solution.py:300
  45.8 3.0 %copy-done.2 = bf16[1,27,256,512]{3,2,1,0:T(8,128)(2,1)S(1)} copy-done((bf16[1,27,256,512]{3,2,1,0:T(8,128)(2,1)S(1)}, bf16[1,27,256,512]{3,2,1,0:T(8,128)(2,1)}, u32[]{:S(2)}) %copy-start.2) | copy-done | bytes 7077912
  48.8 2.4 %shard_map.51 = bf16[320,512]{1,0:T(8,128)(2,1)S(1)} custom-call(bf16[2,4,40,256]{3,2,1,0:T(8,128)(2,1)S(1)} %collective-permute-done.1.cur_ref.later_ref, bf16[2,4,40,256]{3,2,1,0:T(8,128)(2,1)S(1)} %broadcast_select_fusion.3.cur_ref.later_ref, bf16[27,256,512]{2,1,0:T(8,128)(2,1)S(1)} %bitcast.172), custom_call_target="tpu_custom_call" | custom-call | flops 2264924160 | bytes 7077888 | tf_op jit(solution)/shard_map/pallas_call | solution.py:47
  51.4 1.3 collective-permute-done.2
  53.1 3.4 %collective-permute-start.3 = (bf16[2,4,40,256]{3,2,1,0:T(8,128)(2,1)S(1)}, bf16[2,4,40,256]{3,2,1,0:T(8,128)(2,1)S(1)}, u32[]{:S(2)}, u32[]{:S(2)}) collective-permute-start(bf16[2,4,40,256]{3,2,1,0:T(8,128)(2,1)S(1)} %get-tuple-element.50), channel_id=1, source_target_pairs={{0,8},{8,16},{16,0},{1,9},{9,17},{17,1},{2,10},{10,18},{18,2},{3,1... | collective-permute-start | bytes 491528 | tf_op jit(solution)/shard_map/ppermute | solution.py:300
  56.6 4.6 %collective-permute-done.3.cur_ref.later_ref = bf16[2,4,40,256]{3,2,1,0:T(8,128)(2,1)S(1)} collective-permute-done((bf16[2,4,40,256]{3,2,1,0:T(8,128)(2,1)S(1)}, bf16[2,4,40,256]{3,2,1,0:T(8,128)(2,1)S(1)}, u32[]{:S(2)}, u32[]{:S(2)}) %collective-permute-start.3) | collective-permute-done | bytes 163872 | tf_op jit(solution)/shard_map/ppermute | solution.py:300
  61.2 2.4 %shard_map.52 = bf16[320,512]{1,0:T(8,128)(2,1)S(1)} custom-call(bf16[2,4,40,256]{3,2,1,0:T(8,128)(2,1)S(1)} %collective-permute-done.3.cur_ref.later_ref, bf16[2,4,40,256]{3,2,1,0:T(8,128)(2,1)S(1)} %collective-permute-done.1.cur_ref.later_ref, bf16[27,256,512]{2,1,0:T(8,128)(2,1)S(1)} %bitcast.173), custom_call_target="tpu_custom_call" | custom-call | flops 2264924160 | bytes 7077888 | tf_op jit(solution)/shard_map/pallas_call | solution.py:47
  63.8 1.3 collective-permute-done.4
  65.5 1.5 collective-permute-start.5
  67.1 5.6 %collective-permute-done.5.cur_ref.later_ref = bf16[2,4,40,256]{3,2,1,0:T(8,128)(2,1)S(1)} collective-permute-done((bf16[2,4,40,256]{3,2,1,0:T(8,128)(2,1)S(1)}, bf16[2,4,40,256]{3,2,1,0:T(8,128)(2,1)S(1)}, u32[]{:S(2)}, u32[]{:S(2)}) %collective-permute-start.5) | collective-permute-done | bytes 163872 | tf_op jit(solution)/shard_map/ppermute | solution.py:300
  72.7 2.4 %shard_map.53 = bf16[320,512]{1,0:T(8,128)(2,1)S(1)} custom-call(bf16[2,4,40,256]{3,2,1,0:T(8,128)(2,1)S(1)} %collective-permute-done.5.cur_ref.later_ref, bf16[2,4,40,256]{3,2,1,0:T(8,128)(2,1)S(1)} %collective-permute-done.3.cur_ref.later_ref, bf16[27,256,512]{2,1,0:T(8,128)(2,1)S(1)} %bitcast.174), custom_call_target="tpu_custom_call" | custom-call | flops 2264924160 | bytes 7077888 | tf_op jit(solution)/shard_map/pallas_call | solution.py:47
  75.3 1.3 collective-permute-done.6
  76.8 2.7 %collective-permute-start.7 = (bf16[2,4,40,256]{3,2,1,0:T(8,128)(2,1)S(1)}, bf16[2,4,40,256]{3,2,1,0:T(8,128)(2,1)S(1)}, u32[]{:S(2)}, u32[]{:S(2)}) collective-permute-start(bf16[2,4,40,256]{3,2,1,0:T(8,128)(2,1)S(1)} %fusion.39), channel_id=1, source_target_pairs={{0,8},{8,16},{16,24},{1,9},{9,17},{17,25},{2,10},{10,18},{18,26},{... | collective-permute-start | bytes 491528 | tf_op jit(solution)/shard_map/ppermute | solution.py:300
  79.6 3.5 %collective-permute-done.7.cur_ref.later_ref = bf16[2,4,40,256]{3,2,1,0:T(8,128)(2,1)S(1)} collective-permute-done((bf16[2,4,40,256]{3,2,1,0:T(8,128)(2,1)S(1)}, bf16[2,4,40,256]{3,2,1,0:T(8,128)(2,1)S(1)}, u32[]{:S(2)}, u32[]{:S(2)}) %collective-permute-start.7) | collective-permute-done | bytes 163872 | tf_op jit(solution)/shard_map/ppermute | solution.py:300
  83.9 2.4 %shard_map.54 = bf16[320,512]{1,0:T(8,128)(2,1)S(1)} custom-call(bf16[2,4,40,256]{3,2,1,0:T(8,128)(2,1)S(1)} %collective-permute-done.7.cur_ref.later_ref, bf16[2,4,40,256]{3,2,1,0:T(8,128)(2,1)S(1)} %collective-permute-done.5.cur_ref.later_ref, bf16[27,256,512]{2,1,0:T(8,128)(2,1)S(1)} %bitcast.175), custom_call_target="tpu_custom_call" | custom-call | flops 2264924160 | bytes 7077888 | tf_op jit(solution)/shard_map/pallas_call | solution.py:47
  89.5 3.9 %all-gather.6.cloned.1.call-done = bf16[8,1024,256]{2,1,0:T(8,128)(2,1)} async-done(((bf16[1,1024,256]{2,1,0:T(8,128)(2,1)}), bf16[8,1024,256]{2,1,0:T(8,128)(2,1)}) %all-gather.6.cloned.1.call-update) | async-done | bytes 4194320 | tf_op jit(solution)/shard_map/all_gather | solution.py:259
  93.3 3.0 %copy-done.3 = bf16[1,27,256,512]{3,2,1,0:T(8,128)(2,1)S(1)} copy-done((bf16[1,27,256,512]{3,2,1,0:T(8,128)(2,1)S(1)}, bf16[1,27,256,512]{3,2,1,0:T(8,128)(2,1)}, u32[]{:S(2)}) %copy-start.3) | copy-done | bytes 7077912
  96.4 2.5 %shard_map.55 = bf16[320,512]{1,0:T(8,128)(2,1)S(1)} custom-call(bf16[2,4,40,256]{3,2,1,0:T(8,128)(2,1)S(1)} %collective-permute-done.9.cur_ref.later_ref, bf16[2,4,40,256]{3,2,1,0:T(8,128)(2,1)S(1)} %collective-permute-done.7.cur_ref.later_ref, bf16[27,256,512]{2,1,0:T(8,128)(2,1)S(1)} %bitcast.176), custom_call_target="tpu_custom_call" | custom-call | flops 2264924160 | bytes 7077888 | tf_op jit(solution)/shard_map/pallas_call | solution.py:47
  102.2 2.4 %shard_map.56 = bf16[320,512]{1,0:T(8,128)(2,1)S(1)} custom-call(bf16[2,4,40,256]{3,2,1,0:T(8,128)(2,1)S(1)} %collective-permute-done.11.cur_ref, bf16[2,4,40,256]{3,2,1,0:T(8,128)(2,1)S(1)} %collective-permute-done.9.cur_ref.later_ref, bf16[27,256,512]{2,1,0:T(8,128)(2,1)S(1)} %bitcast.177), custom_call_target="tpu_custom_call" | custom-call | flops 2264924160 | bytes 7077888 | tf_op jit(solution)/shard_map/pallas_call | solution.py:47
  104.6 17.0 %all-gather.4.cloned.1.call-done.refs_2_ = bf16[4,4,4,32,256]{4,3,2,1,0:T(8,128)(2,1)} async-done(((bf16[1,4,4,32,256]{4,3,2,1,0:T(8,128)(2,1)}), bf16[4,4,4,32,256]{4,3,2,1,0:T(8,128)(2,1)}) %all-gather.4.cloned.1.call-update) | async-done | bytes 1048592 | tf_op jit(solution)/shard_map/all_gather | solution.py:271
  121.6 1.9 %collective-permute-start.15 = (bf16[4,4,32,256]{3,2,1,0:T(8,128)(2,1)}, bf16[4,4,32,256]{3,2,1,0:T(8,128)(2,1)}, u32[]{:S(2)}, u32[]{:S(2)}) collective-permute-start(bf16[4,4,32,256]{3,2,1,0:T(8,128)(2,1)} %bitcast.198), channel_id=1, source_target_pairs={{0,6},{2,0},{4,2},{6,4},{1,7},{3,1},{5,3},{7,5},{8,14},{10,8},{12,... | collective-permute-start | bytes 786440 | tf_op jit(solution)/shard_map/ppermute | solution.py:277
  125.6 20.5 %shard_map.57.refs_2_ = bf16[27,256,512]{2,1,0:T(8,128)(2,1)} custom-call(s32[1]{0:T(128)} %bitcast.67.refs_0_, bf16[4,2,1,1024,256]{4,3,2,1,0:T(8,128)(2,1)} %bitcast.202, bf16[4,4,4,32,256]{4,3,2,1,0:T(8,128)(2,1)} %all-gather.4.cloned.1.call-done.refs_2_), custom_call_target="tpu_custom_call" | custom-call | flops 14495514624 | bytes 21233664 | tf_op jit(solution)/shard_map/pallas_call | solution.py:191
  147.5 4.0 %all-to-all-start.2 = ((bf16[4,8,1,32,256]{4,3,1,2,0:T(8,128)(2,1)}), bf16[4,8,1,32,256]{4,3,1,2,0:T(8,128)(2,1)S(1)}, u32[]{:S(2)}, u32[]{:S(2)}) async-start(bf16[4,8,1,32,256]{4,3,1,2,0:T(8,128)(2,1)} %copy_bitcast_fusion), calls=%async_computation.2 | async-start | bytes 1048576 | tf_op jit(solution)/shard_map/all_to_all | solution.py:311
  151.5 18.6 %shard_map.58 = bf16[27,256,512]{2,1,0:T(8,128)(2,1)} custom-call(s32[1]{0:T(128)} %bitcast.67.refs_0_, bf16[4,2,1,1024,256]{4,3,2,1,0:T(8,128)(2,1)} %bitcast.203, bf16[27,256,512]{2,1,0:T(8,128)(2,1)} %shard_map.57.refs_2_, bf16[4,4,32,256]{3,2,1,0:T(8,128)(2,1)} %bitcast.201, bf16[4,4,32,256]{3,2,1,0:T(8,128)(2,1)} %collective-permute-done.13.refs_4_, ...), custom_call_target="tpu_custom_call" | custom-call | flops 14495514624 | bytes 21233664 | tf_op jit(solution)/shard_map/pallas_call | solution.py:191
  (99 shorter events, 17.6 us)
Async XLA Ops:
  7.2 1.4 copy-start
  9.9 16.6 %all-to-all-start = ((bf16[4,2,2,1,40,256]{5,4,2,3,1,0:T(8,128)(2,1)}), bf16[4,2,2,1,40,256]{5,4,2,3,1,0:T(8,128)(2,1)S(1)}, u32[]{:S(2)}, u32[]{:S(2)}) async-start(bf16[4,2,2,1,40,256]{5,4,2,3,1,0:T(8,128)(2,1)} %pad_maximum_fusion.2), calls=%async_computation | async-start | bytes 655360 | tf_op jit(solution)/shard_map/all_to_all | solution.py:231
  26.5 15.6 %all-to-all-start.1 = ((bf16[4,6,1,40,256]{4,3,1,2,0:T(8,128)(2,1)}), bf16[4,6,1,40,256]{4,3,1,2,0:T(8,128)(2,1)S(1)}, u32[]{:S(2)}, u32[]{:S(2)}) async-start(bf16[4,6,1,40,256]{4,3,1,2,0:T(8,128)(2,1)} %pad_maximum_fusion.1), calls=%async_computation.1 | async-start | bytes 983040 | tf_op jit(solution)/shard_map/all_to_all | solution.py:231
  30.0 63.3 %all-gather.6.cloned.1.call-start = ((), (), s32[]{:S(2)}) async-start(), calls=%async_computation.4 | async-start | bytes 4718592 | tf_op jit(solution)/shard_map/all_gather | solution.py:259
  30.1 3.0 %copy-start.1 = (bf16[1,27,256,512]{3,2,1,0:T(8,128)(2,1)S(1)}, bf16[1,27,256,512]{3,2,1,0:T(8,128)(2,1)}, u32[]{:S(2)}) copy-start(bf16[1,27,256,512]{3,2,1,0:T(8,128)(2,1)} %param.5) | copy-start | bytes 21233668
  35.6 1.5 collective-permute-start
  37.4 8.2 %collective-permute-start.1 = (bf16[2,4,40,256]{3,2,1,0:T(8,128)(2,1)S(1)}, bf16[2,4,40,256]{3,2,1,0:T(8,128)(2,1)S(1)}, u32[]{:S(2)}, u32[]{:S(2)}) collective-permute-start(bf16[2,4,40,256]{3,2,1,0:T(8,128)(2,1)S(1)} %get-tuple-element.52), channel_id=1, source_target_pairs={{0,8},{8,0},{1,9},{9,1},{2,10},{10,2},{3,11},{11,3},{4,12},{12,4},... | collective-permute-start | bytes 491528 | tf_op jit(solution)/shard_map/ppermute | solution.py:300
  45.6 76.0 %all-gather.4.cloned.1.call-start = ((), (), s32[]{:S(2)}) async-start(), calls=%async_computation.3 | async-start | bytes 1310720 | tf_op jit(solution)/shard_map/all_gather | solution.py:271
  45.8 3.0 %copy-start.2 = (bf16[1,27,256,512]{3,2,1,0:T(8,128)(2,1)S(1)}, bf16[1,27,256,512]{3,2,1,0:T(8,128)(2,1)}, u32[]{:S(2)}) copy-start(bf16[1,27,256,512]{3,2,1,0:T(8,128)(2,1)} %param.5) | copy-start | bytes 21233668
  51.3 1.5 collective-permute-start.2
  53.1 8.1 %collective-permute-start.3 = (bf16[2,4,40,256]{3,2,1,0:T(8,128)(2,1)S(1)}, bf16[2,4,40,256]{3,2,1,0:T(8,128)(2,1)S(1)}, u32[]{:S(2)}, u32[]{:S(2)}) collective-permute-start(bf16[2,4,40,256]{3,2,1,0:T(8,128)(2,1)S(1)} %get-tuple-element.50), channel_id=1, source_target_pairs={{0,8},{8,16},{16,0},{1,9},{9,17},{17,1},{2,10},{10,18},{18,2},{3,1... | collective-permute-start | bytes 491528 | tf_op jit(solution)/shard_map/ppermute | solution.py:300
  63.7 1.5 collective-permute-start.4
  65.5 7.2 %collective-permute-start.5 = (bf16[2,4,40,256]{3,2,1,0:T(8,128)(2,1)S(1)}, bf16[2,4,40,256]{3,2,1,0:T(8,128)(2,1)S(1)}, u32[]{:S(2)}, u32[]{:S(2)}) collective-permute-start(bf16[2,4,40,256]{3,2,1,0:T(8,128)(2,1)S(1)} %get-tuple-element.48), channel_id=1, source_target_pairs={{0,8},{8,16},{16,24},{24,0},{1,9},{9,17},{17,25},{25,1},{2,10},{10... | collective-permute-start | bytes 491528 | tf_op jit(solution)/shard_map/ppermute | solution.py:300
  75.1 1.5 collective-permute-start.6
  76.8 6.2 %collective-permute-start.7 = (bf16[2,4,40,256]{3,2,1,0:T(8,128)(2,1)S(1)}, bf16[2,4,40,256]{3,2,1,0:T(8,128)(2,1)S(1)}, u32[]{:S(2)}, u32[]{:S(2)}) collective-permute-start(bf16[2,4,40,256]{3,2,1,0:T(8,128)(2,1)S(1)} %fusion.39), channel_id=1, source_target_pairs={{0,8},{8,16},{16,24},{1,9},{9,17},{17,25},{2,10},{10,18},{18,26},{... | collective-permute-start | bytes 491528 | tf_op jit(solution)/shard_map/ppermute | solution.py:300
  83.1 3.4 %copy-start.6 = (bf16[5,2,4,32,256]{4,3,2,1,0:T(8,128)(2,1)}, bf16[5,2,4,32,256]{4,3,2,1,0:T(8,128)(2,1)S(1)}, u32[]{:S(2)}) copy-start(bf16[5,2,4,32,256]{4,3,2,1,0:T(8,128)(2,1)S(1)} %get-tuple-element.68) | copy-start | bytes 1966084
  86.4 1.5 collective-permute-start.8
  86.5 0.9 copy-start.4
  88.1 1.4 collective-permute-start.9
  93.3 3.0 %copy-start.3 = (bf16[1,27,256,512]{3,2,1,0:T(8,128)(2,1)S(1)}, bf16[1,27,256,512]{3,2,1,0:T(8,128)(2,1)}, u32[]{:S(2)}) copy-start(bf16[1,27,256,512]{3,2,1,0:T(8,128)(2,1)} %param.5) | copy-start | bytes 21233668
  96.4 2.8 %copy-start.7 = (bf16[5,2,4,32,256]{4,3,2,1,0:T(8,128)(2,1)S(1)}, bf16[5,2,4,32,256]{4,3,2,1,0:T(8,128)(2,1)}, u32[]{:S(2)}) copy-start(bf16[5,2,4,32,256]{4,3,2,1,0:T(8,128)(2,1)} %copy-done.6) | copy-start | bytes 1966084
  96.4 5.0 %copy-start.5 = (bf16[7,2,4,32,256]{4,3,2,1,0:T(8,128)(2,1)S(1)}, bf16[7,2,4,32,256]{4,3,2,1,0:T(8,128)(2,1)}, u32[]{:S(2)}) copy-start(bf16[7,2,4,32,256]{4,3,2,1,0:T(8,128)(2,1)} %fusion.73) | copy-start | bytes 2752516
  98.8 1.5 collective-permute-start.10
  100.6 0.7 collective-permute-start.11
  121.6 25.8 %collective-permute-start.15 = (bf16[4,4,32,256]{3,2,1,0:T(8,128)(2,1)}, bf16[4,4,32,256]{3,2,1,0:T(8,128)(2,1)}, u32[]{:S(2)}, u32[]{:S(2)}) collective-permute-start(bf16[4,4,32,256]{3,2,1,0:T(8,128)(2,1)} %bitcast.198), channel_id=1, source_target_pairs={{0,6},{2,0},{4,2},{6,4},{1,7},{3,1},{5,3},{7,5},{8,14},{10,8},{12,... | collective-permute-start | bytes 786440 | tf_op jit(solution)/shard_map/ppermute | solution.py:277
  123.5 24.0 %collective-permute-start.14 = (bf16[4,4,32,256]{3,2,1,0:T(8,128)(2,1)}, bf16[4,4,32,256]{3,2,1,0:T(8,128)(2,1)}, u32[]{:S(2)}, u32[]{:S(2)}) collective-permute-start(bf16[4,4,32,256]{3,2,1,0:T(8,128)(2,1)} %bitcast.199), channel_id=1, source_target_pairs={{0,4},{2,6},{4,0},{6,2},{1,5},{3,7},{5,1},{7,3},{8,12},{10,14},{12... | collective-permute-start | bytes 786440 | tf_op jit(solution)/shard_map/ppermute | solution.py:277
  124.5 23.0 %collective-permute-start.13 = (bf16[4,4,32,256]{3,2,1,0:T(8,128)(2,1)}, bf16[4,4,32,256]{3,2,1,0:T(8,128)(2,1)}, u32[]{:S(2)}, u32[]{:S(2)}) collective-permute-start(bf16[4,4,32,256]{3,2,1,0:T(8,128)(2,1)} %bitcast.200), channel_id=1, source_target_pairs={{0,2},{2,4},{4,6},{6,0},{1,3},{3,5},{5,7},{7,1},{8,10},{10,12},{12... | collective-permute-start | bytes 786440 | tf_op jit(solution)/shard_map/ppermute | solution.py:277
  125.5 20.6 %collective-permute-start.12 = (bf16[320,256]{1,0:T(8,128)(2,1)S(1)}, bf16[320,256]{1,0:T(8,128)(2,1)S(1)}, u32[]{:S(2)}, u32[]{:S(2)}) collective-permute-start(bf16[320,256]{1,0:T(8,128)(2,1)S(1)} %constant_dynamic-slice_fusion.1), channel_id=1, source_target_pairs={{0,1},{1,0},{2,3},{3,2},{4,5},{5,4},{6,7},{7,6},{8,9},{9,8},{10,11... | collective-permute-start | bytes 491528 | tf_op jit(solution)/shard_map/ppermute | solution.py:284
  147.5 22.6 %all-to-all-start.2 = ((bf16[4,8,1,32,256]{4,3,1,2,0:T(8,128)(2,1)}), bf16[4,8,1,32,256]{4,3,1,2,0:T(8,128)(2,1)S(1)}, u32[]{:S(2)}, u32[]{:S(2)}) async-start(bf16[4,8,1,32,256]{4,3,1,2,0:T(8,128)(2,1)} %copy_bitcast_fusion), calls=%async_computation.2 | async-start | bytes 1048576 | tf_op jit(solution)/shard_map/all_to_all | solution.py:311
Sparse Core Ops, SparseCore 0:
  45.7 47.5 all-gather.5
  94.9 26.6 all-gather.3
